TPU v7x, 32 devices: a whole 2x2x4 slice. The times are simulated.
32 devices in a mesh: dp: 4 (over y, x), expert: 8 (over z, core).
Axes of the slice: x: 2, y: 2, z: 4, core: 2. Of those that a mesh axis runs over, the one named last changes fastest.
Arguments:
- layer_input: bfloat16 [4096, 1024], P(('dp', 'expert')), may hold values from -6 to 6
- cotangent: bfloat16 [4096, 1024], P(('dp', 'expert')), may hold values from -6 to 6
- lengths: int32 [32], P(('dp', 'expert')), may hold values from 64 to 128, as said below
- value_routes: int32 [4096, 4, 2], P(('dp', 'expert')), may hold values from 0 to 4, all different within a row
- output_routes: int32 [4096, 4, 2], P(('dp', 'expert')), may hold values from 0 to 4, all different within a row
- ffn_routes: int32 [4096, 16], P(('dp', 'expert')), may hold values from 0 to 386, all different within a row; in each aligned block of 128 rows (0 to 127, 128 to 255, ...) at most 8 rows name the same one
- att_gain: float32 [1024], replicated, may hold values from 0.1 to 1.9
- att_shift: float32 [1024], replicated, may hold values from -1.5 to 1.5
- query_weight: bfloat16 [1024, 512], replicated, may hold values from -0.1875 to 0.1875
- key_weight: bfloat16 [1024, 512], replicated, may hold values from -0.1875 to 0.1875
- value_weight: bfloat16 [1024, 2560], replicated, may hold values from -0.1875 to 0.1875
- output_weight: bfloat16 [2560, 1024], replicated, may hold values from -1.5 to 1.5
- value_selector: bfloat16 [1024, 20], replicated, may hold values from -0.09375 to 0.09375
- output_selector: bfloat16 [1024, 20], replicated, may hold values from -0.09375 to 0.09375
- ffn_gain: float32 [1024], replicated, may hold values from 0.1 to 1.9
- ffn_shift: float32 [1024], replicated, may hold values from -1.5 to 1.5
- ffn_selector: bfloat16 [1024, 387], replicated, may hold values from -0.09375 to 0.09375
- up_weight: bfloat16 [392, 1024, 128], P('expert'), may hold values from -0.1875 to 0.1875
- down_weight: bfloat16 [392, 128, 1024], P('expert'), may hold values from -0.5 to 0.5
Outputs:
- output: bfloat16 [4096, 1024], P(('dp', 'expert'))
- input_grad: float32 [4096, 1024], P(('dp', 'expert'))
- att_gain_grad: float32 [1024], P(('dp', 'expert'))
- att_shift_grad: float32 [1024], P(('dp', 'expert'))
- query_grad: float32 [1024, 512], P(('dp', 'expert'))
- key_grad: float32 [1024, 512], P(('dp', 'expert'))
- value_grad: float32 [1024, 2560], P(('dp', 'expert'))
- output_grad: float32 [2560, 1024], P(None, ('dp', 'expert'))
- value_selector_grad: float32 [1024, 20], P(('dp', 'expert'))
- output_selector_grad: float32 [1024, 20], P(('dp', 'expert'))
- ffn_gain_grad: float32 [1024], P(('dp', 'expert'))
- ffn_shift_grad: float32 [1024], P(('dp', 'expert'))
- ffn_selector_grad: float32 [1024, 387], P(('dp', 'expert'))
- up_grad: float32 [392, 1024, 128], P('expert', 'dp')
- down_grad: float32 [392, 128, 1024], P('expert', None, 'dp')
- expert_counts: float32 [387], replicated
Inputs may be any that keep to these rules, and one draw needn't show every extreme that they name: `lengths`: at least 64; one sequence of every draw has length 128. `value_routes`: the 2 experts of a token in a head differ. `output_routes`: the 2 experts of a token in a head differ. `ffn_routes`: the 16 experts of a token differ; among the 128 rows of one device no expert is named by more than 8 rows, and in some device's rows some expert is named by exactly 8.
All inputs are finite; a program needn't handle non-finite values.
Results may differ from a plain program's by a relative error of at most 0.015.
Values may be sent and summed in bfloat16 or wider, within the bound.
No kernel may reach another device: no remote copies, remote signals or barrier semaphores. Data moves between devices by JAX's collectives and lax.ppermute only.
A program may use at most 256 MiB of HBM per device.

v0:
```python
import math
from functools import partial

import jax
import jax.numpy as jnp
from jax import lax
from jax.experimental import pallas as pl
from jax.experimental.pallas import tpu as pltpu
from jax.sharding import PartitionSpec as P

EXPERTS = 387
MOST = 8
EPSILON = 1e-05
NEGATIVE = -1e30
f32 = jnp.float32
bf16 = jnp.bfloat16
VMEM_LIMIT = 56 * 1024 * 1024
GELU_A = math.sqrt(2.0 / math.pi)
GELU_B = 0.044715


def layer_norm(values, scaling, offset):
    centred = values - jnp.mean(values, axis=-1, keepdims=True)
    inverse = lax.rsqrt(jnp.mean(centred * centred, axis=-1, keepdims=True) + EPSILON)
    normed = centred * inverse
    return (normed * scaling + offset, normed, inverse)


def norm_backward(upstream, normed, inverse, scaling):
    scaled = upstream * scaling
    centre_term = jnp.mean(scaled, axis=-1, keepdims=True)
    slope_term = jnp.mean(scaled * normed, axis=-1, keepdims=True)
    return inverse * (scaled - centre_term - normed * slope_term)


def gate_table(logits, routes, choices_count):
    chosen = jnp.any(routes[..., None] == jnp.arange(choices_count), axis=-2)
    sigmas = jax.nn.sigmoid(logits)
    return (chosen, sigmas, jnp.where(chosen, sigmas, 0.0))


def general_path(
    layer_input,
    cotangent,
    lengths,
    value_routes,
    output_routes,
    ffn_routes,
    att_gain,
    att_shift,
    query_weight,
    key_weight,
    value_weight,
    output_weight,
    value_selector,
    output_selector,
    ffn_gain,
    ffn_shift,
    ffn_selector,
    up_weight,
    down_weight,
):
    f32 = jnp.float32
    bf16 = jnp.bfloat16
    seq_len, width = layer_input.shape
    heads = value_routes.shape[1]
    head_dim = query_weight.shape[1] // heads
    att_experts = value_selector.shape[1] // heads
    top_ffn = ffn_routes.shape[1]
    exp_local = up_weight.shape[0]
    owners = lax.axis_size("expert")
    padded_experts = exp_local * owners
    capacity = MOST
    scaling = 1.0 / math.sqrt(head_dim)
    positions = jnp.arange(seq_len)
    is_valid = positions < lengths[0]
    validity = is_valid.astype(f32)
    input_float = layer_input.astype(f32)
    norm_att, hat_att, inv_att = layer_norm(input_float, att_gain, att_shift)
    act_att = norm_att.astype(bf16)
    queries = (
        jnp.dot(act_att, query_weight, preferred_element_type=f32)
        .astype(bf16)
        .reshape(seq_len, heads, head_dim)
    )
    key_rows = (
        jnp.dot(act_att, key_weight, preferred_element_type=f32)
        .astype(bf16)
        .reshape(seq_len, heads, head_dim)
    )
    projected = jnp.dot(layer_input, value_weight, preferred_element_type=f32).reshape(
        seq_len, heads, att_experts, head_dim
    )
    value_logits = jnp.dot(act_att, value_selector, preferred_element_type=f32).reshape(
        seq_len, heads, att_experts
    )
    output_logits = jnp.dot(act_att, output_selector, preferred_element_type=f32).reshape(
        seq_len, heads, att_experts
    )
    value_pick, value_sig, value_gates = gate_table(value_logits, value_routes, att_experts)
    out_pick, out_sig, out_gates = gate_table(output_logits, output_routes, att_experts)
    values_low = jnp.sum(value_gates[..., None] * projected, axis=2).astype(bf16)
    causal = (positions[None, :] <= positions[:, None]) & is_valid[None, :]
    raw_scores = jnp.einsum("qhd,khd->hqk", queries, key_rows, preferred_element_type=f32) * scaling
    scores = jnp.where(causal[None], raw_scores, NEGATIVE)
    row_peak = jnp.max(scores, axis=-1, keepdims=True)
    log_total = row_peak + jnp.log(jnp.sum(jnp.exp(scores - row_peak), axis=-1, keepdims=True))
    weights_p = jnp.exp(scores - log_total)
    weights_low = weights_p.astype(bf16)
    attended = jnp.einsum("hqk,khd->qhd", weights_low, values_low, preferred_element_type=f32)
    mixed_rows = (out_gates[..., None] * attended[:, :, None, :]).reshape(seq_len, -1).astype(bf16)
    residual = input_float + jnp.dot(mixed_rows, output_weight, preferred_element_type=f32)
    norm_ffn, hat_ffn, inv_ffn = layer_norm(residual, ffn_gain, ffn_shift)
    act_ffn = norm_ffn.astype(bf16)
    ffn_logits = jnp.dot(act_ffn, ffn_selector, preferred_element_type=f32)
    ffn_sig = jax.nn.sigmoid(jnp.take_along_axis(ffn_logits, ffn_routes, axis=1))
    gate_weights = ffn_sig * validity[:, None]
    entries = ffn_routes.reshape(-1)
    live_entry = jnp.broadcast_to(is_valid[:, None], ffn_routes.shape).reshape(-1)
    onehot_table = (
        (entries[:, None] == jnp.arange(padded_experts)[None, :]) & live_entry[:, None]
    ).astype(jnp.int32)
    before = jnp.cumsum(onehot_table, axis=0) - onehot_table
    slot_rank = jnp.sum(before * onehot_table, axis=1)
    counts_local = jnp.sum(onehot_table, axis=0).astype(f32)
    target = jnp.where(live_entry, entries * capacity + slot_rank, padded_experts * capacity)
    fetch = jnp.minimum(target, padded_experts * capacity - 1)
    total_slots = padded_experts * capacity
    residual_low = residual.astype(bf16)
    copies = jnp.broadcast_to(residual_low[:, None, :], (seq_len, top_ffn, width)).reshape(
        -1, width
    )
    send_rows = jnp.zeros((total_slots, width), bf16).at[target].set(copies, mode="drop")
    received = lax.all_to_all(
        send_rows.reshape(owners, exp_local * capacity, width),
        "expert",
        split_axis=0,
        concat_axis=0,
        tiled=True,
    )
    received = received.reshape(owners, exp_local, capacity, width)
    hidden_pre = jnp.einsum("semd,edh->semh", received, up_weight, preferred_element_type=f32)
    hidden_act = jax.nn.gelu(hidden_pre).astype(bf16)
    expert_out = jnp.einsum(
        "semh,ehd->semd", hidden_act, down_weight, preferred_element_type=f32
    ).astype(bf16)
    returned = lax.all_to_all(
        expert_out.reshape(owners, exp_local * capacity, width),
        "expert",
        split_axis=0,
        concat_axis=0,
        tiled=True,
    )
    gathered = (
        returned.reshape(total_slots, width)[fetch].reshape(seq_len, top_ffn, width).astype(f32)
    )
    final = residual + jnp.einsum("tk,tkd->td", gate_weights, gathered)
    output = final.astype(bf16)
    counts_all = lax.psum(counts_local, ("dp", "expert"))
    grad_final = cotangent.astype(f32)
    grad_rows = (gate_weights[:, :, None] * grad_final[:, None, :]).astype(bf16).reshape(-1, width)
    grad_gate = validity[:, None] * jnp.einsum("tkd,td->tk", gathered, grad_final)
    send_grad = jnp.zeros((total_slots, width), bf16).at[target].set(grad_rows, mode="drop")
    grad_recv = lax.all_to_all(
        send_grad.reshape(owners, exp_local * capacity, width),
        "expert",
        split_axis=0,
        concat_axis=0,
        tiled=True,
    )
    grad_recv = grad_recv.reshape(owners, exp_local, capacity, width)
    down_local = jnp.einsum("semh,semd->ehd", hidden_act, grad_recv, preferred_element_type=f32)
    grad_act = jnp.einsum("semd,ehd->semh", grad_recv, down_weight, preferred_element_type=f32)
    gelu_value, gelu_back = jax.vjp(jax.nn.gelu, hidden_pre)
    grad_pre = gelu_back(grad_act)[0].astype(bf16)
    up_local = jnp.einsum("semd,semh->edh", received, grad_pre, preferred_element_type=f32)
    grad_in = jnp.einsum("semh,edh->semd", grad_pre, up_weight, preferred_element_type=f32).astype(
        bf16
    )
    grad_back = lax.all_to_all(
        grad_in.reshape(owners, exp_local * capacity, width),
        "expert",
        split_axis=0,
        concat_axis=0,
        tiled=True,
    )
    grad_copies = (
        grad_back.reshape(total_slots, width)[fetch].reshape(seq_len, top_ffn, width).astype(f32)
    )
    grad_residual = grad_final + jnp.einsum("t,tkd->td", validity, grad_copies)
    sig_grad = grad_gate * ffn_sig * (1.0 - ffn_sig)
    dense_select = jnp.sum(
        jnp.where(ffn_routes[:, :, None] == jnp.arange(EXPERTS), sig_grad[:, :, None], 0.0), axis=1
    ).astype(bf16)
    ffn_selector_local = jnp.einsum("td,te->de", act_ffn, dense_select, preferred_element_type=f32)
    grad_norm_ffn = jnp.einsum("te,de->td", dense_select, ffn_selector, preferred_element_type=f32)
    ffn_gain_local = jnp.sum(grad_norm_ffn * hat_ffn, axis=0)
    ffn_shift_local = jnp.sum(grad_norm_ffn, axis=0)
    grad_residual = grad_residual + norm_backward(grad_norm_ffn, hat_ffn, inv_ffn, ffn_gain)
    grad_att_low = grad_residual.astype(bf16)
    output_local = jnp.einsum("tc,td->cd", mixed_rows, grad_att_low, preferred_element_type=f32)
    grad_mixed = jnp.einsum("td,cd->tc", grad_att_low, output_weight, preferred_element_type=f32)
    grad_mixed = grad_mixed.reshape(seq_len, heads, att_experts, head_dim)
    grad_attended = jnp.sum(out_gates[..., None] * grad_mixed, axis=2).astype(bf16)
    grad_out_gates = jnp.sum(grad_mixed * attended[:, :, None, :], axis=-1)
    out_select = (
        jnp.where(out_pick, grad_out_gates * out_sig * (1.0 - out_sig), 0.0)
        .reshape(seq_len, -1)
        .astype(bf16)
    )
    grad_weights = jnp.einsum("qhd,khd->hqk", grad_attended, values_low, preferred_element_type=f32)
    row_delta = jnp.sum(weights_p * grad_weights, axis=-1, keepdims=True)
    grad_scores = (weights_p * (grad_weights - row_delta)).astype(bf16)
    grad_queries = (
        (jnp.einsum("hqk,khd->qhd", grad_scores, key_rows, preferred_element_type=f32) * scaling)
        .reshape(seq_len, -1)
        .astype(bf16)
    )
    grad_keys = (
        (jnp.einsum("hqk,qhd->khd", grad_scores, queries, preferred_element_type=f32) * scaling)
        .reshape(seq_len, -1)
        .astype(bf16)
    )
    grad_values = jnp.einsum(
        "hqk,qhd->khd", weights_low, grad_attended, preferred_element_type=f32
    ).astype(bf16)
    grad_values_float = grad_values.astype(f32)
    grad_projected = (
        (value_gates[..., None] * grad_values_float[:, :, None, :])
        .reshape(seq_len, -1)
        .astype(bf16)
    )
    grad_value_gates = jnp.sum(grad_values_float[:, :, None, :] * projected, axis=-1)
    value_select = (
        jnp.where(value_pick, grad_value_gates * value_sig * (1.0 - value_sig), 0.0)
        .reshape(seq_len, -1)
        .astype(bf16)
    )
    value_local = jnp.einsum("td,tc->dc", layer_input, grad_projected, preferred_element_type=f32)
    query_local = jnp.einsum("td,tc->dc", act_att, grad_queries, preferred_element_type=f32)
    key_local = jnp.einsum("td,tc->dc", act_att, grad_keys, preferred_element_type=f32)
    value_selector_local = jnp.einsum(
        "td,tc->dc", act_att, value_select, preferred_element_type=f32
    )
    output_selector_local = jnp.einsum("td,tc->dc", act_att, out_select, preferred_element_type=f32)
    grad_norm_att = jnp.einsum("tc,dc->td", grad_queries, query_weight, preferred_element_type=f32)
    grad_norm_att = grad_norm_att + jnp.einsum(
        "tc,dc->td", grad_keys, key_weight, preferred_element_type=f32
    )
    grad_norm_att = grad_norm_att + jnp.einsum(
        "tc,dc->td", value_select, value_selector, preferred_element_type=f32
    )
    grad_norm_att = grad_norm_att + jnp.einsum(
        "tc,dc->td", out_select, output_selector, preferred_element_type=f32
    )
    att_gain_local = jnp.sum(grad_norm_att * hat_att, axis=0)
    att_shift_local = jnp.sum(grad_norm_att, axis=0)
    input_grad = grad_residual + jnp.einsum(
        "tc,dc->td", grad_projected, value_weight, preferred_element_type=f32
    )
    input_grad = input_grad + norm_backward(grad_norm_att, hat_att, inv_att, att_gain)
    reduced = (
        lax.psum_scatter(att_gain_local, ("dp", "expert"), scatter_dimension=0, tiled=True),
        lax.psum_scatter(att_shift_local, ("dp", "expert"), scatter_dimension=0, tiled=True),
        lax.psum_scatter(query_local, ("dp", "expert"), scatter_dimension=0, tiled=True),
        lax.psum_scatter(key_local, ("dp", "expert"), scatter_dimension=0, tiled=True),
        lax.psum_scatter(value_local, ("dp", "expert"), scatter_dimension=0, tiled=True),
        lax.psum_scatter(output_local, ("dp", "expert"), scatter_dimension=1, tiled=True),
        lax.psum_scatter(value_selector_local, ("dp", "expert"), scatter_dimension=0, tiled=True),
        lax.psum_scatter(output_selector_local, ("dp", "expert"), scatter_dimension=0, tiled=True),
        lax.psum_scatter(ffn_gain_local, ("dp", "expert"), scatter_dimension=0, tiled=True),
        lax.psum_scatter(ffn_shift_local, ("dp", "expert"), scatter_dimension=0, tiled=True),
        lax.psum_scatter(ffn_selector_local, ("dp", "expert"), scatter_dimension=0, tiled=True),
    )
    up_grad, down_grad = (
        lax.psum_scatter(
            up_local.astype(jnp.bfloat16), "dp", scatter_dimension=1, tiled=True
        ).astype(jnp.float32),
        lax.psum_scatter(
            down_local.astype(jnp.bfloat16), "dp", scatter_dimension=2, tiled=True
        ).astype(jnp.float32),
    )
    return (
        output,
        input_grad,
        reduced[0],
        reduced[1],
        reduced[2],
        reduced[3],
        reduced[4],
        reduced[5],
        reduced[6],
        reduced[7],
        reduced[8],
        reduced[9],
        reduced[10],
        up_grad,
        down_grad,
        counts_all[:EXPERTS],
    )


def mm(a, b, ca, cb):
    return lax.dot_general(a, b, (((ca,), (cb,)), ((), ())), preferred_element_type=f32)


def iota(shape, dim):
    return lax.broadcasted_iota(jnp.int32, shape, dim)


def centre(values):
    centred = values - jnp.mean(values, axis=-1, keepdims=True)
    inverse = lax.rsqrt(jnp.mean(centred * centred, axis=-1, keepdims=True) + EPSILON)
    return centred * inverse, inverse


def centre_back(upstream, normed, inverse, gain):
    scaled = upstream * gain
    mean = jnp.mean(scaled, axis=-1, keepdims=True)
    slope = jnp.mean(scaled * normed, axis=-1, keepdims=True)
    return inverse * (scaled - mean - normed * slope)


def device_of(ids, s, x):
    return 2 * s + (ids[1] + x - 2 * ids[1] * x)


SHORT = pl.CostEstimate(flops=1, bytes_accessed=1, transcendentals=0)


LONG = pl.CostEstimate(flops=1, bytes_accessed=1 << 28, transcendentals=0)


def call(body, outs, args, scratch=(), smem=(), name=None, cost=SHORT):
    return pl.pallas_call(
        body,
        out_shape=[jax.ShapeDtypeStruct(s, d) for s, d in outs],
        in_specs=[pl.BlockSpec(memory_space=pltpu.SMEM)] * len(smem)
        + [pl.BlockSpec(memory_space=pltpu.VMEM)] * len(args),
        out_specs=[pl.BlockSpec(memory_space=pltpu.VMEM)] * len(outs),
        scratch_shapes=list(scratch),
        compiler_params=pltpu.CompilerParams(vmem_limit_bytes=VMEM_LIMIT),
        cost_estimate=cost,
        name=name,
    )(*smem, *args)


def forward_body(
    length, li, vroutes, oroutes, froutes, att_gain, att_shift, wq, wk, wv, wo, vsel, osel,
    ffn_gain, ffn_shift, fsel,
    h1_o, xpack_o, q_o, k_o, v_o, p_o, a_o, o_o, gt_o, a1_o, a2_o, mixed,
):
    T, D = li.shape
    heads = vroutes.shape[0]
    dh = wq.shape[1] // heads
    ea = wv.shape[1] // (heads * dh)
    he = heads * ea
    top = froutes.shape[0]
    routes = [vroutes[h] for h in range(heads)] + [oroutes[h] for h in range(heads)] + [froutes[...]]
    routes = jnp.concatenate([r.astype(f32) for r in routes], axis=0)
    routes = jnp.concatenate([routes, jnp.zeros((128 - routes.shape[0], T), f32)], axis=0).T.astype(jnp.int32)
    scaling = 1.0 / math.sqrt(dh)
    x = li[...].astype(f32)
    hat, inv = centre(x)
    mean = jnp.mean(x, axis=-1, keepdims=True)
    a1 = (hat * att_gain[...] + att_shift[...]).astype(bf16)
    a1_o[...] = a1
    logits = jnp.concatenate(
        [mm(a1, vsel[...], 1, 1), mm(a1, osel[...], 1, 1), jnp.zeros((T, 128 - 2 * he), f32)], axis=1
    )
    lane = iota((T, 128), 1)
    chosen = jnp.zeros((T, 128), jnp.bool_)
    for j in range(2 * heads):
        h = j // 2
        chosen |= lane == routes[:, j : j + 1] + h * ea
        chosen |= lane == routes[:, 2 * heads + j : 2 * heads + j + 1] + (he + h * ea)
    gt = jnp.where(chosen, jax.nn.sigmoid(logits), 0.0)
    gt_o[...] = jnp.where(lane == 2 * he, mean, jnp.where(lane == 2 * he + 1, inv, gt))
    q = mm(a1, wq[...], 1, 0).astype(bf16)
    k = mm(a1, wk[...], 1, 0).astype(bf16)
    q_o[...] = q
    k_o[...] = k
    n_live = length[0]
    row, col = iota((T, T), 0), iota((T, T), 1)
    causal = (col <= row) & (col < n_live)
    width = ea * dh
    for h in range(heads):
        proj = mm(li[...], wv[:, h * width : (h + 1) * width], 1, 0)
        p_o[:, h * width : (h + 1) * width] = proj
        v = jnp.zeros((T, dh), f32)
        for e in range(ea):
            v += gt[:, h * ea + e : h * ea + e + 1] * proj[:, e * dh : (e + 1) * dh]
        v = v.astype(bf16)
        v_o[:, h * dh : (h + 1) * dh] = v
        s = mm(q[:, h * dh : (h + 1) * dh], k[:, h * dh : (h + 1) * dh], 1, 1) * scaling
        s = jnp.where(causal, s, NEGATIVE)
        ex = jnp.exp(s - jnp.max(s, axis=-1, keepdims=True))
        a = ex / jnp.sum(ex, axis=-1, keepdims=True)
        a_o[h] = a
        o = mm(a.astype(bf16), v, 1, 0)
        o_o[:, h * dh : (h + 1) * dh] = o
        for e in range(ea):
            c = he + h * ea + e
            mixed[:, (h * ea + e) * dh : (h * ea + e + 1) * dh] = (gt[:, c : c + 1] * o).astype(bf16)
    h1 = x + mm(mixed[...], wo[...], 1, 0)
    h1_o[...] = h1
    hat2, _ = centre(h1)
    a2 = (hat2 * ffn_gain[...] + ffn_shift[...]).astype(bf16)
    a2_o[...] = a2
    sig = jax.nn.sigmoid(mm(a2, fsel[...], 1, 1))
    wide = iota(sig.shape, 1)
    g = jnp.zeros((T, 128), f32)
    for i in range(top):
        c = 4 * heads + i
        one = jnp.sum(jnp.where(wide == routes[:, c : c + 1], sig, 0.0), axis=-1, keepdims=True)
        g = jnp.where(lane == i, one, g)
    g = g.T[:16]
    hi = g.astype(bf16)
    low = h1.astype(bf16)
    for s in range(xpack_o.shape[0]):
        xpack_o[s, :T] = low
        xpack_o[s, T:] = jnp.zeros((16, D), bf16)
        xpack_o[s, T:, :128] = hi
        xpack_o[s, T:, 128:256] = (g - hi.astype(f32)).astype(bf16)


def take_slices(v, n_p, S, e):
    D = v.shape[1]
    w = D // (n_p * S)
    return jnp.concatenate(
        [v[:, (b * S + e) * w : (b * S + e + 1) * w] for b in range(n_p)], axis=1
    )


def views(mine, theirs):
    return [r.at[s] for s in range(mine.shape[0]) for r in (mine, theirs)]


def views_from(ids, mine, theirs):
    return [r.at[ids[0] ^ s] for s in range(mine.shape[0]) for r in (mine, theirs)]


def early_body(n_p, S, ids, li, a1, a2, o, gt, *rest):
    msgs, scratch = rest
    msgs = [msgs.at[s] for s in range(S // 2)]
    hd = o.shape[1]
    for e in range(S):
        for i, v in enumerate((li, a1, a2)):
            scratch[e, :, i * 128 : (i + 1) * 128] = take_slices(v[...].astype(f32), n_p, S, e).astype(bf16)
    hi = gt[...].astype(bf16).astype(f32)
    both = (hi + pltpu.roll(gt[...] - hi, 64, 1)).astype(bf16)
    for s, m in enumerate(msgs):
        m[:, :hd] = o[...].astype(bf16)
        m[:, hd : hd + 128] = both
        m[:, hd + 128 : hd + 512] = scratch[device_of(ids, s, 1)]
        m[:, hd + 512 : hd + 896] = scratch[device_of(ids, s, 0)]


def codes_body(S, ids, *refs):
    c, (code_o, cnt_o, routes_o) = views_from(ids, *refs[:2]), refs[2:]
    ep = cnt_o.shape[1]
    T = code_o.shape[2] // 2
    strict = (iota((T, T), 0) < iota((T, T), 1)).astype(f32).astype(bf16)
    e_id = iota((ep, T), 0).astype(f32)
    cnt = jnp.zeros((8, ep), f32)
    start = ids[3].astype(f32)
    for k in range(S):
        r = c[k][:, :T].astype(f32) * 32.0 + c[k][:, T:].astype(f32)
        routes_o[k * 16 : (k + 1) * 16, :] = r
        r -= start
        mask = jnp.zeros((ep, T), f32)
        for i in range(r.shape[0]):
            mask = jnp.where(r[i : i + 1] == e_id, 1.0, mask)
        low = mask.astype(bf16)
        rank = mm(low, strict, 1, 0) + (MOST * (k % 2))
        cnt += mm(jnp.ones((8, T), bf16), low, 1, 1)
        code_o[k // 2, :, (k % 2) * T : (k % 2 + 1) * T] = jnp.where(mask > 0.5, rank, -1.0).astype(bf16)
    cnt_o[...] = cnt


def columns_body(n_p, order, ids, x, *refs):
    outs = refs[-n_p:]
    T = x.shape[1] - 16
    wide = outs[0].shape[2]
    for k in range(x.shape[0]):
        rows = x.at[ids[0] ^ k if order else k]
        for s in range(n_p):
            at = pl.multiple_of((ids[2] ^ s) * wide, 128)
            outs[s][k, :T, :] = rows[:T, pl.ds(at, wide)]
    if len(refs) > n_p:
        for s in range(n_p):
            outs[s][:, T:, :] = refs[0][...]


def gelu_both(u):
    t = jnp.tanh(GELU_A * (u + GELU_B * u * u * u))
    value = 0.5 * u * (1.0 + t)
    slope = 0.5 * (1.0 + t) + 0.5 * u * (1.0 - t * t) * (GELU_A * (1.0 + 3.0 * GELU_B * u * u))
    return value, slope


def experts_body(S, eb, ids, *refs):
    x, c = views(*refs[:2]), views_from(ids, *refs[2:4])
    code, up, down, dx0, dx1, gy0, gy1, gr_o, du_o, ct, gts, dl, ps, xs, cs, gys, dxs = refs[4:]
    step = pl.program_id(0)
    pairs = S // 2
    R = 2 * MOST
    T = x[0].shape[0] - 16
    D = x[0].shape[1]
    ep = ct.shape[1]
    rows = pairs * R
    H = up.shape[2]

    @pl.when(step == 0)
    def _():
        e_id = iota((ep, T), 0).astype(f32)
        start = ids[3].astype(f32)
        dl[...] = jnp.zeros_like(dl)
        for pr in range(pairs):
            ct[pr] = code[pr].astype(f32)
        for k in range(S):
            r = c[k][T:, :T].astype(f32) * 32.0 + c[k][T:, T : 2 * T].astype(f32) - start
            g = x[k][T:, :T].astype(f32) + x[k][T:, T : 2 * T].astype(f32)
            dense = jnp.zeros((ep, T), f32)
            for i in range(r.shape[0]):
                dense = jnp.where(r[i : i + 1] == e_id, g[i : i + 1], dense)
            gts[:, k * T : (k + 1) * T] = dense

    slot = iota((R, 2 * T), 0).astype(f32)
    g_slot = [[None] * pairs for _ in range(eb)]
    onehot = [[None] * pairs for _ in range(eb)]
    for pr in range(pairs):
        blocks = []
        for j in range(eb):
            e = step * eb + j
            hot = jnp.where(ct[pr, pl.ds(e, 1), :] == slot, 1.0, 0.0)
            onehot[j][pr] = hot
            g_slot[j][pr] = jnp.sum(
                hot * gts[pl.ds(e, 1), pr * 2 * T : (pr + 1) * 2 * T], axis=-1, keepdims=True
            )
            blocks.append(hot.astype(bf16))
        block = jnp.concatenate(blocks, axis=0)
        ps[pr, pl.ds(pl.multiple_of(step * (eb * R), R), eb * R), :] = block
        for src, dst in ((x, xs), (c, cs)):
            both = jnp.concatenate([src[2 * pr][:T], src[2 * pr + 1][:T]], axis=0)
            got = mm(block, both, 1, 0).astype(bf16)
            for j in range(eb):
                dst[j * rows + pr * R : j * rows + (pr + 1) * R, :] = got[j * R : (j + 1) * R]
    for first in range(0, eb, 2):
        js = list(range(first, min(first + 2, eb)))
        n = len(js)
        span = slice(first * rows, (first + n) * rows)
        g = jnp.concatenate([p for j in js for p in g_slot[j]], axis=0)
        cj = cs[span, :].astype(f32)
        ups = jnp.concatenate([up[j] for j in js], axis=1)
        downs = jnp.concatenate([down[j] for j in js], axis=0)

        def own(v):
            return jnp.concatenate([v[i * rows : (i + 1) * rows, i * H : (i + 1) * H] for i in range(n)], axis=0)

        def spread_out(v):
            if n == 1:
                return v
            zero = jnp.zeros((rows, H), v.dtype)
            return jnp.concatenate(
                [
                    jnp.concatenate([v[i * rows : (i + 1) * rows] if i == b else zero for b in range(n)], axis=1)
                    for i in range(n)
                ],
                axis=0,
            )

        u = own(mm(xs[span, :], ups, 1, 0))
        value, slope = gelu_both(u)
        r = value.astype(bf16)
        y = mm(spread_out(r), downs, 1, 0).astype(bf16).astype(f32)
        dgate = jnp.sum(cj * y, axis=-1, keepdims=True)
        gy = (g * y).astype(bf16)
        dr = own(mm((g * cj).astype(bf16), downs, 1, 1))
        du = (dr * slope).astype(bf16)
        dx = mm(spread_out(du), ups, 1, 1).astype(bf16)
        gr = (g * r.astype(f32)).astype(bf16)
        dlog = dgate * g * (1.0 - g)
        for i, j in enumerate(js):
            e = step * eb + j
            gr_o[j] = gr[i * rows : (i + 1) * rows]
            du_o[j] = du[i * rows : (i + 1) * rows]
            for pr in range(pairs):
                at = pl.ds(pl.multiple_of(step * (eb * R) + j * R, R), R)
                cut = slice(i * rows + pr * R, i * rows + (pr + 1) * R)
                gys[pr, at, :] = gy[cut]
                dxs[pr, at, :] = dx[cut]
                dl[pl.ds(e, 1), pr * 2 * T : (pr + 1) * 2 * T] = jnp.sum(
                    onehot[j][pr] * dlog[cut], axis=0, keepdims=True
                )

    @pl.when(step == pl.num_programs(0) - 1)
    def _():
        for pr in range(pairs):
            for src, d0, d1 in ((dxs, dx0, dx1), (gys, gy0, gy1)):
                got = mm(ps[pr], src[pr], 0, 0).astype(bf16)
                d0[pr, :T] = got[:T]
                d1[pr, :T] = got[T:]
            for x_i, d in ((0, dx0), (1, dx1)):
                k = 2 * pr + x_i
                part = dl[:, k * T : (k + 1) * T].astype(bf16)
                d[pr, T:] = jnp.zeros((16, D), bf16)
                for b in range(ep // 16):
                    d[pr, T:, b * T : (b + 1) * T] = part[16 * b : 16 * b + 16]


def join_body(T, mine, recv, out):
    half = mine.shape[2] // 2
    for s in range(mine.shape[0]):
        out[s, :T] = (mine[s, :T].astype(f32) + recv[s, :T].astype(f32)).astype(bf16)
        if mine.shape[1] > T:
            out[s, T:, :half] = mine[s, T:, :half]
            out[s, T:, half:] = recv[s, T:, :half]


def join_apart_body(nz, ids, mine, recv, *outs):
    for s in range(nz):
        outs[s][...] = (mine[ids[0] ^ s].astype(f32) + recv[ids[0] ^ s].astype(f32)).astype(bf16)


def ffn_back_body(n_p, S, nz, ids, parts, h1, c, fsel, gain, froutes, cnt, dh1_o, db_o, mid_o, dlt, sl):
    T, D = h1.shape
    ep = dlt.shape[0] // S
    half = D // 2
    dxs = parts[0, :T].astype(f32)
    for s in range(1, nz):
        dxs += parts[s, :T].astype(f32)
    for s in range(nz):
        for x in range(2):
            for b in range(ep // 16):
                at = pl.multiple_of(device_of(ids, s, x) * ep + 16 * b, 16)
                dlt[pl.ds(at, 16), :] = parts[s, T:, x * half + b * T : x * half + (b + 1) * T].astype(f32)
    dl = dlt[...].T
    da2 = mm(dl.astype(bf16), fsel[...], 1, 0)
    hat, inv = centre(h1[...])
    dh1 = c[...].astype(f32) + dxs + centre_back(da2, hat, inv, gain[...])
    dh1_o[...] = dh1
    db = dh1.astype(bf16)
    db_o[...] = db
    low = db.astype(f32)
    for e in range(S):
        sl[e] = take_slices(low, n_p, S, e).astype(bf16)
    slot = iota(dlt.shape, 0)
    few = [
        jnp.sum(jnp.where(slot == froutes[i : i + 1, :], dlt[...], 0.0), axis=0, keepdims=True)
        for i in range(froutes.shape[0])
    ]
    few = jnp.concatenate(few, axis=0).astype(bf16)
    hi = cnt[...].astype(bf16)
    lo = (cnt[...] - hi.astype(f32)).astype(bf16)
    vectors = []
    for v in (jnp.sum(da2 * hat, axis=0, keepdims=True), jnp.sum(da2, axis=0, keepdims=True)):
        high = v.astype(bf16).astype(f32)
        for part in (high, v - high):
            vectors += [part[:, b * 256 : (b + 1) * 256] for b in range(D // 256)]
    vectors = jnp.concatenate(vectors, axis=0).astype(bf16)
    for s in range(nz):
        m = mid_o.at[s]
        m[:T, :128] = sl[device_of(ids, s, 1)]
        m[:T, 128:] = sl[device_of(ids, s, 0)]
        m[T : T + 16, :T] = few
        m[T : T + 16, T:] = jnp.zeros((16, 256 - T), bf16)
        m[T : T + 16, T : T + ep] = jnp.concatenate([hi, lo], axis=0)
        m[T + 16 :] = vectors


def attention_back_body(db, wo, gt, o, q, k, v, a, p, late_o, dp_o):
    T, D = db.shape
    heads = a.shape[0]
    dh = q.shape[1] // heads
    ea = p.shape[1] // (heads * dh)
    he, hd = heads * ea, heads * dh
    width = ea * dh
    scaling = 1.0 / math.sqrt(dh)
    gates = gt[...]
    lane = iota((T, 128), 1)
    every = range(heads)
    hs = [slice(h * dh, (h + 1) * dh) for h in every]
    dz = [mm(db[...], wo[h * width : (h + 1) * width, :], 1, 1) for h in every]
    do = []
    for h in every:
        total = jnp.zeros((T, dh), f32)
        for e in range(ea):
            c = he + h * ea + e
            total += gates[:, c : c + 1] * dz[h][:, e * dh : (e + 1) * dh]
        do.append(total.astype(bf16))
    da = [mm(do[h], v[:, hs[h]], 1, 1) for h in every]
    dv = [mm(a[h].astype(bf16), do[h], 0, 0).astype(bf16) for h in every]
    ds = [(a[h] * (da[h] - jnp.sum(a[h] * da[h], axis=-1, keepdims=True))).astype(bf16) for h in every]
    dq = [(mm(ds[h], k[:, hs[h]], 1, 0) * scaling).astype(bf16) for h in every]
    dk = [(mm(ds[h], q[:, hs[h]], 0, 0) * scaling).astype(bf16) for h in every]
    dgates = jnp.zeros((T, 128), f32)
    for h in every:
        oh, dvf = o[:, hs[h]], dv[h].astype(f32)
        for e in range(ea):
            c = h * ea + e
            es = slice(c * dh, (c + 1) * dh)
            dp_o[:, es] = (gates[:, c : c + 1] * dvf).astype(bf16)
            out_sum = jnp.sum(dz[h][:, e * dh : (e + 1) * dh] * oh, axis=-1, keepdims=True)
            in_sum = jnp.sum(dvf * p[:, es], axis=-1, keepdims=True)
            dgates = jnp.where(lane == he + c, out_sum, jnp.where(lane == c, in_sum, dgates))
    sel = (dgates * gates * (1.0 - gates)).astype(bf16)
    for s in range(late_o.shape[0]):
        for h in every:
            late_o[s, :, hs[h]] = dv[h]
            late_o[s, :, hd + h * dh : hd + (h + 1) * dh] = dq[h]
            late_o[s, :, 2 * hd + h * dh : 2 * hd + (h + 1) * dh] = dk[h]
        late_o[s, :, 3 * hd :] = sel


def input_back_body(late, dp, wq, wk, wv, selw, li, gain, dh1, ig_o):
    hd = wq.shape[1]
    da1 = mm(late[0, :, hd : 2 * hd], wq[...], 1, 1)
    da1 += mm(late[0, :, 2 * hd : 3 * hd], wk[...], 1, 1)
    da1 += mm(late[0, :, 3 * hd :], selw[...], 1, 1)
    hat, inv = centre(li[...].astype(f32))
    ig_o[...] = dh1[...] + mm(dp[...], wv[...], 1, 1) + centre_back(da1, hat, inv, gain[...])


def spread(values, gates, lo, heads, ea, dh):
    return jnp.concatenate(
        [
            (gates[:, lo + h * ea + e : lo + h * ea + e + 1] * values[:, h * dh : (h + 1) * dh]).astype(bf16)
            for h in range(heads)
            for e in range(ea)
        ],
        axis=1,
    )


def spread_body(S, n_p, w, heads, ea, ids, e0, e1, wq, wk, selw, z_o, a2_o, lia1_o, hat_o, gates_o, wsl_o):
    early = views(e0, e1)
    T = early[0].shape[0]
    D, hd = wq.shape
    for b in range(n_p):
        at = pl.ds(pl.multiple_of(b * (D // n_p) + (2 * ids[0] + ids[1]) * w, 16), w)
        bs = slice(b * w, (b + 1) * w)
        wsl_o[bs, :hd] = wq[at, :]
        wsl_o[bs, hd : 2 * hd] = wk[at, :]
        wsl_o[bs, 2 * hd :] = selw[at, :]
    for k in range(S):
        ts = slice(k * T, (k + 1) * T)
        m = early[k]
        both = m[:, hd : hd + 128].astype(f32)
        gates = both + pltpu.roll(both, 64, 1)
        gates_o[ts, :] = gates
        z_o[ts, :] = spread(m[:, :hd].astype(f32), gates, heads * ea, heads, ea, hd // heads)
        at = hd + 512 if k % 2 == 0 else hd + 128
        li = m[:, at : at + 128].astype(f32)
        he2 = 2 * heads * ea
        lia1_o[:128, ts] = li.T.astype(bf16)
        lia1_o[128:, ts] = m[:, at + 128 : at + 256].astype(f32).T.astype(bf16)
        hat_o[:, ts] = ((li - gates[:, he2 : he2 + 1]) * gates[:, he2 + 1 : he2 + 2]).T
        a2_o[ts, :] = m[:, at + 256 : at + 384]


def out_rows(acc, outs, ids, w):
    for s, ref in enumerate(outs):
        plane = ids[2] ^ s
        ref[:, : acc.shape[1]] = acc[pl.ds(pl.multiple_of(plane * w, 8), w), :].astype(ref.dtype)


def out_grads_body(S, n_p, w, ids, m0, m1, z, a2, routes, *refs):
    mid, outs = views(m0, m1), refs[:n_p]
    acc, lhs, dlt, cnt = refs[n_p:]
    T = z.shape[0] // S
    EP = dlt.shape[0]
    e_id = iota((EP, T), 0).astype(f32)
    norms = jnp.zeros((16, 256), f32)
    for k in range(S):
        n = mid[k]
        ts = slice(k * T, (k + 1) * T)
        at = 128 if k % 2 == 0 else 0
        lhs[ts, :] = n[:T, at : at + 128]
        few = n[T : T + 16, :T].astype(f32)
        route = routes[k * 16 : (k + 1) * 16, :]
        dense = jnp.zeros((EP, T), f32)
        for i in range(16):
            dense = jnp.where(route[i : i + 1] == e_id, few[i : i + 1], dense)
        dlt[:, ts] = dense.astype(bf16)
        tally = n[T : T + 16, T:].astype(f32)
        at = device_of(ids, k // 2, k % 2)
        cnt[pl.ds(at, 1), :] = tally[:1]
        cnt[pl.ds(at + 8, 1), :] = tally[8:9]
        norms += n[T + 16 :].astype(f32)
    wide = z.shape[1]
    acc[:, :wide] = mm(lhs[...], z[...], 0, 0)
    acc[:, wide:] = mm(dlt[...], a2[...], 1, 0).T
    out_rows(acc, outs, ids, w)
    norms = pltpu.roll(norms, lax.rem(256 - (2 * ids[0] + ids[1]) * w, 256), 1)
    norms = jnp.concatenate([norms[0:4] + norms[4:8], norms[8:12] + norms[12:16]], axis=0)
    extra = jnp.concatenate([cnt[...], norms[:, :128], jnp.zeros((w - 24, 128), f32)], axis=0)
    for ref in outs:
        ref[:, acc.shape[1] :] = extra.astype(ref.dtype)


def in_grads_body(n_p, heads, ea, w, hd, ids, l0, l1, lia1, hat, gates, wsl, *refs):
    outs, (acc, rhs, qk, sums) = refs[:n_p], refs[n_p:]
    step = pl.program_id(0)
    T = l0.shape[1]
    wide = rhs.shape[1]

    @pl.when(step == 0)
    def _():
        acc[...] = jnp.zeros_like(acc)
        sums[...] = jnp.zeros_like(sums)

    for x, n in enumerate((l0, l1)):
        ts = slice(x * T, (x + 1) * T)
        rhs[ts, :] = spread(n[0, :, :hd].astype(f32), gates[ts, :], 0, heads, ea, hd // heads)
        qk[ts, :] = n[0, :, hd:]
    acc[:, :wide] += mm(lia1[:128, :], rhs[...], 1, 0)
    acc[:, wide:] += mm(lia1[128:, :], qk[...], 1, 0)
    da1 = mm(wsl[...], qk[...], 1, 1)
    gain = jnp.sum(da1 * hat[...], axis=1, keepdims=True)
    shift = jnp.sum(da1, axis=1, keepdims=True)
    lane = iota((128, 128), 1)
    sums[...] += jnp.where(lane == 64, gain, jnp.where(lane == 65, shift, 0.0))

    @pl.when(step == pl.num_programs(0) - 1)
    def _():
        acc[:, wide + 2 * hd :] += sums[...]
        out_rows(acc, outs, ids, w)


def last_a_body(n_p, S, w, el, ids, *refs):
    parts, (og_o, fg_o, gain_o, shift_o, counts_o, rows) = refs[:n_p], refs[n_p:]
    total = parts[0][...]
    for m in parts[1:]:
        total += m[...].astype(f32)
    wide = og_o.shape[1]
    og_o[...] = total[:w, :wide]
    ep = (total.shape[1] - 128 - wide) // S
    sel = total[:, wide:]
    fg_o[...] = jnp.concatenate([sel[:, e * ep : e * ep + el] for e in range(S)], axis=1)[:, : fg_o.shape[1]]
    extra = total[:, wide + S * ep :]
    rows[...] = extra[16:24]
    gain_o[...] = rows[pl.ds(ids[2], 1), :w]
    shift_o[...] = rows[pl.ds(ids[2] + n_p, 1), :w]
    cnt = extra[0:8] + extra[8:16]
    counts_o[...] = jnp.concatenate([cnt[e : e + 1, :el] for e in range(S)], axis=1)[:, : counts_o.shape[1]]


def last_b_body(n_p, w, hd, he, *refs):
    parts, (vg_o, qg_o, kg_o, vs_o, os_o, gain_o, shift_o) = refs[:n_p], refs[n_p:]
    total = parts[0][...]
    for m in parts[1:]:
        total += m[...].astype(f32)
    wide = vg_o.shape[1]
    vg_o[...] = total[:w, :wide]
    qg_o[...] = total[:w, wide : wide + hd]
    kg_o[...] = total[:w, wide + hd : wide + 2 * hd]
    sel = total[:w, wide + 2 * hd :].T
    vs_o[...] = sel[:he]
    os_o[...] = sel[he : 2 * he]
    gain_o[...] = sel[64:65]
    shift_o[...] = sel[65:66]


def expert_grads_body(n_p, eb, first, xm, xo, cm, co, *refs):
    gr_in, du_in = refs[:n_p], refs[n_p : 2 * n_p]
    up_o, down_o, ct, got = refs[-4:]
    start = pl.program_id(0)
    step = start + first
    _, pairs, T, wide = cm.shape
    T2 = 2 * T
    R = 2 * MOST
    rows = pairs * R

    @pl.when(start == 0)
    def _():
        for s in range(n_p):
            for pr in range(pairs):
                ct[s * pairs + pr] = xm[s, pr, T:, :].astype(f32)

    slot = iota((R, T2), 0).astype(f32)
    for s in range(n_p):
        for pr in range(pairs):
            block = jnp.concatenate(
                [
                    jnp.where(ct[s * pairs + pr, pl.ds(step * eb + j, 1), :] == slot, 1.0, 0.0).astype(bf16)
                    for j in range(eb)
                ],
                axis=0,
            )
            both = jnp.concatenate(
                [jnp.concatenate([x[s, pr, :T], c[s, pr]], axis=1) for x, c in ((xm, cm), (xo, co))], axis=0
            )
            res = mm(block, both, 1, 0).astype(bf16)
            for j in range(eb):
                at = j * n_p * rows + s * rows + pr * R
                got[at : at + R, :] = res[j * R : (j + 1) * R]
    for j in range(eb):
        at = j * n_p * rows
        xj = got[at : at + n_p * rows, :wide]
        cj = got[at : at + n_p * rows, wide:]
        gr = jnp.concatenate([gr_in[s][j] for s in range(n_p)], axis=0)
        du = jnp.concatenate([du_in[s][j] for s in range(n_p)], axis=0)
        up_o[j] = mm(xj, du, 0, 0)
        down_o[j] = mm(gr, cj, 0, 0)


def after(values, *deps):
    return lax.optimization_barrier((values, deps))[0]


class Links:
    def __init__(self):
        self.n_e = lax.axis_size("expert")
        self.nz = self.n_e // 2
        self.n_p = lax.axis_size("dp")
        self.me = lax.axis_index("expert")
        self.z, self.c = self.me // 2, self.me % 2
        self.p = lax.axis_index("dp")

    def core(self, v):
        return lax.ppermute(v, "expert", [(e, e ^ 1) for e in range(self.n_e)])

    def chips(self, v):
        groups = [[2 * s + c for s in range(self.nz)] for c in range(2)]
        return lax.all_to_all(v, "expert", 0, 0, axis_index_groups=groups, tiled=True)

    def chip(self, v, s):
        return lax.ppermute(v, "expert", [(e, (e + 2 * s) % self.n_e) for e in range(self.n_e)])

    def plane(self, v, s):
        return lax.ppermute(v, "dp", [(p, p ^ s) for p in range(self.n_p)])

    def near(self, msgs):
        pairs = [[(e, e ^ (2 * s)) for e in range(self.n_e)] for s in range(self.nz)]
        return [msgs[0]] + [lax.ppermute(msgs[s], "expert", pairs[s]) for s in range(1, self.nz)]

    def relay(self, mine):
        return [mine, self.core(mine)]

    def planes_of(self, msgs):
        return [msgs[0]] + [self.plane(msgs[s], s) for s in range(1, self.n_p)]


def fast_path(
    layer_input, cotangent, lengths, value_routes, output_routes, ffn_routes, att_gain, att_shift,
    query_weight, key_weight, value_weight, output_weight, value_selector, output_selector,
    ffn_gain, ffn_shift, ffn_selector, up_weight, down_weight,
):
    L = Links()
    S, nz, n_p = L.n_e, L.nz, L.n_p
    pairs = S // 2
    T, D = layer_input.shape
    heads = value_routes.shape[1]
    dh = query_weight.shape[1] // heads
    ea = value_selector.shape[1] // heads
    hd, he, wide = heads * dh, heads * ea, heads * ea * dh
    el, _, H = up_weight.shape
    ep = -(-el // 16) * 16
    EP = ep * S
    w = D // (n_p * S)
    Dp = D // n_p
    R = 2 * MOST
    eb = max(d for d in (7, 4, 2, 1) if el % d == 0)

    ids = jnp.stack([L.z, L.c, L.p, L.me * ep]).astype(jnp.int32)
    raw = ffn_routes.T
    padded = (raw // el) * ep + raw % el

    rt = jnp.where(jnp.arange(T)[None, :] < lengths[0], padded, EP)
    tail = jnp.concatenate([rt // 32, rt % 32], axis=1).astype(bf16)
    cpack = jnp.concatenate([cotangent, jnp.pad(tail, ((0, 0), (0, D - 2 * T)))], axis=0)
    c_far = L.near([cpack] * nz)

    h1, xpack, q, k, v, proj, a, o, gt, a1, a2 = call(
        forward_body,
        [
            ((T, D), f32), ((nz, T + 16, D), bf16), ((T, hd), bf16), ((T, hd), bf16), ((T, hd), bf16),
            ((T, wide), f32), ((heads, T, T), f32), ((T, hd), f32), ((T, 128), f32),
            ((T, D), bf16), ((T, D), bf16),
        ],
        [
            layer_input, value_routes.transpose(1, 2, 0), output_routes.transpose(1, 2, 0), raw,
            att_gain[None], att_shift[None], query_weight, key_weight, value_weight, output_weight,
            value_selector.T, output_selector.T, ffn_gain[None], ffn_shift[None], ffn_selector.T,
        ],
        scratch=[pltpu.VMEM((T, wide), bf16)],
        smem=[lengths],
        name="forward",
    )
    x_far = L.chips(xpack)
    selectors = after((ffn_selector, value_selector, output_selector), xpack)
    fsel = jnp.pad(selectors[0].T, ((0, S * el - ffn_selector.shape[1]), (0, 0)))
    fsel = jnp.pad(fsel.reshape(S, el, D), ((0, 0), (0, ep - el), (0, 0))).reshape(EP, D)
    selw = jnp.pad(jnp.concatenate(selectors[1:], axis=1), ((0, 0), (0, 128 - 2 * he)))
    (early,) = call(
        partial(early_body, n_p, S),
        [((nz, T, hd + 896), bf16)],
        [layer_input, a1, a2, o, gt],
        scratch=[pltpu.VMEM((S, T, 384), bf16)],
        smem=[ids],
        name="early_slices",
    )
    c_msgs = L.relay(jnp.stack(after(c_far, early, fsel, selw)))
    ccols = call(
        partial(columns_body, n_p, True), [((nz, T, Dp), bf16)] * n_p, [after(c_msgs[0], c_msgs[1])], smem=[ids],
        name="cotangent_columns",
    )
    cc_all = [ccols[0], L.plane(ccols[1], 1), L.plane(ccols[2], 2)]
    tail_rows = pl.BlockSpec((nz, 16, 2 * T), lambda i: (0, T // 16, 0))
    code, cnt, routes = pl.pallas_call(
        partial(codes_body, S),
        grid=(1,),
        in_specs=[pl.BlockSpec(memory_space=pltpu.SMEM), tail_rows, tail_rows],
        out_specs=[pl.BlockSpec(memory_space=pltpu.VMEM)] * 3,
        out_shape=[
            jax.ShapeDtypeStruct((pairs, ep, 2 * T), bf16), jax.ShapeDtypeStruct((8, ep), f32),
            jax.ShapeDtypeStruct((S * 16, T), f32),
        ],
        compiler_params=pltpu.CompilerParams(vmem_limit_bytes=VMEM_LIMIT),
        cost_estimate=SHORT,
        name="codes",
    )(ids, *after(c_msgs, ccols))
    x_far = after(x_far, code, cc_all[1:])
    x_msgs = L.relay(x_far)
    xcols = call(
        partial(columns_body, n_p, False), [((nz, T + ep, Dp), bf16)] * n_p, [x_far, code],
        smem=[ids],
        name="token_columns",
    )
    xc_all = L.planes_of(xcols)
    early_far = L.chips(after(early, x_far))

    n_eb = el // eb
    whole = [pl.BlockSpec(memory_space=pltpu.VMEM)]
    dx0, dx1, gy0, gy1, gr, du = pl.pallas_call(
        partial(experts_body, S, eb),
        grid=(n_eb,),
        out_shape=[
            jax.ShapeDtypeStruct((pairs, T + 16, D), bf16), jax.ShapeDtypeStruct((pairs, T + 16, D), bf16),
            jax.ShapeDtypeStruct((pairs, T, D), bf16), jax.ShapeDtypeStruct((pairs, T, D), bf16),
            jax.ShapeDtypeStruct((el, pairs * R, H), bf16), jax.ShapeDtypeStruct((el, pairs * R, H), bf16),
        ],
        in_specs=[pl.BlockSpec(memory_space=pltpu.SMEM)]
        + whole * 5
        + [
            pl.BlockSpec((eb, D, H), lambda i: (i, 0, 0)),
            pl.BlockSpec((eb, H, D), lambda i: (i, 0, 0)),
        ],
        out_specs=whole * 4 + [pl.BlockSpec((eb, pairs * R, H), lambda i: (i, 0, 0))] * 2,
        scratch_shapes=[
            pltpu.VMEM((pairs, ep, 2 * T), f32), pltpu.VMEM((ep, S * T), f32), pltpu.VMEM((ep, S * T), f32),
            pltpu.VMEM((pairs, el * R, 2 * T), bf16),
            pltpu.VMEM((eb * pairs * R, D), bf16), pltpu.VMEM((eb * pairs * R, D), bf16),
            pltpu.VMEM((pairs, el * R, D), bf16), pltpu.VMEM((pairs, el * R, D), bf16),
        ],
        compiler_params=pltpu.CompilerParams(vmem_limit_bytes=VMEM_LIMIT),
        cost_estimate=SHORT,
        name="experts",
    )(after(ids, xcols), *x_msgs, *c_msgs, code, up_weight, down_weight)

    def join(mine, other, name):
        return call(partial(join_body, T), [(mine.shape, bf16)], [mine, L.core(other)], name=name)[0]

    def join_apart(mine, other, name):
        return call(
            partial(join_apart_body, nz), [(mine.shape[1:], bf16)] * nz, [mine, L.core(other)], smem=[ids], name=name
        )

    dx0, dx1, early_far, xc_all = lax.optimization_barrier((dx0, dx1, early_far, xc_all))
    dx_join = join(dx0, dx1, "join_dx")
    dx_parts = L.chips(dx_join)
    gr, du = after((gr, du), dx_join)
    gr1, du1 = L.plane(gr, 1), L.plane(du, 2)
    early_far, gy0, gy1, cc3, xc_all = after((early_far, gy0, gy1, ccols[3], xc_all), dx_join)
    xc_both = L.relay(jnp.stack(xc_all))
    cc_all += [L.plane(cc3, 3)]
    gy_join = join_apart(gy0, gy1, "join_out")
    z_all, a2_s, lia1, hat_s, gates, wsl = call(
        partial(spread_body, S, n_p, w, heads, ea),
        [
            ((S * T, wide), bf16), ((S * T, 128), bf16), ((256, S * T), bf16), ((128, S * T), f32),
            ((S * T, 128), f32), ((128, 2 * hd + 128), bf16),
        ],
        [*L.relay(early_far), query_weight, key_weight, selw],
        smem=[ids],
        cost=LONG,
        name="spread_tokens",
    )
    dx_parts, gr1, du1, z_all, gy_join, cc_all, xc_both = lax.optimization_barrier(
        (dx_parts, gr1, du1, z_all, gy_join, cc_all, xc_both)
    )
    cols_both = xc_both + L.relay(jnp.stack(cc_all))
    gr, du = after((gr, du), dx_parts)
    gr_all = [gr, gr1, L.plane(gr, 2)]
    du_all = [du, L.plane(du, 1), du1]

    dh1, db, mid = call(
        partial(ffn_back_body, n_p, S, nz),
        [((T, D), f32), ((T, D), bf16), ((nz, T + 32, 256), bf16)],
        [dx_parts, h1, cotangent, fsel, ffn_gain[None], padded, cnt],
        scratch=[pltpu.VMEM((EP, T), f32), pltpu.VMEM((S, T, 128), bf16)],
        smem=[ids],
        name="ffn_back",
    )
    mid_far = L.chips(mid)
    late, dp = call(
        attention_back_body,
        [((nz, T, 3 * hd + 128), bf16), ((T, wide), bf16)],
        [db, output_weight, gt, o, q, k, v, a, proj],
        cost=LONG,
        name="attention_back",
    )
    late = after(late, mid_far, gr_all[2], du_all[1])
    gr1, du1 = after((gr1, du1), late)
    gr_all += [L.plane(gr1, 2)]
    du_all += [L.plane(du1, 1)]
    late_far = L.chips(late)
    (input_grad,) = call(
        input_back_body,
        [((T, D), f32)],
        [late, dp, query_weight, key_weight, value_weight, selw, layer_input, att_gain[None], dh1],
        name="input_back",
    )
    mid_far = after(mid_far, input_grad)
    grads_a = call(
        partial(out_grads_body, S, n_p, w),
        [((w, wide + EP + 128), f32)] + [((w, wide + EP + 128), bf16)] * (n_p - 1),
        [*L.relay(mid_far), z_all, a2_s, routes],
        scratch=[
            pltpu.VMEM((128, wide + EP), f32), pltpu.VMEM((S * T, 128), bf16),
            pltpu.VMEM((EP, S * T), bf16), pltpu.VMEM((16, 128), f32),
        ],
        smem=[ids],
        name="out_grads",
    )
    a_parts = L.planes_of(grads_a)
    def expert_grads(first, last, args, so_far=()):
        n = len(args)
        return pl.pallas_call(
            partial(expert_grads_body, n_p, eb, first),
            grid=(last - first,),
            in_specs=whole * 4
            + [pl.BlockSpec((eb, pairs * R, H), lambda i: (i + first, 0, 0))] * (2 * n_p)
            + [pl.BlockSpec(memory_space=pl.ANY)] * len(so_far),
            out_specs=[
                pl.BlockSpec((eb, Dp, H), lambda i: (i + first, 0, 0)),
                pl.BlockSpec((eb, H, Dp), lambda i: (i + first, 0, 0)),
            ],
            scratch_shapes=[
                pltpu.VMEM((n_p * pairs, ep, 2 * T), f32),
                pltpu.VMEM((eb * n_p * pairs * R, 2 * Dp), bf16),
            ],
            out_shape=[jax.ShapeDtypeStruct((el, Dp, H), f32), jax.ShapeDtypeStruct((el, H, Dp), f32)],
            input_output_aliases={n + i: i for i in range(len(so_far))},
            compiler_params=pltpu.CompilerParams(vmem_limit_bytes=VMEM_LIMIT),
            cost_estimate=SHORT,
            name="expert_grads",
        )(*args, *so_far)

    cut = (n_eb + 1) // 2
    grads_in = (*cols_both, *after(gr_all + du_all, grads_a))
    half = expert_grads(0, cut, grads_in)
    late_far, a_parts, half = lax.optimization_barrier((late_far, a_parts, half))
    gy_parts = L.near(after(gy_join, late_far))
    late_block = pl.BlockSpec((1, T, 3 * hd + 128), lambda i: (i, 0, 0))
    grads_b = pl.pallas_call(
        partial(in_grads_body, n_p, heads, ea, w, hd),
        grid=(nz,),
        in_specs=[
            pl.BlockSpec(memory_space=pltpu.SMEM), late_block, late_block,
            pl.BlockSpec((256, 2 * T), lambda i: (0, i)), pl.BlockSpec((128, 2 * T), lambda i: (0, i)),
            pl.BlockSpec((2 * T, 128), lambda i: (i, 0)), whole[0],
        ],
        out_specs=whole * n_p,
        out_shape=[
            jax.ShapeDtypeStruct((w, wide + 2 * hd + 128), f32 if s == 0 else bf16) for s in range(n_p)
        ],
        scratch_shapes=[
            pltpu.VMEM((128, wide + 2 * hd + 128), f32), pltpu.VMEM((2 * T, wide), bf16),
            pltpu.VMEM((2 * T, 2 * hd + 128), bf16), pltpu.VMEM((128, 128), f32),
        ],
        compiler_params=pltpu.CompilerParams(vmem_limit_bytes=VMEM_LIMIT),
        cost_estimate=LONG,
        name="in_grads",
    )(ids, *L.relay(late_far), lia1, hat_s, gates, wsl)
    b_parts = L.planes_of(grads_b)
    up_grad, down_grad = expert_grads(cut, n_eb, after(grads_in, grads_b), half)

    output_grad, fgrad, ffn_gain_grad, ffn_shift_grad, counts = call(
        partial(last_a_body, n_p, S, w, el),
        [((w, wide), f32), ((w, EXPERTS), f32), ((1, w), f32), ((1, w), f32), ((1, EXPERTS), f32)],
        after(a_parts, up_grad),
        scratch=[pltpu.VMEM((8, 128), f32)],
        smem=[ids],
        name="last_sum_a",
    )
    gy_parts, b_parts = after((gy_parts, b_parts), fgrad)
    output = (h1 + sum(m.astype(f32) for m in gy_parts)).astype(bf16)
    value_grad, query_grad, key_grad, vsel, osel, att_gain_grad, att_shift_grad = call(
        partial(last_b_body, n_p, w, hd, he),
        [
            ((w, wide), f32), ((w, hd), f32), ((w, hd), f32), ((he, w), f32), ((he, w), f32),
            ((1, w), f32), ((1, w), f32),
        ],
        after(b_parts, output),
        name="last_sum_b",
    )
    return (
        output, input_grad, att_gain_grad[0], att_shift_grad[0], query_grad, key_grad, value_grad,
        output_grad.T, vsel.T, osel.T, ffn_gain_grad[0], ffn_shift_grad[0], fgrad, up_grad, down_grad, counts[0],
    )


def solution(mesh):
    path = fast_path if mesh.shape["expert"] == 8 and mesh.shape["dp"] == 4 else general_path
    placed = (
        P(("dp", "expert"), None),
        P(("dp", "expert"), None),
        P(("dp", "expert")),
        P(("dp", "expert"), None, None),
        P(("dp", "expert"), None, None),
        P(("dp", "expert"), None),
        P(),
        P(),
        P(),
        P(),
        P(),
        P(),
        P(),
        P(),
        P(),
        P(),
        P(),
        P("expert", None, None),
        P("expert", None, None),
    )
    return jax.shard_map(
        path,
        mesh=mesh,
        in_specs=placed,
        out_specs=(
            P(("dp", "expert"), None),
            P(("dp", "expert"), None),
            P(("dp", "expert")),
            P(("dp", "expert")),
            P(("dp", "expert"), None),
            P(("dp", "expert"), None),
            P(("dp", "expert"), None),
            P(None, ("dp", "expert")),
            P(("dp", "expert"), None),
            P(("dp", "expert"), None),
            P(("dp", "expert")),
            P(("dp", "expert")),
            P(("dp", "expert"), None),
            P("expert", "dp", None),
            P("expert", None, "dp"),
            P(),
        ),
        check_vma=False,
    )
```

profile of v0, /device:TPU:0, one launch (start us, length us, event | category | flops | bytes accessed | tf_op | source)
XLA Modules:
  0.0 241.1 jit_solution(8735703764641405859)
XLA Ops:
  2.6 1.0 pad_maximum_fusion.3
  3.6 5.1 %collective-permute-start.2 = (bf16[144,1024]{1,0:T(8,128)(2,1)S(1)}, bf16[144,1024]{1,0:T(8,128)(2,1)S(1)}, u32[]{:S(2)}, u32[]{:S(2)}) collective-permute-start(bf16[144,1024]{1,0:T(8,128)(2,1)S(1)} %pad_maximum_fusion.3), channel_id=1, source_target_pairs={{0,6},{1,7},{2,4},{3,5},{4,2},{5,3},{6,0},{7,1},{8,14},{9,15},{10,... | collective-permute-start | bytes 884744 | tf_op jit(solution)/shard_map/ppermute | solution.py:936
  9.4 10.7 %forward.1 = (f32[128,1024]{1,0:T(8,128)}, bf16[4,144,1024]{2,1,0:T(8,128)(2,1)}, bf16[128,512]{1,0:T(8,128)(2,1)}, bf16[128,512]{1,0:T(8,128)(2,1)}, bf16[128,5...) custom-call(s32[1]{0:T(128)} %copy.44.length, ...), custom_call_target="tpu_custom_call" | custom-call | flops 1 | bytes 1 | tf_op jit(solution)/shard_map/forward/pallas_call | solution.py:335
  20.0 5.0 %all-to-all-start = ((bf16[4,144,1024]{2,1,0:T(8,128)(2,1)}), bf16[4,144,1024]{2,1,0:T(8,128)(2,1)S(1)}, u32[]{:S(2)}, u32[]{:S(2)}) async-start(bf16[4,144,1024]{2,1,0:T(8,128)(2,1)} %get-tuple-element.181), calls=%async_computation | async-start | bytes 2359296 | tf_op jit(solution)/shard_map/all_to_all | solution.py:926
  25.7 3.2 %early_slices.1 = bf16[4,128,1408]{2,1,0:T(8,128)(2,1)} custom-call(s32[4]{0:T(128)} %pad_add_fusion.ids, bf16[128,1024]{1,0:T(8,128)(2,1)} %li.5, bf16[128,1024]{1,0:T(8,128)(2,1)} %get-tuple-element.182.a1, bf16[128,1024]{1,0:T(8,128)(2,1)} %get-tuple-element.183.a2, f32[128,512]{1,0:T(8,128)} %get-tuple-element.184.o, f32[128,128]{1,0:T(8,128)} %get-tuple-element.185.gt), custom_call_target="tpu_custom_call" | custom-call | flops 1 | bytes 1 | tf_op jit(solution)/shard_map/early_slices/pallas_call | solution.py:335
  29.0 0.8 pad.19.selw
  30.1 1.1 pad.18
  31.2 12.2 %collective-permute-done.1 = bf16[144,1024]{1,0:T(8,128)(2,1)} collective-permute-done((bf16[144,1024]{1,0:T(8,128)(2,1)S(1)}, bf16[144,1024]{1,0:T(8,128)(2,1)}, u32[]{:S(2)}, u32[]{:S(2)}) %collective-permute-start.1) | collective-permute-done | bytes 294944 | tf_op jit(solution)/shard_map/ppermute | solution.py:936
  43.4 1.2 pad_maximum_fusion.1.x.refs_0_.refs_2_
  44.7 2.8 %collective-permute-done.3.refs_1_.refs_3_ = bf16[4,144,1024]{2,1,0:T(8,128)(2,1)S(1)} collective-permute-done((bf16[4,144,1024]{2,1,0:T(8,128)(2,1)S(1)}, bf16[4,144,1024]{2,1,0:T(8,128)(2,1)S(1)}, u32[]{:S(2)}, u32[]{:S(2)}) %collective-permute-start.3) | collective-permute-done | bytes 1179680 | tf_op jit(solution)/shard_map/ppermute | solution.py:922
  47.5 2.8 %cotangent_columns.1 = (bf16[4,128,256]{2,1,0:T(8,128)(2,1)}, bf16[4,128,256]{2,1,0:T(8,128)(2,1)}, bf16[4,128,256]{2,1,0:T(8,128)(2,1)}, bf16[4,128,256]{2,1,0:T(8,128)(2,1)}) custom-call(s32[4]{0:T(128)} %pad_add_fusion.ids, bf16[4,144,1024]{2,1,0:T(8,128)(2,1)} %copy-done), custom_call_target="tpu_custom_call" | custom-call | flops 1 | bytes 1 | tf_op jit(solution)/shard_map/cotangent_columns/pallas_call | solution.py:335
  50.3 1.5 collective-permute-start.4
  51.8 1.5 collective-permute-start.5
  53.4 1.9 codes.1
  55.3 3.6 %collective-permute-done.4 = bf16[4,128,256]{2,1,0:T(8,128)(2,1)S(1)} collective-permute-done((bf16[4,128,256]{2,1,0:T(8,128)(2,1)}, bf16[4,128,256]{2,1,0:T(8,128)(2,1)S(1)}, u32[]{:S(2)}, u32[]{:S(2)}) %collective-permute-start.4) | collective-permute-done | bytes 262176 | tf_op jit(solution)/shard_map/ppermute | solution.py:932
  60.2 3.7 %all-to-all-start.1 = ((bf16[4,128,1408]{2,1,0:T(8,128)(2,1)}), bf16[4,128,1408]{2,1,0:T(8,128)(2,1)S(1)}, u32[]{:S(2)}, u32[]{:S(2)}) async-start(bf16[4,128,1408]{2,1,0:T(8,128)(2,1)} %early_slices.1), calls=%async_computation.1 | async-start | bytes 2883584 | tf_op jit(solution)/shard_map/all_to_all | solution.py:926
  64.0 2.6 %token_columns.1 = (bf16[4,192,256]{2,1,0:T(8,128)(2,1)}, bf16[4,192,256]{2,1,0:T(8,128)(2,1)}, bf16[4,192,256]{2,1,0:T(8,128)(2,1)}, bf16[4,192,256]{2,1,0:T(8,128)(2,1)}) custom-call(s32[4]{0:T(128)} %pad_add_fusion.ids, bf16[4,144,1024]{2,1,0:T(8,128)(2,1)} %copy-done.2, bf16[4,64,256]{2,1,0:T(8,128)(2,1)} %get-tuple-element.200.refs_0_.refs_4_), custom_call_target="tpu_custom_call" | custom-call | flops 1 | bytes 1 | tf_op jit(solution)/shard_map/token_columns/pallas_call | solution.py:335
  66.6 0.9 collective-permute-start.7
  67.5 1.5 collective-permute-start.8
  69.0 1.1 collective-permute-start.9
  70.1 1.1 copy-done.22
  71.2 31.7 %experts.1 = (bf16[4,144,1024]{2,1,0:T(8,128)(2,1)}, bf16[4,144,1024]{2,1,0:T(8,128)(2,1)}, bf16[4,128,1024]{2,1,0:T(8,128)(2,1)}, bf16[4,128,1024]{2,1,0:T(8,12...) custom-call(s32[4]{0:T(128)} %pad_add_fusion.ids, bf16[4,144,1024]{2,1,0:T(8,128)(2,1)} %copy-done.2, ...), custom_call_target="tpu_custom_call" | custom-call | flops 1 | bytes 1 | tf_op jit(solution)/shard_map/experts/pallas_call | solution.py:1036
  103.0 3.0 %collective-permute-done.10.recv = bf16[4,144,1024]{2,1,0:T(8,128)(2,1)S(1)} collective-permute-done((bf16[4,144,1024]{2,1,0:T(8,128)(2,1)}, bf16[4,144,1024]{2,1,0:T(8,128)(2,1)S(1)}, u32[]{:S(2)}, u32[]{:S(2)}) %collective-permute-start.10) | collective-permute-done | bytes 1179680 | tf_op jit(solution)/shard_map/ppermute | solution.py:922
  106.1 1.0 copy-done.23
  107.1 3.0 %join_dx.1 = bf16[4,144,1024]{2,1,0:T(8,128)(2,1)} custom-call(bf16[4,144,1024]{2,1,0:T(8,128)(2,1)} %get-tuple-element.210.mine, bf16[4,144,1024]{2,1,0:T(8,128)(2,1)} %copy-done.23), custom_call_target="tpu_custom_call" | custom-call | flops 1 | bytes 1 | tf_op jit(solution)/shard_map/join_dx/pallas_call | solution.py:335
  110.1 4.9 %all-to-all-start.2 = ((bf16[4,144,1024]{2,1,0:T(8,128)(2,1)}), bf16[4,144,1024]{2,1,0:T(8,128)(2,1)S(1)}, u32[]{:S(2)}, u32[]{:S(2)}) async-start(bf16[4,144,1024]{2,1,0:T(8,128)(2,1)} %join_dx.1), calls=%async_computation.2 | async-start | bytes 2359296 | tf_op jit(solution)/shard_map/all_to_all | solution.py:926
  115.0 1.5 pad_maximum_fusion.xm
  117.2 0.9 collective-permute-start.11
  118.1 1.5 collective-permute-start.12
  119.6 4.3 %collective-permute-done.14.recv = bf16[4,128,1024]{2,1,0:T(8,128)(2,1)} collective-permute-done((bf16[4,128,1024]{2,1,0:T(8,128)(2,1)}, bf16[4,128,1024]{2,1,0:T(8,128)(2,1)}, u32[]{:S(2)}, u32[]{:S(2)}) %collective-permute-start.14) | collective-permute-done | bytes 1048608 | tf_op jit(solution)/shard_map/ppermute | solution.py:922
  123.9 1.9 collective-permute-start.15
  125.7 2.7 %join_out.1 = (bf16[128,1024]{1,0:T(8,128)(2,1)}, bf16[128,1024]{1,0:T(8,128)(2,1)}, bf16[128,1024]{1,0:T(8,128)(2,1)}, bf16[128,1024]{1,0:T(8,128)(2,1)}) custom-call(s32[4]{0:T(128)} %pad_add_fusion.ids, bf16[4,128,1024]{2,1,0:T(8,128)(2,1)} %get-tuple-element.225.mine, bf16[4,128,1024]{2,1,0:T(8,128)(2,1)} %collective-permute-done.14.recv), custom_call_target="tpu_custom_call" | custom-call | flops 1 | bytes 1 | tf_op jit(solution)/shard_map/join_out/pallas_call | solution.py:335
  128.4 9.2 %spread_tokens.1 = (bf16[1024,2560]{1,0:T(8,128)(2,1)}, bf16[1024,128]{1,0:T(8,128)(2,1)}, bf16[256,1024]{1,0:T(8,128)(2,1)}, f32[128,1024]{1,0:T(8,128)}, f32[1...) custom-call(s32[4]{0:T(128)} %pad_add_fusion.ids, bf16[4,128,1408]{2,1,0:T(8,128)(2,1)} %copy-done.6, ...), custom_call_target="tpu_custom_call" | custom-call | flops 1 | bytes 268435456 | tf_op jit(solution)/shard_map/spread_tokens/pallas_call | solution.py:335
  137.6 6.5 %collective-permute-done.15 = bf16[4,128,256]{2,1,0:T(8,128)(2,1)} collective-permute-done((bf16[4,128,256]{2,1,0:T(8,128)(2,1)}, bf16[4,128,256]{2,1,0:T(8,128)(2,1)}, u32[]{:S(2)}, u32[]{:S(2)}) %collective-permute-start.15) | collective-permute-done | bytes 262176 | tf_op jit(solution)/shard_map/ppermute | solution.py:932
  144.1 0.9 copy-done.13
  145.7 0.9 collective-permute-start.18
  146.6 4.3 %ffn_back.1 = (f32[128,1024]{1,0:T(8,128)}, bf16[128,1024]{1,0:T(8,128)(2,1)}, bf16[4,160,256]{2,1,0:T(8,128)(2,1)}) custom-call(s32[4]{0:T(128)} %pad_add_fusion.ids, bf16[4,144,1024]{2,1,0:T(8,128)(2,1)} %copy-done.9, f32[128,1024]{1,0:T(8,128)} %get-tuple-element.180.h1, bf16[128,1024]{1,0:T(8,128)(2,1)} %c.1, bf16[512,1024]{1,0:T(8,128)(2,1)} %bitcast.40, ...), custom_call_target="tpu_custom_call" | custom-call | flops 1 | bytes 1 | tf_op jit(solution)/shard_map/ffn_back/pallas_call | solution.py:335
  150.9 5.1 %all-to-all-start.3 = ((bf16[4,160,256]{2,1,0:T(8,128)(2,1)}), bf16[4,160,256]{2,1,0:T(8,128)(2,1)S(1)}, u32[]{:S(2)}, u32[]{:S(2)}) async-start(bf16[4,160,256]{2,1,0:T(8,128)(2,1)} %get-tuple-element.249), calls=%async_computation.3 | async-start | bytes 655360 | tf_op jit(solution)/shard_map/all_to_all | solution.py:926
  156.0 7.5 %attention_back.1 = (bf16[4,128,1664]{2,1,0:T(8,128)(2,1)}, bf16[128,2560]{1,0:T(8,128)(2,1)}) custom-call(bf16[128,1024]{1,0:T(8,128)(2,1)} %get-tuple-element.242.db, bf16[2560,1024]{1,0:T(8,128)(2,1)} %wo.3, f32[128,128]{1,0:T(8,128)} %get-tuple-element.185.gt, f32[128,512]{1,0:T(8,128)} %get-tuple-element.184.o, bf16[128,512]{1,0:T(8,128)(2,1)} %get-tuple-element.243.q, ...), custom_call_target="tpu_custom_call" | custom-call | flops 1 | bytes 268435456 | tf_op jit(solution)/shard_map/attention_back/pallas_call | solution.py:335
  163.5 2.0 all-to-all-done.3.m0
  166.3 4.1 %all-to-all-start.4 = ((bf16[4,128,1664]{2,1,0:T(8,128)(2,1)}), bf16[4,128,1664]{2,1,0:T(8,128)(2,1)S(1)}, u32[]{:S(2)}, u32[]{:S(2)}) async-start(bf16[4,128,1664]{2,1,0:T(8,128)(2,1)} %get-tuple-element.252.late), calls=%async_computation.4 | async-start | bytes 3407872 | tf_op jit(solution)/shard_map/all_to_all | solution.py:926
  170.3 1.2 pad_maximum_fusion.2.cm
  171.7 1.6 collective-permute-start.24
  173.2 0.9 collective-permute-start.25
  174.1 7.5 %input_back.1 = f32[128,1024]{1,0:T(8,128)} custom-call(bf16[4,128,1664]{2,1,0:T(8,128)(2,1)} %get-tuple-element.252.late, bf16[128,2560]{1,0:T(8,128)(2,1)} %get-tuple-element.253.dp, bf16[1024,512]{1,0:T(8,128)(2,1)} %wq.5, bf16[1024,512]{1,0:T(8,128)(2,1)} %wk.5, bf16[1024,2560]{1,0:T(8,128)(2,1)} %wv.3, bf16[1024,128]{1,0:T(8,128)(2,1)} %pad.19.selw, ...), custom_call_target="tpu_custom_call" | custom-call | flops 1 | bytes 1 | tf_op jit(solution)/shard_map/input_back/pallas_call | solution.py:335
  181.7 1.6 collective-permute-done.19.m1
  184.0 7.3 %out_grads.1 = (f32[32,3200]{1,0:T(8,128)}, bf16[32,3200]{1,0:T(8,128)(2,1)}, bf16[32,3200]{1,0:T(8,128)(2,1)}, bf16[32,3200]{1,0:T(8,128)(2,1)}) custom-call(s32[4]{0:T(128)} %pad_add_fusion.ids, bf16[4,160,256]{2,1,0:T(8,128)(2,1)} %copy-done.20, bf16[4,160,256]{2,1,0:T(8,128)(2,1)} %copy-done.26, bf16[1024,2560]{1,0:T(8,128)(2,1)} %get-tuple-element.256.z, ...), custom_call_target="tpu_custom_call" | custom-call | flops 1 | bytes 1 | tf_op jit(solution)/shard_map/out_grads/pallas_call | solution.py:335
  191.3 1.1 collective-permute-start.20
  193.0 1.8 collective-permute-start.22
  194.8 0.9 copy-done.16
  195.7 1.0 copy-done.10
  196.7 10.1 %expert_grads.2 = (f32[49,256,128]{2,1,0:T(8,128)}, f32[49,128,256]{2,1,0:T(8,128)}) custom-call(bf16[4,4,192,256]{3,2,1,0:T(8,128)(2,1)} %copy-done.1, bf16[4,4,192,256]{3,2,1,0:T(8,128)(2,1)} %copy-done.5, bf16[4,4,128,256]{3,2,1,0:T(8,128)(2,1)} %copy-done.3, bf16[4,4,128,256]{3,2,1,0:T(8,128)(2,1)} %copy-done.10, ...), custom_call_target="tpu_custom_call" | custom-call | flops 1 | bytes 1 | tf_op jit(solution)/shard_map/expert_grads/pallas_call | solution.py:1140
  206.9 1.8 all-to-all-done.4.l0
  209.1 2.3 collective-permute-start.27
  211.4 1.7 collective-permute-start.28
  213.1 1.2 copy-done.19
  214.3 9.0 %in_grads.1 = (f32[32,3712]{1,0:T(8,128)}, bf16[32,3712]{1,0:T(8,128)(2,1)}, bf16[32,3712]{1,0:T(8,128)(2,1)}, bf16[32,3712]{1,0:T(8,128)(2,1)}) custom-call(s32[4]{0:T(128)} %pad_add_fusion.ids, bf16[4,128,1664]{2,1,0:T(8,128)(2,1)} %copy-done.4, bf16[4,128,1664]{2,1,0:T(8,128)(2,1)} %copy-done.19, bf16[256,1024]{1,0:T(8,128)(2,1)} %get-tuple-element.288.lia1, ...), custom_call_target="tpu_custom_call" | custom-call | flops 1 | bytes 268435456 | tf_op jit(solution)/shard_map/in_grads/pallas_call | solution.py:1167
  223.4 0.9 collective-permute-start.30
  224.3 1.5 collective-permute-start.31
  225.8 1.0 collective-permute-start.32
  226.9 8.9 %expert_grads.3 = (f32[49,256,128]{2,1,0:T(8,128)}, f32[49,128,256]{2,1,0:T(8,128)}) custom-call(bf16[4,4,192,256]{3,2,1,0:T(8,128)(2,1)} %copy-done.1, bf16[4,4,192,256]{3,2,1,0:T(8,128)(2,1)} %copy-done.5, bf16[4,4,128,256]{3,2,1,0:T(8,128)(2,1)} %copy-done.3, bf16[4,4,128,256]{3,2,1,0:T(8,128)(2,1)} %copy-done.10, ...), custom_call_target="tpu_custom_call", output_to_operand_aliasing={{0}: (12, {}), {1}: (13, {})} | custom-call | flops 1 | bytes 1 | tf_op jit(solution)/shard_map/expert_grads/pallas_call | solution.py:1140
  235.8 2.1 last_sum_a.1
  238.0 0.9 add_convert_fusion
  238.9 2.1 last_sum_b.1
  (132 shorter events, 8.6 us)
Async XLA Ops:
  3.6 27.6 %collective-permute-start.2 = (bf16[144,1024]{1,0:T(8,128)(2,1)S(1)}, bf16[144,1024]{1,0:T(8,128)(2,1)S(1)}, u32[]{:S(2)}, u32[]{:S(2)}) collective-permute-start(bf16[144,1024]{1,0:T(8,128)(2,1)S(1)} %pad_maximum_fusion.3), channel_id=1, source_target_pairs={{0,6},{1,7},{2,4},{3,5},{4,2},{5,3},{6,0},{7,1},{8,14},{9,15},{10,... | collective-permute-start | bytes 884744 | tf_op jit(solution)/shard_map/ppermute | solution.py:936
  8.7 34.7 %collective-permute-start.1 = (bf16[144,1024]{1,0:T(8,128)(2,1)S(1)}, bf16[144,1024]{1,0:T(8,128)(2,1)}, u32[]{:S(2)}, u32[]{:S(2)}) collective-permute-start(bf16[144,1024]{1,0:T(8,128)(2,1)S(1)} %pad_maximum_fusion.3), channel_id=1, source_target_pairs={{0,4},{1,5},{2,6},{3,7},{4,0},{5,1},{6,2},{7,3},{8,12},{9,13},{10,... | collective-permute-start | bytes 884744 | tf_op jit(solution)/shard_map/ppermute | solution.py:936
  8.7 34.7 %collective-permute-start = (bf16[144,1024]{1,0:T(8,128)(2,1)S(1)}, bf16[144,1024]{1,0:T(8,128)(2,1)}, u32[]{:S(2)}, u32[]{:S(2)}) collective-permute-start(bf16[144,1024]{1,0:T(8,128)(2,1)S(1)} %pad_maximum_fusion.3), channel_id=1, source_target_pairs={{0,2},{1,3},{2,0},{3,1},{4,6},{5,7},{6,4},{7,5},{8,10},{9,11},{10,... | collective-permute-start | bytes 884744 | tf_op jit(solution)/shard_map/ppermute | solution.py:936
  20.0 40.2 %all-to-all-start = ((bf16[4,144,1024]{2,1,0:T(8,128)(2,1)}), bf16[4,144,1024]{2,1,0:T(8,128)(2,1)S(1)}, u32[]{:S(2)}, u32[]{:S(2)}) async-start(bf16[4,144,1024]{2,1,0:T(8,128)(2,1)} %get-tuple-element.181), calls=%async_computation | async-start | bytes 2359296 | tf_op jit(solution)/shard_map/all_to_all | solution.py:926
  25.1 3.8 %copy-start.37 = (bf16[1024,20]{0,1:T(8,128)(2,1)S(1)}, bf16[1024,20]{0,1:T(8,128)(2,1)}, u32[]{:S(2)}) copy-start(bf16[1024,20]{0,1:T(8,128)(2,1)} %param.31) | copy-start | bytes 122884
  25.1 3.8 %copy-start.38 = (bf16[1024,20]{0,1:T(8,128)(2,1)S(1)}, bf16[1024,20]{0,1:T(8,128)(2,1)}, u32[]{:S(2)}) copy-start(bf16[1024,20]{0,1:T(8,128)(2,1)} %param.32) | copy-start | bytes 122884
  25.7 4.1 %copy-start.17 = (bf16[1024,387]{0,1:T(8,128)(2,1)S(1)}, bf16[1024,387]{0,1:T(8,128)(2,1)}, u32[]{:S(2)}) copy-start(bf16[1024,387]{0,1:T(8,128)(2,1)} %param.35) | copy-start | bytes 2377732
  44.6 2.9 %copy-start = (bf16[4,144,1024]{2,1,0:T(8,128)(2,1)}, bf16[4,144,1024]{2,1,0:T(8,128)(2,1)S(1)}, u32[]{:S(2)}) copy-start(bf16[4,144,1024]{2,1,0:T(8,128)(2,1)S(1)} %pad_maximum_fusion.1.x.refs_0_.refs_2_) | copy-start | bytes 3538948
  44.6 2.9 %collective-permute-start.3 = (bf16[4,144,1024]{2,1,0:T(8,128)(2,1)S(1)}, bf16[4,144,1024]{2,1,0:T(8,128)(2,1)S(1)}, u32[]{:S(2)}, u32[]{:S(2)}) collective-permute-start(bf16[4,144,1024]{2,1,0:T(8,128)(2,1)S(1)} %pad_maximum_fusion.1.x.refs_0_.refs_2_), channel_id=1, source_target_pairs={{0,1},{1,0},{2,3},{3,2},{4,5},{5,4},{6,7},{7,6},{8,9},{9,8},{10,11... | collective-permute-start | bytes 3538952 | tf_op jit(solution)/shard_map/ppermute | solution.py:922
  47.5 5.8 %copy-start.8 = (bf16[4,144,1024]{2,1,0:T(8,128)(2,1)}, bf16[4,144,1024]{2,1,0:T(8,128)(2,1)S(1)}, u32[]{:S(2)}) copy-start(bf16[4,144,1024]{2,1,0:T(8,128)(2,1)S(1)} %collective-permute-done.3.refs_1_.refs_3_) | copy-start | bytes 3538948
  50.3 8.6 %collective-permute-start.4 = (bf16[4,128,256]{2,1,0:T(8,128)(2,1)}, bf16[4,128,256]{2,1,0:T(8,128)(2,1)S(1)}, u32[]{:S(2)}, u32[]{:S(2)}) collective-permute-start(bf16[4,128,256]{2,1,0:T(8,128)(2,1)} %get-tuple-element.195), channel_id=1, source_target_pairs={{0,8},{8,0},{16,24},{24,16},{1,9},{9,1},{17,25},{25,17},{2,10},{10... | collective-permute-start | bytes 786440 | tf_op jit(solution)/shard_map/ppermute | solution.py:932
  51.8 8.4 %collective-permute-start.5 = (bf16[4,128,256]{2,1,0:T(8,128)(2,1)}, bf16[4,128,256]{2,1,0:T(8,128)(2,1)}, u32[]{:S(2)}, u32[]{:S(2)}) collective-permute-start(bf16[4,128,256]{2,1,0:T(8,128)(2,1)} %get-tuple-element.196), channel_id=1, source_target_pairs={{0,16},{8,24},{16,0},{24,8},{1,17},{9,25},{17,1},{25,9},{2,18},{10... | collective-permute-start | bytes 786440 | tf_op jit(solution)/shard_map/ppermute | solution.py:932
  60.2 3.8 %copy-start.2 = (bf16[4,144,1024]{2,1,0:T(8,128)(2,1)}, bf16[4,144,1024]{2,1,0:T(8,128)(2,1)S(1)}, u32[]{:S(2)}) copy-start(bf16[4,144,1024]{2,1,0:T(8,128)(2,1)S(1)} %all-to-all-done.x.refs_0_) | copy-start | bytes 3538948
  60.2 42.7 %all-to-all-start.1 = ((bf16[4,128,1408]{2,1,0:T(8,128)(2,1)}), bf16[4,128,1408]{2,1,0:T(8,128)(2,1)S(1)}, u32[]{:S(2)}, u32[]{:S(2)}) async-start(bf16[4,128,1408]{2,1,0:T(8,128)(2,1)} %early_slices.1), calls=%async_computation.1 | async-start | bytes 2883584 | tf_op jit(solution)/shard_map/all_to_all | solution.py:926
  63.9 6.1 %collective-permute-start.6 = (bf16[4,144,1024]{2,1,0:T(8,128)(2,1)S(1)}, bf16[4,144,1024]{2,1,0:T(8,128)(2,1)S(1)}, u32[]{:S(2)}, u32[]{:S(2)}) collective-permute-start(bf16[4,144,1024]{2,1,0:T(8,128)(2,1)S(1)} %all-to-all-done.x.refs_0_), channel_id=1, source_target_pairs={{0,1},{1,0},{2,3},{3,2},{4,5},{5,4},{6,7},{7,6},{8,9},{9,8},{10,11... | collective-permute-start | bytes 3538952 | tf_op jit(solution)/shard_map/ppermute | solution.py:922
  66.6 36.3 %collective-permute-start.7 = (bf16[4,192,256]{2,1,0:T(8,128)(2,1)}, bf16[4,192,256]{2,1,0:T(8,128)(2,1)S(1)}, u32[]{:S(2)}, u32[]{:S(2)}) collective-permute-start(bf16[4,192,256]{2,1,0:T(8,128)(2,1)} %get-tuple-element.203), channel_id=1, source_target_pairs={{0,8},{8,0},{16,24},{24,16},{1,9},{9,1},{17,25},{25,17},{2,10},{10... | collective-permute-start | bytes 1179656 | tf_op jit(solution)/shard_map/ppermute | solution.py:932
  67.5 35.4 %collective-permute-start.8 = (bf16[4,192,256]{2,1,0:T(8,128)(2,1)}, bf16[4,192,256]{2,1,0:T(8,128)(2,1)S(1)}, u32[]{:S(2)}, u32[]{:S(2)}) collective-permute-start(bf16[4,192,256]{2,1,0:T(8,128)(2,1)} %get-tuple-element.204), channel_id=1, source_target_pairs={{0,16},{8,24},{16,0},{24,8},{1,17},{9,25},{17,1},{25,9},{2,18},{10... | collective-permute-start | bytes 1179656 | tf_op jit(solution)/shard_map/ppermute | solution.py:932
  69.0 33.9 %collective-permute-start.9 = (bf16[4,192,256]{2,1,0:T(8,128)(2,1)}, bf16[4,192,256]{2,1,0:T(8,128)(2,1)}, u32[]{:S(2)}, u32[]{:S(2)}) collective-permute-start(bf16[4,192,256]{2,1,0:T(8,128)(2,1)} %get-tuple-element.205), channel_id=1, source_target_pairs={{0,24},{8,16},{16,8},{24,0},{1,25},{9,17},{17,9},{25,1},{2,26},{10... | collective-permute-start | bytes 1179656 | tf_op jit(solution)/shard_map/ppermute | solution.py:932
  102.9 3.2 %copy-start.25 = (bf16[4,192,256]{2,1,0:T(8,128)(2,1)}, bf16[4,192,256]{2,1,0:T(8,128)(2,1)S(1)}, u32[]{:S(2)}) copy-start(bf16[4,192,256]{2,1,0:T(8,128)(2,1)S(1)} %collective-permute-done.8) | copy-start | bytes 1179652
  102.9 7.1 %copy-start.6 = (bf16[4,128,1408]{2,1,0:T(8,128)(2,1)}, bf16[4,128,1408]{2,1,0:T(8,128)(2,1)S(1)}, u32[]{:S(2)}) copy-start(bf16[4,128,1408]{2,1,0:T(8,128)(2,1)S(1)} %all-to-all-done.1.e0) | copy-start | bytes 4325380
  103.0 3.1 %collective-permute-start.10 = (bf16[4,144,1024]{2,1,0:T(8,128)(2,1)}, bf16[4,144,1024]{2,1,0:T(8,128)(2,1)S(1)}, u32[]{:S(2)}, u32[]{:S(2)}) collective-permute-start(bf16[4,144,1024]{2,1,0:T(8,128)(2,1)} %get-tuple-element.211), channel_id=1, source_target_pairs={{0,1},{1,0},{2,3},{3,2},{4,5},{5,4},{6,7},{7,6},{8,9},{9,8},{10,11... | collective-permute-start | bytes 3538952 | tf_op jit(solution)/shard_map/ppermute | solution.py:922
  110.1 4.9 %copy-start.24 = (bf16[4,192,256]{2,1,0:T(8,128)(2,1)S(1)}, bf16[4,192,256]{2,1,0:T(8,128)(2,1)}, u32[]{:S(2)}) copy-start(bf16[4,192,256]{2,1,0:T(8,128)(2,1)} %get-tuple-element.232) | copy-start | bytes 1179652
  110.1 34.9 %all-to-all-start.2 = ((bf16[4,144,1024]{2,1,0:T(8,128)(2,1)}), bf16[4,144,1024]{2,1,0:T(8,128)(2,1)S(1)}, u32[]{:S(2)}, u32[]{:S(2)}) async-start(bf16[4,144,1024]{2,1,0:T(8,128)(2,1)} %join_dx.1), calls=%async_computation.2 | async-start | bytes 2359296 | tf_op jit(solution)/shard_map/all_to_all | solution.py:926
  115.0 2.2 copy-start.11
  115.0 3.1 %copy-start.12 = (bf16[49,64,128]{2,1,0:T(8,128)(2,1)S(1)}, bf16[49,64,128]{2,1,0:T(8,128)(2,1)}, u32[]{:S(2)}) copy-start(bf16[49,64,128]{2,1,0:T(8,128)(2,1)} %get-tuple-element.308.refs_4_) | copy-start | bytes 2408452
  116.5 21.1 %copy-start.1 = (bf16[4,4,192,256]{3,2,1,0:T(8,128)(2,1)}, bf16[4,4,192,256]{3,2,1,0:T(8,128)(2,1)S(1)}, u32[]{:S(2)}) copy-start(bf16[4,4,192,256]{3,2,1,0:T(8,128)(2,1)S(1)} %pad_maximum_fusion.xm) | copy-start | bytes 4718596
  116.5 28.5 %collective-permute-start.16 = (bf16[4,4,192,256]{3,2,1,0:T(8,128)(2,1)S(1)}, bf16[4,4,192,256]{3,2,1,0:T(8,128)(2,1)S(1)}, u32[]{:S(2)}, u32[]{:S(2)}) collective-permute-start(bf16[4,4,192,256]{3,2,1,0:T(8,128)(2,1)S(1)} %pad_maximum_fusion.xm), channel_id=1, source_target_pairs={{0,1},{1,0},{2,3},{3,2},{4,5},{5,4},{6,7},{7,6},{8,9},{9,8},{10,11... | collective-permute-start | bytes 4718600 | tf_op jit(solution)/shard_map/ppermute | solution.py:922
  116.6 11.8 %collective-permute-start.13 = (bf16[4,128,1408]{2,1,0:T(8,128)(2,1)S(1)}, bf16[4,128,1408]{2,1,0:T(8,128)(2,1)}, u32[]{:S(2)}, u32[]{:S(2)}) collective-permute-start(bf16[4,128,1408]{2,1,0:T(8,128)(2,1)S(1)} %copy-done.7), channel_id=1, source_target_pairs={{0,1},{1,0},{2,3},{3,2},{4,5},{5,4},{6,7},{7,6},{8,9},{9,8},{10,11... | collective-permute-start | bytes 4325384 | tf_op jit(solution)/shard_map/ppermute | solution.py:922
  117.1 6.8 %collective-permute-start.14 = (bf16[4,128,1024]{2,1,0:T(8,128)(2,1)}, bf16[4,128,1024]{2,1,0:T(8,128)(2,1)}, u32[]{:S(2)}, u32[]{:S(2)}) collective-permute-start(bf16[4,128,1024]{2,1,0:T(8,128)(2,1)} %get-tuple-element.226), channel_id=1, source_target_pairs={{0,1},{1,0},{2,3},{3,2},{4,5},{5,4},{6,7},{7,6},{8,9},{9,8},{10,11... | collective-permute-start | bytes 3145736 | tf_op jit(solution)/shard_map/ppermute | solution.py:922
  117.2 26.9 %collective-permute-start.11 = (bf16[49,64,128]{2,1,0:T(8,128)(2,1)S(1)}, bf16[49,64,128]{2,1,0:T(8,128)(2,1)S(1)}, u32[]{:S(2)}, u32[]{:S(2)}) collective-permute-start(bf16[49,64,128]{2,1,0:T(8,128)(2,1)S(1)} %copy-done.11), channel_id=1, source_target_pairs={{0,8},{8,0},{16,24},{24,16},{1,9},{9,1},{17,25},{25,17},{2,10},{10... | collective-permute-start | bytes 2408456 | tf_op jit(solution)/shard_map/ppermute | solution.py:932
  118.1 26.0 %collective-permute-start.12 = (bf16[49,64,128]{2,1,0:T(8,128)(2,1)S(1)}, bf16[49,64,128]{2,1,0:T(8,128)(2,1)}, u32[]{:S(2)}, u32[]{:S(2)}) collective-permute-start(bf16[49,64,128]{2,1,0:T(8,128)(2,1)S(1)} %copy-done.12), channel_id=1, source_target_pairs={{0,16},{8,24},{16,0},{24,8},{1,17},{9,25},{17,1},{25,9},{2,18},{10... | collective-permute-start | bytes 2408456 | tf_op jit(solution)/shard_map/ppermute | solution.py:932
  123.9 20.2 %collective-permute-start.15 = (bf16[4,128,256]{2,1,0:T(8,128)(2,1)}, bf16[4,128,256]{2,1,0:T(8,128)(2,1)}, u32[]{:S(2)}, u32[]{:S(2)}) collective-permute-start(bf16[4,128,256]{2,1,0:T(8,128)(2,1)} %get-tuple-element.231), channel_id=1, source_target_pairs={{0,24},{8,16},{16,8},{24,0},{1,25},{9,17},{17,9},{25,1},{2,26},{10... | collective-permute-start | bytes 786440 | tf_op jit(solution)/shard_map/ppermute | solution.py:932
  145.0 5.9 %copy-start.5 = (bf16[4,4,192,256]{3,2,1,0:T(8,128)(2,1)}, bf16[4,4,192,256]{3,2,1,0:T(8,128)(2,1)S(1)}, u32[]{:S(2)}) copy-start(bf16[4,4,192,256]{3,2,1,0:T(8,128)(2,1)S(1)} %collective-permute-done.16.xo) | copy-start | bytes 4718596
  145.0 20.5 %collective-permute-start.17 = (bf16[49,64,128]{2,1,0:T(8,128)(2,1)S(1)}, bf16[49,64,128]{2,1,0:T(8,128)(2,1)}, u32[]{:S(2)}, u32[]{:S(2)}) collective-permute-start(bf16[49,64,128]{2,1,0:T(8,128)(2,1)S(1)} %copy-done.11), channel_id=1, source_target_pairs={{0,16},{8,24},{16,0},{24,8},{1,17},{9,25},{17,1},{25,9},{2,18},{10... | collective-permute-start | bytes 2408456 | tf_op jit(solution)/shard_map/ppermute | solution.py:932
  145.7 19.9 %collective-permute-start.18 = (bf16[49,64,128]{2,1,0:T(8,128)(2,1)}, bf16[49,64,128]{2,1,0:T(8,128)(2,1)}, u32[]{:S(2)}, u32[]{:S(2)}) collective-permute-start(bf16[49,64,128]{2,1,0:T(8,128)(2,1)} %get-tuple-element.308.refs_4_), channel_id=1, source_target_pairs={{0,8},{8,0},{16,24},{24,16},{1,9},{9,1},{17,25},{25,17},{2,10},{10... | collective-permute-start | bytes 2408456 | tf_op jit(solution)/shard_map/ppermute | solution.py:932
  150.9 14.7 %all-to-all-start.3 = ((bf16[4,160,256]{2,1,0:T(8,128)(2,1)}), bf16[4,160,256]{2,1,0:T(8,128)(2,1)S(1)}, u32[]{:S(2)}, u32[]{:S(2)}) async-start(bf16[4,160,256]{2,1,0:T(8,128)(2,1)} %get-tuple-element.249), calls=%async_computation.3 | async-start | bytes 655360 | tf_op jit(solution)/shard_map/all_to_all | solution.py:926
  165.5 4.8 %copy-start.28 = (bf16[4,128,256]{2,1,0:T(8,128)(2,1)S(1)}, bf16[4,128,256]{2,1,0:T(8,128)(2,1)}, u32[]{:S(2)}) copy-start(bf16[4,128,256]{2,1,0:T(8,128)(2,1)} %get-tuple-element.265) | copy-start | bytes 786436
  165.6 4.8 %copy-start.30 = (bf16[4,128,256]{2,1,0:T(8,128)(2,1)S(1)}, bf16[4,128,256]{2,1,0:T(8,128)(2,1)}, u32[]{:S(2)}) copy-start(bf16[4,128,256]{2,1,0:T(8,128)(2,1)} %copy-done.29) | copy-start | bytes 786436
  166.3 42.4 %all-to-all-start.4 = ((bf16[4,128,1664]{2,1,0:T(8,128)(2,1)}), bf16[4,128,1664]{2,1,0:T(8,128)(2,1)S(1)}, u32[]{:S(2)}, u32[]{:S(2)}) async-start(bf16[4,128,1664]{2,1,0:T(8,128)(2,1)} %get-tuple-element.252.late), calls=%async_computation.4 | async-start | bytes 3407872 | tf_op jit(solution)/shard_map/all_to_all | solution.py:926
  171.6 10.0 %copy-start.3 = (bf16[4,4,128,256]{3,2,1,0:T(8,128)(2,1)}, bf16[4,4,128,256]{3,2,1,0:T(8,128)(2,1)S(1)}, u32[]{:S(2)}) copy-start(bf16[4,4,128,256]{3,2,1,0:T(8,128)(2,1)S(1)} %pad_maximum_fusion.2.cm) | copy-start | bytes 3145732
  171.6 23.2 %collective-permute-start.23 = (bf16[4,4,128,256]{3,2,1,0:T(8,128)(2,1)S(1)}, bf16[4,4,128,256]{3,2,1,0:T(8,128)(2,1)S(1)}, u32[]{:S(2)}, u32[]{:S(2)}) collective-permute-start(bf16[4,4,128,256]{3,2,1,0:T(8,128)(2,1)S(1)} %pad_maximum_fusion.2.cm), channel_id=1, source_target_pairs={{0,1},{1,0},{2,3},{3,2},{4,5},{5,4},{6,7},{7,6},{8,9},{9,8},{10,11... | collective-permute-start | bytes 3145736 | tf_op jit(solution)/shard_map/ppermute | solution.py:922
  171.7 21.3 %collective-permute-start.24 = (bf16[49,64,128]{2,1,0:T(8,128)(2,1)S(1)}, bf16[49,64,128]{2,1,0:T(8,128)(2,1)S(1)}, u32[]{:S(2)}, u32[]{:S(2)}) collective-permute-start(bf16[49,64,128]{2,1,0:T(8,128)(2,1)S(1)} %copy-done.14), channel_id=1, source_target_pairs={{0,16},{8,24},{16,0},{24,8},{1,17},{9,25},{17,1},{25,9},{2,18},{10... | collective-permute-start | bytes 2408456 | tf_op jit(solution)/shard_map/ppermute | solution.py:932
  173.2 21.6 %collective-permute-start.25 = (bf16[49,64,128]{2,1,0:T(8,128)(2,1)}, bf16[49,64,128]{2,1,0:T(8,128)(2,1)S(1)}, u32[]{:S(2)}, u32[]{:S(2)}) collective-permute-start(bf16[49,64,128]{2,1,0:T(8,128)(2,1)} %collective-permute-done.12.refs_6_), channel_id=1, source_target_pairs={{0,8},{8,0},{16,24},{24,16},{1,9},{9,1},{17,25},{25,17},{2,10},{10... | collective-permute-start | bytes 2408456 | tf_op jit(solution)/shard_map/ppermute | solution.py:932
  174.1 7.5 %copy-start.21 = (bf16[4,160,256]{2,1,0:T(8,128)(2,1)S(1)}, bf16[4,160,256]{2,1,0:T(8,128)(2,1)}, u32[]{:S(2)}) copy-start(bf16[4,160,256]{2,1,0:T(8,128)(2,1)} %copy-done.20) | copy-start | bytes 983044
  181.6 1.7 collective-permute-start.19
  191.3 15.5 %collective-permute-start.20 = (bf16[32,3200]{1,0:T(8,128)(2,1)}, bf16[32,3200]{1,0:T(8,128)(2,1)S(1)}, u32[]{:S(2)}, u32[]{:S(2)}) collective-permute-start(bf16[32,3200]{1,0:T(8,128)(2,1)} %get-tuple-element.260), channel_id=1, source_target_pairs={{0,8},{8,0},{16,24},{24,16},{1,9},{9,1},{17,25},{25,17},{2,10},{10... | collective-permute-start | bytes 614408 | tf_op jit(solution)/shard_map/ppermute | solution.py:932
  192.4 14.4 %collective-permute-start.21 = (bf16[32,3200]{1,0:T(8,128)(2,1)}, bf16[32,3200]{1,0:T(8,128)(2,1)S(1)}, u32[]{:S(2)}, u32[]{:S(2)}) collective-permute-start(bf16[32,3200]{1,0:T(8,128)(2,1)} %get-tuple-element.261), channel_id=1, source_target_pairs={{0,16},{8,24},{16,0},{24,8},{1,17},{9,25},{17,1},{25,9},{2,18},{10... | collective-permute-start | bytes 614408 | tf_op jit(solution)/shard_map/ppermute | solution.py:932
  193.0 13.9 %collective-permute-start.22 = (bf16[32,3200]{1,0:T(8,128)(2,1)}, bf16[32,3200]{1,0:T(8,128)(2,1)S(1)}, u32[]{:S(2)}, u32[]{:S(2)}) collective-permute-start(bf16[32,3200]{1,0:T(8,128)(2,1)} %get-tuple-element.262), channel_id=1, source_target_pairs={{0,24},{8,16},{16,8},{24,0},{1,25},{9,17},{17,9},{25,1},{2,26},{10... | collective-permute-start | bytes 614408 | tf_op jit(solution)/shard_map/ppermute | solution.py:932
  194.8 13.8 %copy-start.42 = (bf16[128,1024]{1,0:T(8,128)(2,1)S(1)}, bf16[128,1024]{1,0:T(8,128)(2,1)}, u32[]{:S(2)}) copy-start(bf16[128,1024]{1,0:T(8,128)(2,1)} %get-tuple-element.285) | copy-start | bytes 786436
  194.8 14.3 %copy-start.41 = (bf16[128,1024]{1,0:T(8,128)(2,1)S(1)}, bf16[128,1024]{1,0:T(8,128)(2,1)}, u32[]{:S(2)}) copy-start(bf16[128,1024]{1,0:T(8,128)(2,1)} %get-tuple-element.286) | copy-start | bytes 786436
  194.8 16.6 %copy-start.40 = (bf16[128,1024]{1,0:T(8,128)(2,1)S(1)}, bf16[128,1024]{1,0:T(8,128)(2,1)}, u32[]{:S(2)}) copy-start(bf16[128,1024]{1,0:T(8,128)(2,1)} %get-tuple-element.287) | copy-start | bytes 786436
  206.8 28.9 %copy-start.34 = (bf16[32,3200]{1,0:T(8,128)(2,1)}, bf16[32,3200]{1,0:T(8,128)(2,1)S(1)}, u32[]{:S(2)}) copy-start(bf16[32,3200]{1,0:T(8,128)(2,1)S(1)} %collective-permute-done.20.refs_1_) | copy-start | bytes 614404
  206.8 28.9 %copy-start.35 = (bf16[32,3200]{1,0:T(8,128)(2,1)}, bf16[32,3200]{1,0:T(8,128)(2,1)S(1)}, u32[]{:S(2)}) copy-start(bf16[32,3200]{1,0:T(8,128)(2,1)S(1)} %collective-permute-done.21.refs_2_) | copy-start | bytes 614404
  206.9 28.9 %copy-start.36 = (bf16[32,3200]{1,0:T(8,128)(2,1)}, bf16[32,3200]{1,0:T(8,128)(2,1)S(1)}, u32[]{:S(2)}) copy-start(bf16[32,3200]{1,0:T(8,128)(2,1)S(1)} %collective-permute-done.22.refs_3_) | copy-start | bytes 614404
  208.6 4.5 %copy-start.4 = (bf16[4,128,1664]{2,1,0:T(8,128)(2,1)}, bf16[4,128,1664]{2,1,0:T(8,128)(2,1)S(1)}, u32[]{:S(2)}) copy-start(bf16[4,128,1664]{2,1,0:T(8,128)(2,1)S(1)} %all-to-all-done.4.l0) | copy-start | bytes 5111812
  208.6 4.5 %collective-permute-start.29 = (bf16[4,128,1664]{2,1,0:T(8,128)(2,1)S(1)}, bf16[4,128,1664]{2,1,0:T(8,128)(2,1)S(1)}, u32[]{:S(2)}, u32[]{:S(2)}) collective-permute-start(bf16[4,128,1664]{2,1,0:T(8,128)(2,1)S(1)} %all-to-all-done.4.l0), channel_id=1, source_target_pairs={{0,1},{1,0},{2,3},{3,2},{4,5},{5,4},{6,7},{7,6},{8,9},{9,8},{10,11... | collective-permute-start | bytes 5111816 | tf_op jit(solution)/shard_map/ppermute | solution.py:922
  208.7 17.2 %collective-permute-start.26 = (bf16[128,1024]{1,0:T(8,128)(2,1)S(1)}, bf16[128,1024]{1,0:T(8,128)(2,1)S(1)}, u32[]{:S(2)}, u32[]{:S(2)}) collective-permute-start(bf16[128,1024]{1,0:T(8,128)(2,1)S(1)} %copy-done.42), channel_id=1, source_target_pairs={{0,2},{1,3},{2,0},{3,1},{4,6},{5,7},{6,4},{7,5},{8,10},{9,11},{10,... | collective-permute-start | bytes 786440 | tf_op jit(solution)/shard_map/ppermute | solution.py:936
  209.1 28.8 %collective-permute-start.27 = (bf16[128,1024]{1,0:T(8,128)(2,1)S(1)}, bf16[128,1024]{1,0:T(8,128)(2,1)S(1)}, u32[]{:S(2)}, u32[]{:S(2)}) collective-permute-start(bf16[128,1024]{1,0:T(8,128)(2,1)S(1)} %copy-done.41), channel_id=1, source_target_pairs={{0,4},{1,5},{2,6},{3,7},{4,0},{5,1},{6,2},{7,3},{8,12},{9,13},{10,... | collective-permute-start | bytes 786440 | tf_op jit(solution)/shard_map/ppermute | solution.py:936
  211.4 26.5 %collective-permute-start.28 = (bf16[128,1024]{1,0:T(8,128)(2,1)S(1)}, bf16[128,1024]{1,0:T(8,128)(2,1)S(1)}, u32[]{:S(2)}, u32[]{:S(2)}) collective-permute-start(bf16[128,1024]{1,0:T(8,128)(2,1)S(1)} %copy-done.40), channel_id=1, source_target_pairs={{0,6},{1,7},{2,4},{3,5},{4,2},{5,3},{6,0},{7,1},{8,14},{9,15},{10,... | collective-permute-start | bytes 786440 | tf_op jit(solution)/shard_map/ppermute | solution.py:936
  223.4 14.6 %collective-permute-start.30 = (bf16[32,3712]{1,0:T(8,128)(2,1)}, bf16[32,3712]{1,0:T(8,128)(2,1)S(1)}, u32[]{:S(2)}, u32[]{:S(2)}) collective-permute-start(bf16[32,3712]{1,0:T(8,128)(2,1)} %get-tuple-element.293), channel_id=1, source_target_pairs={{0,8},{8,0},{16,24},{24,16},{1,9},{9,1},{17,25},{25,17},{2,10},{10... | collective-permute-start | bytes 712712 | tf_op jit(solution)/shard_map/ppermute | solution.py:932
  224.3 13.7 %collective-permute-start.31 = (bf16[32,3712]{1,0:T(8,128)(2,1)}, bf16[32,3712]{1,0:T(8,128)(2,1)S(1)}, u32[]{:S(2)}, u32[]{:S(2)}) collective-permute-start(bf16[32,3712]{1,0:T(8,128)(2,1)} %get-tuple-element.294), channel_id=1, source_target_pairs={{0,16},{8,24},{16,0},{24,8},{1,17},{9,25},{17,1},{25,9},{2,18},{10... | collective-permute-start | bytes 712712 | tf_op jit(solution)/shard_map/ppermute | solution.py:932
  225.8 12.2 %collective-permute-start.32 = (bf16[32,3712]{1,0:T(8,128)(2,1)}, bf16[32,3712]{1,0:T(8,128)(2,1)S(1)}, u32[]{:S(2)}, u32[]{:S(2)}) collective-permute-start(bf16[32,3712]{1,0:T(8,128)(2,1)} %get-tuple-element.295), channel_id=1, source_target_pairs={{0,24},{8,16},{16,8},{24,0},{1,25},{9,17},{17,9},{25,1},{2,26},{10... | collective-permute-start | bytes 712712 | tf_op jit(solution)/shard_map/ppermute | solution.py:932
  226.9 11.1 %copy-start.18 = (f32[128,1024]{1,0:T(8,128)S(1)}, f32[128,1024]{1,0:T(8,128)}, u32[]{:S(2)}) copy-start(f32[128,1024]{1,0:T(8,128)} %get-tuple-element.180.h1) | copy-start | bytes 1572868
  226.9 11.1 %copy-start.27 = (bf16[128,1024]{1,0:T(8,128)(2,1)S(1)}, bf16[128,1024]{1,0:T(8,128)(2,1)}, u32[]{:S(2)}) copy-start(bf16[128,1024]{1,0:T(8,128)(2,1)} %get-tuple-element.320) | copy-start | bytes 786436
  (17 other events, 18.1 us)
where the time goes:
time: 242 us; the launch traced here: 241 us
  Pallas kernels  127 us (52%)
  starting transfers between devices  55.8 us (23%)
  waiting for transfers between devices  38.5 us (16%)
  local copies, waits for them, and re-layouts  11.2 us (5%)
  other arithmetic  7.12 us (3%)
    pallas_call x13, Pallas kernels, call(): pl.pallas_call(body, out_shape=[jax.ShapeDtypeStruct(s, d) for s, d in ou...  64.9 us
    pallas_call x1, Pallas kernels, fast_path(): pl.pallas_call(partial(experts_body, S, eb), grid=(n_eb,), out_shape=[jax...  31.7 us
    all_to_all x5, starting transfers between devices, chips(): lax.all_to_all(v, 'expert', 0, 0, axis_index_groups=groups, tiled=True)  22.8 us
    ppermute x18, starting transfers between devices, plane(): return lax.ppermute(v, 'dp', [(p, p ^ s) for p in range(self.n_p)])  21.8 us
    pallas_call x2, Pallas kernels, expert_grads(): pl.pallas_call(partial(expert_grads_body, n_p, eb, first), grid=(last - f...  19 us
    ppermute x6, waiting for transfers between devices, near(): lax.ppermute(msgs[s], 'expert', pairs[s])  12.2 us
    ppermute x9, waiting for transfers between devices, core(): return lax.ppermute(v, 'expert', [(e, e ^ 1) for e in range(self.n_e)])  11.8 us
    ppermute x18, waiting for transfers between devices, plane(): return lax.ppermute(v, 'dp', [(p, p ^ s) for p in range(self.n_p)])  10.7 us
  transfers between devices with their start and end apart: 38, of which 10 were waited for; matrix products, arithmetic and copies ran while one was open for 3% of the time, Pallas kernels for 50%

commit v1 on v0

--- a/solution.py
+++ b/solution.py
@@ -546,39 +546,46 @@
             got = mm(block, both, 1, 0).astype(bf16)
             for j in range(eb):
                 dst[j * rows + pr * R : j * rows + (pr + 1) * R, :] = got[j * R : (j + 1) * R]
-    for first in range(0, eb, 2):
-        js = list(range(first, min(first + 2, eb)))
-        n = len(js)
-        span = slice(first * rows, (first + n) * rows)
-        g = jnp.concatenate([p for j in js for p in g_slot[j]], axis=0)
-        cj = cs[span, :].astype(f32)
-        ups = jnp.concatenate([up[j] for j in js], axis=1)
-        downs = jnp.concatenate([down[j] for j in js], axis=0)
-
-        def own(v):
-            return jnp.concatenate([v[i * rows : (i + 1) * rows, i * H : (i + 1) * H] for i in range(n)], axis=0)
-
-        def spread_out(v):
-            if n == 1:
-                return v
-            zero = jnp.zeros((rows, H), v.dtype)
-            return jnp.concatenate(
-                [
-                    jnp.concatenate([v[i * rows : (i + 1) * rows] if i == b else zero for b in range(n)], axis=1)
-                    for i in range(n)
-                ],
-                axis=0,
-            )
-
-        u = own(mm(xs[span, :], ups, 1, 0))
-        value, slope = gelu_both(u)
-        r = value.astype(bf16)
-        y = mm(spread_out(r), downs, 1, 0).astype(bf16).astype(f32)
-        dgate = jnp.sum(cj * y, axis=-1, keepdims=True)
+    units = [list(range(first, min(first + 2, eb))) for first in range(0, eb, 2)]
+    every = range(len(units))
+    spans = [slice(js[0] * rows, (js[-1] + 1) * rows) for js in units]
+
+    def own(v, n):
+        return jnp.concatenate([v[i * rows : (i + 1) * rows, i * H : (i + 1) * H] for i in range(n)], axis=0)
+
+    def spread_out(v, n):
+        if n == 1:
+            return v
+        zero = jnp.zeros((rows, H), v.dtype)
+        return jnp.concatenate(
+            [
+                jnp.concatenate([v[i * rows : (i + 1) * rows] if i == b else zero for b in range(n)], axis=1)
+                for i in range(n)
+            ],
+            axis=0,
+        )
+
+    gs = [jnp.concatenate([p for j in js for p in g_slot[j]], axis=0) for js in units]
+    ups = [jnp.concatenate([up[j] for j in js], axis=1) for js in units]
+    downs = [jnp.concatenate([down[j] for j in js], axis=0) for js in units]
+    us = [own(mm(xs[spans[m], :], ups[m], 1, 0), len(units[m])) for m in every]
+    drs = [
+        own(mm((gs[m] * cs[spans[m], :].astype(f32)).astype(bf16), downs[m], 1, 1), len(units[m])) for m in every
+    ]
+    dus, rs = [], []
+    for m in every:
+        value, slope = gelu_both(us[m])
+        rs.append(value.astype(bf16))
+        dus.append((drs[m] * slope).astype(bf16))
+    ys = [mm(spread_out(rs[m], len(units[m])), downs[m], 1, 0).astype(bf16) for m in every]
+    dxu = [mm(spread_out(dus[m], len(units[m])), ups[m], 1, 1).astype(bf16) for m in every]
+    for m in every:
+        js = units[m]
+        g = gs[m]
+        r, du = rs[m], dus[m]
+        y, dx = ys[m].astype(f32), dxu[m]
+        dgate = jnp.sum(cs[spans[m], :].astype(f32) * y, axis=-1, keepdims=True)
         gy = (g * y).astype(bf16)
-        dr = own(mm((g * cj).astype(bf16), downs, 1, 1))
-        du = (dr * slope).astype(bf16)
-        dx = mm(spread_out(du), ups, 1, 1).astype(bf16)
         gr = (g * r.astype(f32)).astype(bf16)
         dlog = dgate * g * (1.0 - g)
         for i, j in enumerate(js):

time: 242 us -> 238 us (0.983)
  Pallas kernels: 127 us -> 123 us
    pallas_call x1, Pallas kernels: 31.7 us -> 27.9 us  [fast_path(): pl.pallas_call(partial(experts_body, S, eb), grid=(n_eb,), out_shape=[jax...]
where the time goes in v1:
time: 238 us; the launch traced here: 237 us
  Pallas kernels  123 us (52%)
  starting transfers between devices  55.8 us (23%)
  waiting for transfers between devices  38.6 us (16%)
  local copies, waits for them, and re-layouts  11.2 us (5%)
  other arithmetic  7.12 us (3%)
    pallas_call x13, Pallas kernels, call(): pl.pallas_call(body, out_shape=[jax.ShapeDtypeStruct(s, d) for s, d in ou...  64.9 us
    pallas_call x1, Pallas kernels, fast_path(): pl.pallas_call(partial(experts_body, S, eb), grid=(n_eb,), out_shape=[jax...  27.9 us
    all_to_all x5, starting transfers between devices, chips(): lax.all_to_all(v, 'expert', 0, 0, axis_index_groups=groups, tiled=True)  22.8 us
    ppermute x18, starting transfers between devices, plane(): return lax.ppermute(v, 'dp', [(p, p ^ s) for p in range(self.n_p)])  21.8 us
    pallas_call x2, Pallas kernels, expert_grads(): pl.pallas_call(partial(expert_grads_body, n_p, eb, first), grid=(last - f...  19 us
    ppermute x6, waiting for transfers between devices, near(): lax.ppermute(msgs[s], 'expert', pairs[s])  12.2 us
    ppermute x9, waiting for transfers between devices, core(): return lax.ppermute(v, 'expert', [(e, e ^ 1) for e in range(self.n_e)])  11.8 us
    ppermute x18, waiting for transfers between devices, plane(): return lax.ppermute(v, 'dp', [(p, p ^ s) for p in range(self.n_p)])  10.8 us
  transfers between devices with their start and end apart: 38, of which 10 were waited for; matrix products, arithmetic and copies ran while one was open for 3% of the time, Pallas kernels for 50%

profile of v1, /device:TPU:0, one launch (start us, length us, event | category | flops | bytes accessed | tf_op | source)
XLA Modules:
  0.0 237.2 jit_solution(5773743631251343331)
XLA Ops:
  2.6 1.0 pad_maximum_fusion.3
  3.6 5.1 %collective-permute-start.2 = (bf16[144,1024]{1,0:T(8,128)(2,1)S(1)}, bf16[144,1024]{1,0:T(8,128)(2,1)S(1)}, u32[]{:S(2)}, u32[]{:S(2)}) collective-permute-start(bf16[144,1024]{1,0:T(8,128)(2,1)S(1)} %pad_maximum_fusion.3), channel_id=1, source_target_pairs={{0,6},{1,7},{2,4},{3,5},{4,2},{5,3},{6,0},{7,1},{8,14},{9,15},{10,... | collective-permute-start | bytes 884744 | tf_op jit(solution)/shard_map/ppermute | solution.py:943
  9.4 10.7 %forward.1 = (f32[128,1024]{1,0:T(8,128)}, bf16[4,144,1024]{2,1,0:T(8,128)(2,1)}, bf16[128,512]{1,0:T(8,128)(2,1)}, bf16[128,512]{1,0:T(8,128)(2,1)}, bf16[128,5...) custom-call(s32[1]{0:T(128)} %copy.44.length, ...), custom_call_target="tpu_custom_call" | custom-call | flops 1 | bytes 1 | tf_op jit(solution)/shard_map/forward/pallas_call | solution.py:335
  20.0 5.0 %all-to-all-start = ((bf16[4,144,1024]{2,1,0:T(8,128)(2,1)}), bf16[4,144,1024]{2,1,0:T(8,128)(2,1)S(1)}, u32[]{:S(2)}, u32[]{:S(2)}) async-start(bf16[4,144,1024]{2,1,0:T(8,128)(2,1)} %get-tuple-element.181), calls=%async_computation | async-start | bytes 2359296 | tf_op jit(solution)/shard_map/all_to_all | solution.py:933
  25.7 3.2 %early_slices.1 = bf16[4,128,1408]{2,1,0:T(8,128)(2,1)} custom-call(s32[4]{0:T(128)} %pad_add_fusion.ids, bf16[128,1024]{1,0:T(8,128)(2,1)} %li.5, bf16[128,1024]{1,0:T(8,128)(2,1)} %get-tuple-element.182.a1, bf16[128,1024]{1,0:T(8,128)(2,1)} %get-tuple-element.183.a2, f32[128,512]{1,0:T(8,128)} %get-tuple-element.184.o, f32[128,128]{1,0:T(8,128)} %get-tuple-element.185.gt), custom_call_target="tpu_custom_call" | custom-call | flops 1 | bytes 1 | tf_op jit(solution)/shard_map/early_slices/pallas_call | solution.py:335
  29.0 0.8 pad.19.selw
  30.1 1.1 pad.18
  31.2 12.2 %collective-permute-done.1 = bf16[144,1024]{1,0:T(8,128)(2,1)} collective-permute-done((bf16[144,1024]{1,0:T(8,128)(2,1)S(1)}, bf16[144,1024]{1,0:T(8,128)(2,1)}, u32[]{:S(2)}, u32[]{:S(2)}) %collective-permute-start.1) | collective-permute-done | bytes 294944 | tf_op jit(solution)/shard_map/ppermute | solution.py:943
  43.4 1.2 pad_maximum_fusion.1.x.refs_0_.refs_2_
  44.7 2.8 %collective-permute-done.3.refs_1_.refs_3_ = bf16[4,144,1024]{2,1,0:T(8,128)(2,1)S(1)} collective-permute-done((bf16[4,144,1024]{2,1,0:T(8,128)(2,1)S(1)}, bf16[4,144,1024]{2,1,0:T(8,128)(2,1)S(1)}, u32[]{:S(2)}, u32[]{:S(2)}) %collective-permute-start.3) | collective-permute-done | bytes 1179680 | tf_op jit(solution)/shard_map/ppermute | solution.py:929
  47.5 2.8 %cotangent_columns.1 = (bf16[4,128,256]{2,1,0:T(8,128)(2,1)}, bf16[4,128,256]{2,1,0:T(8,128)(2,1)}, bf16[4,128,256]{2,1,0:T(8,128)(2,1)}, bf16[4,128,256]{2,1,0:T(8,128)(2,1)}) custom-call(s32[4]{0:T(128)} %pad_add_fusion.ids, bf16[4,144,1024]{2,1,0:T(8,128)(2,1)} %copy-done), custom_call_target="tpu_custom_call" | custom-call | flops 1 | bytes 1 | tf_op jit(solution)/shard_map/cotangent_columns/pallas_call | solution.py:335
  50.3 1.5 collective-permute-start.4
  51.8 1.5 collective-permute-start.5
  53.4 1.9 codes.1
  55.3 3.6 %collective-permute-done.4 = bf16[4,128,256]{2,1,0:T(8,128)(2,1)S(1)} collective-permute-done((bf16[4,128,256]{2,1,0:T(8,128)(2,1)}, bf16[4,128,256]{2,1,0:T(8,128)(2,1)S(1)}, u32[]{:S(2)}, u32[]{:S(2)}) %collective-permute-start.4) | collective-permute-done | bytes 262176 | tf_op jit(solution)/shard_map/ppermute | solution.py:939
  60.2 3.7 %all-to-all-start.1 = ((bf16[4,128,1408]{2,1,0:T(8,128)(2,1)}), bf16[4,128,1408]{2,1,0:T(8,128)(2,1)S(1)}, u32[]{:S(2)}, u32[]{:S(2)}) async-start(bf16[4,128,1408]{2,1,0:T(8,128)(2,1)} %early_slices.1), calls=%async_computation.1 | async-start | bytes 2883584 | tf_op jit(solution)/shard_map/all_to_all | solution.py:933
  64.0 2.6 %token_columns.1 = (bf16[4,192,256]{2,1,0:T(8,128)(2,1)}, bf16[4,192,256]{2,1,0:T(8,128)(2,1)}, bf16[4,192,256]{2,1,0:T(8,128)(2,1)}, bf16[4,192,256]{2,1,0:T(8,128)(2,1)}) custom-call(s32[4]{0:T(128)} %pad_add_fusion.ids, bf16[4,144,1024]{2,1,0:T(8,128)(2,1)} %copy-done.2, bf16[4,64,256]{2,1,0:T(8,128)(2,1)} %get-tuple-element.200.refs_0_.refs_4_), custom_call_target="tpu_custom_call" | custom-call | flops 1 | bytes 1 | tf_op jit(solution)/shard_map/token_columns/pallas_call | solution.py:335
  66.6 0.9 collective-permute-start.7
  67.5 1.5 collective-permute-start.8
  69.0 1.1 collective-permute-start.9
  70.1 1.1 copy-done.22
  71.2 27.9 %experts.1 = (bf16[4,144,1024]{2,1,0:T(8,128)(2,1)}, bf16[4,144,1024]{2,1,0:T(8,128)(2,1)}, bf16[4,128,1024]{2,1,0:T(8,128)(2,1)}, bf16[4,128,1024]{2,1,0:T(8,12...) custom-call(s32[4]{0:T(128)} %pad_add_fusion.ids, bf16[4,144,1024]{2,1,0:T(8,128)(2,1)} %copy-done.2, ...), custom_call_target="tpu_custom_call" | custom-call | flops 1 | bytes 1 | tf_op jit(solution)/shard_map/experts/pallas_call | solution.py:1043
  99.2 3.0 %collective-permute-done.10.recv = bf16[4,144,1024]{2,1,0:T(8,128)(2,1)S(1)} collective-permute-done((bf16[4,144,1024]{2,1,0:T(8,128)(2,1)}, bf16[4,144,1024]{2,1,0:T(8,128)(2,1)S(1)}, u32[]{:S(2)}, u32[]{:S(2)}) %collective-permute-start.10) | collective-permute-done | bytes 1179680 | tf_op jit(solution)/shard_map/ppermute | solution.py:929
  102.3 1.0 copy-done.23
  103.3 3.0 %join_dx.1 = bf16[4,144,1024]{2,1,0:T(8,128)(2,1)} custom-call(bf16[4,144,1024]{2,1,0:T(8,128)(2,1)} %get-tuple-element.210.mine, bf16[4,144,1024]{2,1,0:T(8,128)(2,1)} %copy-done.23), custom_call_target="tpu_custom_call" | custom-call | flops 1 | bytes 1 | tf_op jit(solution)/shard_map/join_dx/pallas_call | solution.py:335
  106.3 4.9 %all-to-all-start.2 = ((bf16[4,144,1024]{2,1,0:T(8,128)(2,1)}), bf16[4,144,1024]{2,1,0:T(8,128)(2,1)S(1)}, u32[]{:S(2)}, u32[]{:S(2)}) async-start(bf16[4,144,1024]{2,1,0:T(8,128)(2,1)} %join_dx.1), calls=%async_computation.2 | async-start | bytes 2359296 | tf_op jit(solution)/shard_map/all_to_all | solution.py:933
  111.2 1.5 pad_maximum_fusion.xm
  113.3 0.9 collective-permute-start.11
  114.2 1.5 collective-permute-start.12
  115.8 4.3 %collective-permute-done.14.recv = bf16[4,128,1024]{2,1,0:T(8,128)(2,1)} collective-permute-done((bf16[4,128,1024]{2,1,0:T(8,128)(2,1)}, bf16[4,128,1024]{2,1,0:T(8,128)(2,1)}, u32[]{:S(2)}, u32[]{:S(2)}) %collective-permute-start.14) | collective-permute-done | bytes 1048608 | tf_op jit(solution)/shard_map/ppermute | solution.py:929
  120.0 1.9 collective-permute-start.15
  121.9 2.7 %join_out.1 = (bf16[128,1024]{1,0:T(8,128)(2,1)}, bf16[128,1024]{1,0:T(8,128)(2,1)}, bf16[128,1024]{1,0:T(8,128)(2,1)}, bf16[128,1024]{1,0:T(8,128)(2,1)}) custom-call(s32[4]{0:T(128)} %pad_add_fusion.ids, bf16[4,128,1024]{2,1,0:T(8,128)(2,1)} %get-tuple-element.225.mine, bf16[4,128,1024]{2,1,0:T(8,128)(2,1)} %collective-permute-done.14.recv), custom_call_target="tpu_custom_call" | custom-call | flops 1 | bytes 1 | tf_op jit(solution)/shard_map/join_out/pallas_call | solution.py:335
  124.6 9.2 %spread_tokens.1 = (bf16[1024,2560]{1,0:T(8,128)(2,1)}, bf16[1024,128]{1,0:T(8,128)(2,1)}, bf16[256,1024]{1,0:T(8,128)(2,1)}, f32[128,1024]{1,0:T(8,128)}, f32[1...) custom-call(s32[4]{0:T(128)} %pad_add_fusion.ids, bf16[4,128,1408]{2,1,0:T(8,128)(2,1)} %copy-done.6, ...), custom_call_target="tpu_custom_call" | custom-call | flops 1 | bytes 268435456 | tf_op jit(solution)/shard_map/spread_tokens/pallas_call | solution.py:335
  133.8 6.5 %collective-permute-done.15 = bf16[4,128,256]{2,1,0:T(8,128)(2,1)} collective-permute-done((bf16[4,128,256]{2,1,0:T(8,128)(2,1)}, bf16[4,128,256]{2,1,0:T(8,128)(2,1)}, u32[]{:S(2)}, u32[]{:S(2)}) %collective-permute-start.15) | collective-permute-done | bytes 262176 | tf_op jit(solution)/shard_map/ppermute | solution.py:939
  140.3 0.9 copy-done.13
  141.8 0.9 collective-permute-start.18
  142.8 4.3 %ffn_back.1 = (f32[128,1024]{1,0:T(8,128)}, bf16[128,1024]{1,0:T(8,128)(2,1)}, bf16[4,160,256]{2,1,0:T(8,128)(2,1)}) custom-call(s32[4]{0:T(128)} %pad_add_fusion.ids, bf16[4,144,1024]{2,1,0:T(8,128)(2,1)} %copy-done.9, f32[128,1024]{1,0:T(8,128)} %get-tuple-element.180.h1, bf16[128,1024]{1,0:T(8,128)(2,1)} %c.1, bf16[512,1024]{1,0:T(8,128)(2,1)} %bitcast.40, ...), custom_call_target="tpu_custom_call" | custom-call | flops 1 | bytes 1 | tf_op jit(solution)/shard_map/ffn_back/pallas_call | solution.py:335
  147.1 5.1 %all-to-all-start.3 = ((bf16[4,160,256]{2,1,0:T(8,128)(2,1)}), bf16[4,160,256]{2,1,0:T(8,128)(2,1)S(1)}, u32[]{:S(2)}, u32[]{:S(2)}) async-start(bf16[4,160,256]{2,1,0:T(8,128)(2,1)} %get-tuple-element.249), calls=%async_computation.3 | async-start | bytes 655360 | tf_op jit(solution)/shard_map/all_to_all | solution.py:933
  152.2 7.6 %attention_back.1 = (bf16[4,128,1664]{2,1,0:T(8,128)(2,1)}, bf16[128,2560]{1,0:T(8,128)(2,1)}) custom-call(bf16[128,1024]{1,0:T(8,128)(2,1)} %get-tuple-element.242.db, bf16[2560,1024]{1,0:T(8,128)(2,1)} %wo.3, f32[128,128]{1,0:T(8,128)} %get-tuple-element.185.gt, f32[128,512]{1,0:T(8,128)} %get-tuple-element.184.o, bf16[128,512]{1,0:T(8,128)(2,1)} %get-tuple-element.243.q, ...), custom_call_target="tpu_custom_call" | custom-call | flops 1 | bytes 268435456 | tf_op jit(solution)/shard_map/attention_back/pallas_call | solution.py:335
  159.7 2.0 all-to-all-done.3.m0
  162.5 4.0 %all-to-all-start.4 = ((bf16[4,128,1664]{2,1,0:T(8,128)(2,1)}), bf16[4,128,1664]{2,1,0:T(8,128)(2,1)S(1)}, u32[]{:S(2)}, u32[]{:S(2)}) async-start(bf16[4,128,1664]{2,1,0:T(8,128)(2,1)} %get-tuple-element.252.late), calls=%async_computation.4 | async-start | bytes 3407872 | tf_op jit(solution)/shard_map/all_to_all | solution.py:933
  166.5 1.2 pad_maximum_fusion.2.cm
  167.8 1.6 collective-permute-start.24
  169.4 0.9 collective-permute-start.25
  170.3 7.5 %input_back.1 = f32[128,1024]{1,0:T(8,128)} custom-call(bf16[4,128,1664]{2,1,0:T(8,128)(2,1)} %get-tuple-element.252.late, bf16[128,2560]{1,0:T(8,128)(2,1)} %get-tuple-element.253.dp, bf16[1024,512]{1,0:T(8,128)(2,1)} %wq.5, bf16[1024,512]{1,0:T(8,128)(2,1)} %wk.5, bf16[1024,2560]{1,0:T(8,128)(2,1)} %wv.3, bf16[1024,128]{1,0:T(8,128)(2,1)} %pad.19.selw, ...), custom_call_target="tpu_custom_call" | custom-call | flops 1 | bytes 1 | tf_op jit(solution)/shard_map/input_back/pallas_call | solution.py:335
  177.9 1.6 collective-permute-done.19.m1
  180.2 7.3 %out_grads.1 = (f32[32,3200]{1,0:T(8,128)}, bf16[32,3200]{1,0:T(8,128)(2,1)}, bf16[32,3200]{1,0:T(8,128)(2,1)}, bf16[32,3200]{1,0:T(8,128)(2,1)}) custom-call(s32[4]{0:T(128)} %pad_add_fusion.ids, bf16[4,160,256]{2,1,0:T(8,128)(2,1)} %copy-done.20, bf16[4,160,256]{2,1,0:T(8,128)(2,1)} %copy-done.26, bf16[1024,2560]{1,0:T(8,128)(2,1)} %get-tuple-element.256.z, ...), custom_call_target="tpu_custom_call" | custom-call | flops 1 | bytes 1 | tf_op jit(solution)/shard_map/out_grads/pallas_call | solution.py:335
  187.5 1.2 collective-permute-start.20
  189.2 1.8 collective-permute-start.22
  191.0 0.9 copy-done.16
  191.9 1.0 copy-done.10
  192.8 10.1 %expert_grads.2 = (f32[49,256,128]{2,1,0:T(8,128)}, f32[49,128,256]{2,1,0:T(8,128)}) custom-call(bf16[4,4,192,256]{3,2,1,0:T(8,128)(2,1)} %copy-done.1, bf16[4,4,192,256]{3,2,1,0:T(8,128)(2,1)} %copy-done.5, bf16[4,4,128,256]{3,2,1,0:T(8,128)(2,1)} %copy-done.3, bf16[4,4,128,256]{3,2,1,0:T(8,128)(2,1)} %copy-done.10, ...), custom_call_target="tpu_custom_call" | custom-call | flops 1 | bytes 1 | tf_op jit(solution)/shard_map/expert_grads/pallas_call | solution.py:1147
  203.1 1.8 all-to-all-done.4.l0
  205.3 2.4 collective-permute-start.27
  207.6 1.7 collective-permute-start.28
  209.3 1.2 copy-done.19
  210.5 9.0 %in_grads.1 = (f32[32,3712]{1,0:T(8,128)}, bf16[32,3712]{1,0:T(8,128)(2,1)}, bf16[32,3712]{1,0:T(8,128)(2,1)}, bf16[32,3712]{1,0:T(8,128)(2,1)}) custom-call(s32[4]{0:T(128)} %pad_add_fusion.ids, bf16[4,128,1664]{2,1,0:T(8,128)(2,1)} %copy-done.4, bf16[4,128,1664]{2,1,0:T(8,128)(2,1)} %copy-done.19, bf16[256,1024]{1,0:T(8,128)(2,1)} %get-tuple-element.288.lia1, ...), custom_call_target="tpu_custom_call" | custom-call | flops 1 | bytes 268435456 | tf_op jit(solution)/shard_map/in_grads/pallas_call | solution.py:1174
  219.5 0.9 collective-permute-start.30
  220.5 1.5 collective-permute-start.31
  222.0 1.0 collective-permute-start.32
  223.0 8.9 %expert_grads.3 = (f32[49,256,128]{2,1,0:T(8,128)}, f32[49,128,256]{2,1,0:T(8,128)}) custom-call(bf16[4,4,192,256]{3,2,1,0:T(8,128)(2,1)} %copy-done.1, bf16[4,4,192,256]{3,2,1,0:T(8,128)(2,1)} %copy-done.5, bf16[4,4,128,256]{3,2,1,0:T(8,128)(2,1)} %copy-done.3, bf16[4,4,128,256]{3,2,1,0:T(8,128)(2,1)} %copy-done.10, ...), custom_call_target="tpu_custom_call", output_to_operand_aliasing={{0}: (12, {}), {1}: (13, {})} | custom-call | flops 1 | bytes 1 | tf_op jit(solution)/shard_map/expert_grads/pallas_call | solution.py:1147
  232.0 2.1 last_sum_a.1
  234.2 0.9 add_convert_fusion
  235.1 2.1 last_sum_b.1
  (132 shorter events, 8.6 us)
Async XLA Ops:
  3.6 27.6 %collective-permute-start.2 = (bf16[144,1024]{1,0:T(8,128)(2,1)S(1)}, bf16[144,1024]{1,0:T(8,128)(2,1)S(1)}, u32[]{:S(2)}, u32[]{:S(2)}) collective-permute-start(bf16[144,1024]{1,0:T(8,128)(2,1)S(1)} %pad_maximum_fusion.3), channel_id=1, source_target_pairs={{0,6},{1,7},{2,4},{3,5},{4,2},{5,3},{6,0},{7,1},{8,14},{9,15},{10,... | collective-permute-start | bytes 884744 | tf_op jit(solution)/shard_map/ppermute | solution.py:943
  8.7 34.7 %collective-permute-start.1 = (bf16[144,1024]{1,0:T(8,128)(2,1)S(1)}, bf16[144,1024]{1,0:T(8,128)(2,1)}, u32[]{:S(2)}, u32[]{:S(2)}) collective-permute-start(bf16[144,1024]{1,0:T(8,128)(2,1)S(1)} %pad_maximum_fusion.3), channel_id=1, source_target_pairs={{0,4},{1,5},{2,6},{3,7},{4,0},{5,1},{6,2},{7,3},{8,12},{9,13},{10,... | collective-permute-start | bytes 884744 | tf_op jit(solution)/shard_map/ppermute | solution.py:943
  8.7 34.7 %collective-permute-start = (bf16[144,1024]{1,0:T(8,128)(2,1)S(1)}, bf16[144,1024]{1,0:T(8,128)(2,1)}, u32[]{:S(2)}, u32[]{:S(2)}) collective-permute-start(bf16[144,1024]{1,0:T(8,128)(2,1)S(1)} %pad_maximum_fusion.3), channel_id=1, source_target_pairs={{0,2},{1,3},{2,0},{3,1},{4,6},{5,7},{6,4},{7,5},{8,10},{9,11},{10,... | collective-permute-start | bytes 884744 | tf_op jit(solution)/shard_map/ppermute | solution.py:943
  20.0 40.2 %all-to-all-start = ((bf16[4,144,1024]{2,1,0:T(8,128)(2,1)}), bf16[4,144,1024]{2,1,0:T(8,128)(2,1)S(1)}, u32[]{:S(2)}, u32[]{:S(2)}) async-start(bf16[4,144,1024]{2,1,0:T(8,128)(2,1)} %get-tuple-element.181), calls=%async_computation | async-start | bytes 2359296 | tf_op jit(solution)/shard_map/all_to_all | solution.py:933
  25.1 3.8 %copy-start.37 = (bf16[1024,20]{0,1:T(8,128)(2,1)S(1)}, bf16[1024,20]{0,1:T(8,128)(2,1)}, u32[]{:S(2)}) copy-start(bf16[1024,20]{0,1:T(8,128)(2,1)} %param.31) | copy-start | bytes 122884
  25.1 3.8 %copy-start.38 = (bf16[1024,20]{0,1:T(8,128)(2,1)S(1)}, bf16[1024,20]{0,1:T(8,128)(2,1)}, u32[]{:S(2)}) copy-start(bf16[1024,20]{0,1:T(8,128)(2,1)} %param.32) | copy-start | bytes 122884
  25.7 4.1 %copy-start.17 = (bf16[1024,387]{0,1:T(8,128)(2,1)S(1)}, bf16[1024,387]{0,1:T(8,128)(2,1)}, u32[]{:S(2)}) copy-start(bf16[1024,387]{0,1:T(8,128)(2,1)} %param.35) | copy-start | bytes 2377732
  44.6 2.9 %copy-start = (bf16[4,144,1024]{2,1,0:T(8,128)(2,1)}, bf16[4,144,1024]{2,1,0:T(8,128)(2,1)S(1)}, u32[]{:S(2)}) copy-start(bf16[4,144,1024]{2,1,0:T(8,128)(2,1)S(1)} %pad_maximum_fusion.1.x.refs_0_.refs_2_) | copy-start | bytes 3538948
  44.6 2.9 %collective-permute-start.3 = (bf16[4,144,1024]{2,1,0:T(8,128)(2,1)S(1)}, bf16[4,144,1024]{2,1,0:T(8,128)(2,1)S(1)}, u32[]{:S(2)}, u32[]{:S(2)}) collective-permute-start(bf16[4,144,1024]{2,1,0:T(8,128)(2,1)S(1)} %pad_maximum_fusion.1.x.refs_0_.refs_2_), channel_id=1, source_target_pairs={{0,1},{1,0},{2,3},{3,2},{4,5},{5,4},{6,7},{7,6},{8,9},{9,8},{10,11... | collective-permute-start | bytes 3538952 | tf_op jit(solution)/shard_map/ppermute | solution.py:929
  47.5 5.8 %copy-start.8 = (bf16[4,144,1024]{2,1,0:T(8,128)(2,1)}, bf16[4,144,1024]{2,1,0:T(8,128)(2,1)S(1)}, u32[]{:S(2)}) copy-start(bf16[4,144,1024]{2,1,0:T(8,128)(2,1)S(1)} %collective-permute-done.3.refs_1_.refs_3_) | copy-start | bytes 3538948
  50.3 8.6 %collective-permute-start.4 = (bf16[4,128,256]{2,1,0:T(8,128)(2,1)}, bf16[4,128,256]{2,1,0:T(8,128)(2,1)S(1)}, u32[]{:S(2)}, u32[]{:S(2)}) collective-permute-start(bf16[4,128,256]{2,1,0:T(8,128)(2,1)} %get-tuple-element.195), channel_id=1, source_target_pairs={{0,8},{8,0},{16,24},{24,16},{1,9},{9,1},{17,25},{25,17},{2,10},{10... | collective-permute-start | bytes 786440 | tf_op jit(solution)/shard_map/ppermute | solution.py:939
  51.8 8.4 %collective-permute-start.5 = (bf16[4,128,256]{2,1,0:T(8,128)(2,1)}, bf16[4,128,256]{2,1,0:T(8,128)(2,1)}, u32[]{:S(2)}, u32[]{:S(2)}) collective-permute-start(bf16[4,128,256]{2,1,0:T(8,128)(2,1)} %get-tuple-element.196), channel_id=1, source_target_pairs={{0,16},{8,24},{16,0},{24,8},{1,17},{9,25},{17,1},{25,9},{2,18},{10... | collective-permute-start | bytes 786440 | tf_op jit(solution)/shard_map/ppermute | solution.py:939
  60.2 3.8 %copy-start.2 = (bf16[4,144,1024]{2,1,0:T(8,128)(2,1)}, bf16[4,144,1024]{2,1,0:T(8,128)(2,1)S(1)}, u32[]{:S(2)}) copy-start(bf16[4,144,1024]{2,1,0:T(8,128)(2,1)S(1)} %all-to-all-done.x.refs_0_) | copy-start | bytes 3538948
  60.2 38.9 %all-to-all-start.1 = ((bf16[4,128,1408]{2,1,0:T(8,128)(2,1)}), bf16[4,128,1408]{2,1,0:T(8,128)(2,1)S(1)}, u32[]{:S(2)}, u32[]{:S(2)}) async-start(bf16[4,128,1408]{2,1,0:T(8,128)(2,1)} %early_slices.1), calls=%async_computation.1 | async-start | bytes 2883584 | tf_op jit(solution)/shard_map/all_to_all | solution.py:933
  63.9 6.1 %collective-permute-start.6 = (bf16[4,144,1024]{2,1,0:T(8,128)(2,1)S(1)}, bf16[4,144,1024]{2,1,0:T(8,128)(2,1)S(1)}, u32[]{:S(2)}, u32[]{:S(2)}) collective-permute-start(bf16[4,144,1024]{2,1,0:T(8,128)(2,1)S(1)} %all-to-all-done.x.refs_0_), channel_id=1, source_target_pairs={{0,1},{1,0},{2,3},{3,2},{4,5},{5,4},{6,7},{7,6},{8,9},{9,8},{10,11... | collective-permute-start | bytes 3538952 | tf_op jit(solution)/shard_map/ppermute | solution.py:929
  66.6 32.5 %collective-permute-start.7 = (bf16[4,192,256]{2,1,0:T(8,128)(2,1)}, bf16[4,192,256]{2,1,0:T(8,128)(2,1)S(1)}, u32[]{:S(2)}, u32[]{:S(2)}) collective-permute-start(bf16[4,192,256]{2,1,0:T(8,128)(2,1)} %get-tuple-element.203), channel_id=1, source_target_pairs={{0,8},{8,0},{16,24},{24,16},{1,9},{9,1},{17,25},{25,17},{2,10},{10... | collective-permute-start | bytes 1179656 | tf_op jit(solution)/shard_map/ppermute | solution.py:939
  67.5 31.6 %collective-permute-start.8 = (bf16[4,192,256]{2,1,0:T(8,128)(2,1)}, bf16[4,192,256]{2,1,0:T(8,128)(2,1)S(1)}, u32[]{:S(2)}, u32[]{:S(2)}) collective-permute-start(bf16[4,192,256]{2,1,0:T(8,128)(2,1)} %get-tuple-element.204), channel_id=1, source_target_pairs={{0,16},{8,24},{16,0},{24,8},{1,17},{9,25},{17,1},{25,9},{2,18},{10... | collective-permute-start | bytes 1179656 | tf_op jit(solution)/shard_map/ppermute | solution.py:939
  69.0 30.1 %collective-permute-start.9 = (bf16[4,192,256]{2,1,0:T(8,128)(2,1)}, bf16[4,192,256]{2,1,0:T(8,128)(2,1)}, u32[]{:S(2)}, u32[]{:S(2)}) collective-permute-start(bf16[4,192,256]{2,1,0:T(8,128)(2,1)} %get-tuple-element.205), channel_id=1, source_target_pairs={{0,24},{8,16},{16,8},{24,0},{1,25},{9,17},{17,9},{25,1},{2,26},{10... | collective-permute-start | bytes 1179656 | tf_op jit(solution)/shard_map/ppermute | solution.py:939
  99.1 3.2 %copy-start.25 = (bf16[4,192,256]{2,1,0:T(8,128)(2,1)}, bf16[4,192,256]{2,1,0:T(8,128)(2,1)S(1)}, u32[]{:S(2)}) copy-start(bf16[4,192,256]{2,1,0:T(8,128)(2,1)S(1)} %collective-permute-done.8) | copy-start | bytes 1179652
  99.1 7.1 %copy-start.6 = (bf16[4,128,1408]{2,1,0:T(8,128)(2,1)}, bf16[4,128,1408]{2,1,0:T(8,128)(2,1)S(1)}, u32[]{:S(2)}) copy-start(bf16[4,128,1408]{2,1,0:T(8,128)(2,1)S(1)} %all-to-all-done.1.e0) | copy-start | bytes 4325380
  99.1 3.1 %collective-permute-start.10 = (bf16[4,144,1024]{2,1,0:T(8,128)(2,1)}, bf16[4,144,1024]{2,1,0:T(8,128)(2,1)S(1)}, u32[]{:S(2)}, u32[]{:S(2)}) collective-permute-start(bf16[4,144,1024]{2,1,0:T(8,128)(2,1)} %get-tuple-element.211), channel_id=1, source_target_pairs={{0,1},{1,0},{2,3},{3,2},{4,5},{5,4},{6,7},{7,6},{8,9},{9,8},{10,11... | collective-permute-start | bytes 3538952 | tf_op jit(solution)/shard_map/ppermute | solution.py:929
  106.3 4.9 %copy-start.24 = (bf16[4,192,256]{2,1,0:T(8,128)(2,1)S(1)}, bf16[4,192,256]{2,1,0:T(8,128)(2,1)}, u32[]{:S(2)}) copy-start(bf16[4,192,256]{2,1,0:T(8,128)(2,1)} %get-tuple-element.232) | copy-start | bytes 1179652
  106.3 34.9 %all-to-all-start.2 = ((bf16[4,144,1024]{2,1,0:T(8,128)(2,1)}), bf16[4,144,1024]{2,1,0:T(8,128)(2,1)S(1)}, u32[]{:S(2)}, u32[]{:S(2)}) async-start(bf16[4,144,1024]{2,1,0:T(8,128)(2,1)} %join_dx.1), calls=%async_computation.2 | async-start | bytes 2359296 | tf_op jit(solution)/shard_map/all_to_all | solution.py:933
  111.2 2.2 copy-start.11
  111.2 3.1 %copy-start.12 = (bf16[49,64,128]{2,1,0:T(8,128)(2,1)S(1)}, bf16[49,64,128]{2,1,0:T(8,128)(2,1)}, u32[]{:S(2)}) copy-start(bf16[49,64,128]{2,1,0:T(8,128)(2,1)} %get-tuple-element.308.refs_4_) | copy-start | bytes 2408452
  112.7 21.2 %copy-start.1 = (bf16[4,4,192,256]{3,2,1,0:T(8,128)(2,1)}, bf16[4,4,192,256]{3,2,1,0:T(8,128)(2,1)S(1)}, u32[]{:S(2)}) copy-start(bf16[4,4,192,256]{3,2,1,0:T(8,128)(2,1)S(1)} %pad_maximum_fusion.xm) | copy-start | bytes 4718596
  112.7 28.5 %collective-permute-start.16 = (bf16[4,4,192,256]{3,2,1,0:T(8,128)(2,1)S(1)}, bf16[4,4,192,256]{3,2,1,0:T(8,128)(2,1)S(1)}, u32[]{:S(2)}, u32[]{:S(2)}) collective-permute-start(bf16[4,4,192,256]{3,2,1,0:T(8,128)(2,1)S(1)} %pad_maximum_fusion.xm), channel_id=1, source_target_pairs={{0,1},{1,0},{2,3},{3,2},{4,5},{5,4},{6,7},{7,6},{8,9},{9,8},{10,11... | collective-permute-start | bytes 4718600 | tf_op jit(solution)/shard_map/ppermute | solution.py:929
  112.8 11.9 %collective-permute-start.13 = (bf16[4,128,1408]{2,1,0:T(8,128)(2,1)S(1)}, bf16[4,128,1408]{2,1,0:T(8,128)(2,1)}, u32[]{:S(2)}, u32[]{:S(2)}) collective-permute-start(bf16[4,128,1408]{2,1,0:T(8,128)(2,1)S(1)} %copy-done.7), channel_id=1, source_target_pairs={{0,1},{1,0},{2,3},{3,2},{4,5},{5,4},{6,7},{7,6},{8,9},{9,8},{10,11... | collective-permute-start | bytes 4325384 | tf_op jit(solution)/shard_map/ppermute | solution.py:929
  113.2 6.8 %collective-permute-start.14 = (bf16[4,128,1024]{2,1,0:T(8,128)(2,1)}, bf16[4,128,1024]{2,1,0:T(8,128)(2,1)}, u32[]{:S(2)}, u32[]{:S(2)}) collective-permute-start(bf16[4,128,1024]{2,1,0:T(8,128)(2,1)} %get-tuple-element.226), channel_id=1, source_target_pairs={{0,1},{1,0},{2,3},{3,2},{4,5},{5,4},{6,7},{7,6},{8,9},{9,8},{10,11... | collective-permute-start | bytes 3145736 | tf_op jit(solution)/shard_map/ppermute | solution.py:929
  113.3 27.0 %collective-permute-start.11 = (bf16[49,64,128]{2,1,0:T(8,128)(2,1)S(1)}, bf16[49,64,128]{2,1,0:T(8,128)(2,1)S(1)}, u32[]{:S(2)}, u32[]{:S(2)}) collective-permute-start(bf16[49,64,128]{2,1,0:T(8,128)(2,1)S(1)} %copy-done.11), channel_id=1, source_target_pairs={{0,8},{8,0},{16,24},{24,16},{1,9},{9,1},{17,25},{25,17},{2,10},{10... | collective-permute-start | bytes 2408456 | tf_op jit(solution)/shard_map/ppermute | solution.py:939
  114.2 26.1 %collective-permute-start.12 = (bf16[49,64,128]{2,1,0:T(8,128)(2,1)S(1)}, bf16[49,64,128]{2,1,0:T(8,128)(2,1)}, u32[]{:S(2)}, u32[]{:S(2)}) collective-permute-start(bf16[49,64,128]{2,1,0:T(8,128)(2,1)S(1)} %copy-done.12), channel_id=1, source_target_pairs={{0,16},{8,24},{16,0},{24,8},{1,17},{9,25},{17,1},{25,9},{2,18},{10... | collective-permute-start | bytes 2408456 | tf_op jit(solution)/shard_map/ppermute | solution.py:939
  120.0 20.3 %collective-permute-start.15 = (bf16[4,128,256]{2,1,0:T(8,128)(2,1)}, bf16[4,128,256]{2,1,0:T(8,128)(2,1)}, u32[]{:S(2)}, u32[]{:S(2)}) collective-permute-start(bf16[4,128,256]{2,1,0:T(8,128)(2,1)} %get-tuple-element.231), channel_id=1, source_target_pairs={{0,24},{8,16},{16,8},{24,0},{1,25},{9,17},{17,9},{25,1},{2,26},{10... | collective-permute-start | bytes 786440 | tf_op jit(solution)/shard_map/ppermute | solution.py:939
  141.2 5.9 %copy-start.5 = (bf16[4,4,192,256]{3,2,1,0:T(8,128)(2,1)}, bf16[4,4,192,256]{3,2,1,0:T(8,128)(2,1)S(1)}, u32[]{:S(2)}) copy-start(bf16[4,4,192,256]{3,2,1,0:T(8,128)(2,1)S(1)} %collective-permute-done.16.xo) | copy-start | bytes 4718596
  141.2 20.5 %collective-permute-start.17 = (bf16[49,64,128]{2,1,0:T(8,128)(2,1)S(1)}, bf16[49,64,128]{2,1,0:T(8,128)(2,1)}, u32[]{:S(2)}, u32[]{:S(2)}) collective-permute-start(bf16[49,64,128]{2,1,0:T(8,128)(2,1)S(1)} %copy-done.11), channel_id=1, source_target_pairs={{0,16},{8,24},{16,0},{24,8},{1,17},{9,25},{17,1},{25,9},{2,18},{10... | collective-permute-start | bytes 2408456 | tf_op jit(solution)/shard_map/ppermute | solution.py:939
  141.8 19.9 %collective-permute-start.18 = (bf16[49,64,128]{2,1,0:T(8,128)(2,1)}, bf16[49,64,128]{2,1,0:T(8,128)(2,1)}, u32[]{:S(2)}, u32[]{:S(2)}) collective-permute-start(bf16[49,64,128]{2,1,0:T(8,128)(2,1)} %get-tuple-element.308.refs_4_), channel_id=1, source_target_pairs={{0,8},{8,0},{16,24},{24,16},{1,9},{9,1},{17,25},{25,17},{2,10},{10... | collective-permute-start | bytes 2408456 | tf_op jit(solution)/shard_map/ppermute | solution.py:939
  147.1 14.7 %all-to-all-start.3 = ((bf16[4,160,256]{2,1,0:T(8,128)(2,1)}), bf16[4,160,256]{2,1,0:T(8,128)(2,1)S(1)}, u32[]{:S(2)}, u32[]{:S(2)}) async-start(bf16[4,160,256]{2,1,0:T(8,128)(2,1)} %get-tuple-element.249), calls=%async_computation.3 | async-start | bytes 655360 | tf_op jit(solution)/shard_map/all_to_all | solution.py:933
  161.8 4.7 %copy-start.28 = (bf16[4,128,256]{2,1,0:T(8,128)(2,1)S(1)}, bf16[4,128,256]{2,1,0:T(8,128)(2,1)}, u32[]{:S(2)}) copy-start(bf16[4,128,256]{2,1,0:T(8,128)(2,1)} %get-tuple-element.265) | copy-start | bytes 786436
  161.8 4.7 %copy-start.30 = (bf16[4,128,256]{2,1,0:T(8,128)(2,1)S(1)}, bf16[4,128,256]{2,1,0:T(8,128)(2,1)}, u32[]{:S(2)}) copy-start(bf16[4,128,256]{2,1,0:T(8,128)(2,1)} %copy-done.29) | copy-start | bytes 786436
  162.5 42.4 %all-to-all-start.4 = ((bf16[4,128,1664]{2,1,0:T(8,128)(2,1)}), bf16[4,128,1664]{2,1,0:T(8,128)(2,1)S(1)}, u32[]{:S(2)}, u32[]{:S(2)}) async-start(bf16[4,128,1664]{2,1,0:T(8,128)(2,1)} %get-tuple-element.252.late), calls=%async_computation.4 | async-start | bytes 3407872 | tf_op jit(solution)/shard_map/all_to_all | solution.py:933
  167.7 10.0 %copy-start.3 = (bf16[4,4,128,256]{3,2,1,0:T(8,128)(2,1)}, bf16[4,4,128,256]{3,2,1,0:T(8,128)(2,1)S(1)}, u32[]{:S(2)}) copy-start(bf16[4,4,128,256]{3,2,1,0:T(8,128)(2,1)S(1)} %pad_maximum_fusion.2.cm) | copy-start | bytes 3145732
  167.8 23.2 %collective-permute-start.23 = (bf16[4,4,128,256]{3,2,1,0:T(8,128)(2,1)S(1)}, bf16[4,4,128,256]{3,2,1,0:T(8,128)(2,1)S(1)}, u32[]{:S(2)}, u32[]{:S(2)}) collective-permute-start(bf16[4,4,128,256]{3,2,1,0:T(8,128)(2,1)S(1)} %pad_maximum_fusion.2.cm), channel_id=1, source_target_pairs={{0,1},{1,0},{2,3},{3,2},{4,5},{5,4},{6,7},{7,6},{8,9},{9,8},{10,11... | collective-permute-start | bytes 3145736 | tf_op jit(solution)/shard_map/ppermute | solution.py:929
  167.8 21.3 %collective-permute-start.24 = (bf16[49,64,128]{2,1,0:T(8,128)(2,1)S(1)}, bf16[49,64,128]{2,1,0:T(8,128)(2,1)S(1)}, u32[]{:S(2)}, u32[]{:S(2)}) collective-permute-start(bf16[49,64,128]{2,1,0:T(8,128)(2,1)S(1)} %copy-done.14), channel_id=1, source_target_pairs={{0,16},{8,24},{16,0},{24,8},{1,17},{9,25},{17,1},{25,9},{2,18},{10... | collective-permute-start | bytes 2408456 | tf_op jit(solution)/shard_map/ppermute | solution.py:939
  169.4 21.5 %collective-permute-start.25 = (bf16[49,64,128]{2,1,0:T(8,128)(2,1)}, bf16[49,64,128]{2,1,0:T(8,128)(2,1)S(1)}, u32[]{:S(2)}, u32[]{:S(2)}) collective-permute-start(bf16[49,64,128]{2,1,0:T(8,128)(2,1)} %collective-permute-done.12.refs_6_), channel_id=1, source_target_pairs={{0,8},{8,0},{16,24},{24,16},{1,9},{9,1},{17,25},{25,17},{2,10},{10... | collective-permute-start | bytes 2408456 | tf_op jit(solution)/shard_map/ppermute | solution.py:939
  170.3 7.5 %copy-start.21 = (bf16[4,160,256]{2,1,0:T(8,128)(2,1)S(1)}, bf16[4,160,256]{2,1,0:T(8,128)(2,1)}, u32[]{:S(2)}) copy-start(bf16[4,160,256]{2,1,0:T(8,128)(2,1)} %copy-done.20) | copy-start | bytes 983044
  177.8 1.7 collective-permute-start.19
  187.5 15.5 %collective-permute-start.20 = (bf16[32,3200]{1,0:T(8,128)(2,1)}, bf16[32,3200]{1,0:T(8,128)(2,1)S(1)}, u32[]{:S(2)}, u32[]{:S(2)}) collective-permute-start(bf16[32,3200]{1,0:T(8,128)(2,1)} %get-tuple-element.260), channel_id=1, source_target_pairs={{0,8},{8,0},{16,24},{24,16},{1,9},{9,1},{17,25},{25,17},{2,10},{10... | collective-permute-start | bytes 614408 | tf_op jit(solution)/shard_map/ppermute | solution.py:939
  188.6 14.4 %collective-permute-start.21 = (bf16[32,3200]{1,0:T(8,128)(2,1)}, bf16[32,3200]{1,0:T(8,128)(2,1)S(1)}, u32[]{:S(2)}, u32[]{:S(2)}) collective-permute-start(bf16[32,3200]{1,0:T(8,128)(2,1)} %get-tuple-element.261), channel_id=1, source_target_pairs={{0,16},{8,24},{16,0},{24,8},{1,17},{9,25},{17,1},{25,9},{2,18},{10... | collective-permute-start | bytes 614408 | tf_op jit(solution)/shard_map/ppermute | solution.py:939
  189.2 13.9 %collective-permute-start.22 = (bf16[32,3200]{1,0:T(8,128)(2,1)}, bf16[32,3200]{1,0:T(8,128)(2,1)S(1)}, u32[]{:S(2)}, u32[]{:S(2)}) collective-permute-start(bf16[32,3200]{1,0:T(8,128)(2,1)} %get-tuple-element.262), channel_id=1, source_target_pairs={{0,24},{8,16},{16,8},{24,0},{1,25},{9,17},{17,9},{25,1},{2,26},{10... | collective-permute-start | bytes 614408 | tf_op jit(solution)/shard_map/ppermute | solution.py:939
  191.0 13.8 %copy-start.42 = (bf16[128,1024]{1,0:T(8,128)(2,1)S(1)}, bf16[128,1024]{1,0:T(8,128)(2,1)}, u32[]{:S(2)}) copy-start(bf16[128,1024]{1,0:T(8,128)(2,1)} %get-tuple-element.285) | copy-start | bytes 786436
  191.0 14.3 %copy-start.41 = (bf16[128,1024]{1,0:T(8,128)(2,1)S(1)}, bf16[128,1024]{1,0:T(8,128)(2,1)}, u32[]{:S(2)}) copy-start(bf16[128,1024]{1,0:T(8,128)(2,1)} %get-tuple-element.286) | copy-start | bytes 786436
  191.0 16.6 %copy-start.40 = (bf16[128,1024]{1,0:T(8,128)(2,1)S(1)}, bf16[128,1024]{1,0:T(8,128)(2,1)}, u32[]{:S(2)}) copy-start(bf16[128,1024]{1,0:T(8,128)(2,1)} %get-tuple-element.287) | copy-start | bytes 786436
  203.0 28.9 %copy-start.34 = (bf16[32,3200]{1,0:T(8,128)(2,1)}, bf16[32,3200]{1,0:T(8,128)(2,1)S(1)}, u32[]{:S(2)}) copy-start(bf16[32,3200]{1,0:T(8,128)(2,1)S(1)} %collective-permute-done.20.refs_1_) | copy-start | bytes 614404
  203.0 28.9 %copy-start.35 = (bf16[32,3200]{1,0:T(8,128)(2,1)}, bf16[32,3200]{1,0:T(8,128)(2,1)S(1)}, u32[]{:S(2)}) copy-start(bf16[32,3200]{1,0:T(8,128)(2,1)S(1)} %collective-permute-done.21.refs_2_) | copy-start | bytes 614404
  203.0 28.9 %copy-start.36 = (bf16[32,3200]{1,0:T(8,128)(2,1)}, bf16[32,3200]{1,0:T(8,128)(2,1)S(1)}, u32[]{:S(2)}) copy-start(bf16[32,3200]{1,0:T(8,128)(2,1)S(1)} %collective-permute-done.22.refs_3_) | copy-start | bytes 614404
  204.8 4.5 %copy-start.4 = (bf16[4,128,1664]{2,1,0:T(8,128)(2,1)}, bf16[4,128,1664]{2,1,0:T(8,128)(2,1)S(1)}, u32[]{:S(2)}) copy-start(bf16[4,128,1664]{2,1,0:T(8,128)(2,1)S(1)} %all-to-all-done.4.l0) | copy-start | bytes 5111812
  204.8 4.5 %collective-permute-start.29 = (bf16[4,128,1664]{2,1,0:T(8,128)(2,1)S(1)}, bf16[4,128,1664]{2,1,0:T(8,128)(2,1)S(1)}, u32[]{:S(2)}, u32[]{:S(2)}) collective-permute-start(bf16[4,128,1664]{2,1,0:T(8,128)(2,1)S(1)} %all-to-all-done.4.l0), channel_id=1, source_target_pairs={{0,1},{1,0},{2,3},{3,2},{4,5},{5,4},{6,7},{7,6},{8,9},{9,8},{10,11... | collective-permute-start | bytes 5111816 | tf_op jit(solution)/shard_map/ppermute | solution.py:929
  204.8 17.2 %collective-permute-start.26 = (bf16[128,1024]{1,0:T(8,128)(2,1)S(1)}, bf16[128,1024]{1,0:T(8,128)(2,1)S(1)}, u32[]{:S(2)}, u32[]{:S(2)}) collective-permute-start(bf16[128,1024]{1,0:T(8,128)(2,1)S(1)} %copy-done.42), channel_id=1, source_target_pairs={{0,2},{1,3},{2,0},{3,1},{4,6},{5,7},{6,4},{7,5},{8,10},{9,11},{10,... | collective-permute-start | bytes 786440 | tf_op jit(solution)/shard_map/ppermute | solution.py:943
  205.3 28.8 %collective-permute-start.27 = (bf16[128,1024]{1,0:T(8,128)(2,1)S(1)}, bf16[128,1024]{1,0:T(8,128)(2,1)S(1)}, u32[]{:S(2)}, u32[]{:S(2)}) collective-permute-start(bf16[128,1024]{1,0:T(8,128)(2,1)S(1)} %copy-done.41), channel_id=1, source_target_pairs={{0,4},{1,5},{2,6},{3,7},{4,0},{5,1},{6,2},{7,3},{8,12},{9,13},{10,... | collective-permute-start | bytes 786440 | tf_op jit(solution)/shard_map/ppermute | solution.py:943
  207.6 26.5 %collective-permute-start.28 = (bf16[128,1024]{1,0:T(8,128)(2,1)S(1)}, bf16[128,1024]{1,0:T(8,128)(2,1)S(1)}, u32[]{:S(2)}, u32[]{:S(2)}) collective-permute-start(bf16[128,1024]{1,0:T(8,128)(2,1)S(1)} %copy-done.40), channel_id=1, source_target_pairs={{0,6},{1,7},{2,4},{3,5},{4,2},{5,3},{6,0},{7,1},{8,14},{9,15},{10,... | collective-permute-start | bytes 786440 | tf_op jit(solution)/shard_map/ppermute | solution.py:943
  219.5 14.6 %collective-permute-start.30 = (bf16[32,3712]{1,0:T(8,128)(2,1)}, bf16[32,3712]{1,0:T(8,128)(2,1)S(1)}, u32[]{:S(2)}, u32[]{:S(2)}) collective-permute-start(bf16[32,3712]{1,0:T(8,128)(2,1)} %get-tuple-element.293), channel_id=1, source_target_pairs={{0,8},{8,0},{16,24},{24,16},{1,9},{9,1},{17,25},{25,17},{2,10},{10... | collective-permute-start | bytes 712712 | tf_op jit(solution)/shard_map/ppermute | solution.py:939
  220.5 13.7 %collective-permute-start.31 = (bf16[32,3712]{1,0:T(8,128)(2,1)}, bf16[32,3712]{1,0:T(8,128)(2,1)S(1)}, u32[]{:S(2)}, u32[]{:S(2)}) collective-permute-start(bf16[32,3712]{1,0:T(8,128)(2,1)} %get-tuple-element.294), channel_id=1, source_target_pairs={{0,16},{8,24},{16,0},{24,8},{1,17},{9,25},{17,1},{25,9},{2,18},{10... | collective-permute-start | bytes 712712 | tf_op jit(solution)/shard_map/ppermute | solution.py:939
  222.0 12.1 %collective-permute-start.32 = (bf16[32,3712]{1,0:T(8,128)(2,1)}, bf16[32,3712]{1,0:T(8,128)(2,1)S(1)}, u32[]{:S(2)}, u32[]{:S(2)}) collective-permute-start(bf16[32,3712]{1,0:T(8,128)(2,1)} %get-tuple-element.295), channel_id=1, source_target_pairs={{0,24},{8,16},{16,8},{24,0},{1,25},{9,17},{17,9},{25,1},{2,26},{10... | collective-permute-start | bytes 712712 | tf_op jit(solution)/shard_map/ppermute | solution.py:939
  223.0 11.1 %copy-start.18 = (f32[128,1024]{1,0:T(8,128)S(1)}, f32[128,1024]{1,0:T(8,128)}, u32[]{:S(2)}) copy-start(f32[128,1024]{1,0:T(8,128)} %get-tuple-element.180.h1) | copy-start | bytes 1572868
  223.0 11.1 %copy-start.27 = (bf16[128,1024]{1,0:T(8,128)(2,1)S(1)}, bf16[128,1024]{1,0:T(8,128)(2,1)}, u32[]{:S(2)}) copy-start(bf16[128,1024]{1,0:T(8,128)(2,1)} %get-tuple-element.320) | copy-start | bytes 786436
  (17 other events, 18.0 us)

commit v2 on v1

--- a/solution.py
+++ b/solution.py
@@ -384,24 +384,28 @@
     row, col = iota((T, T), 0), iota((T, T), 1)
     causal = (col <= row) & (col < n_live)
     width = ea * dh
-    for h in range(heads):
-        proj = mm(li[...], wv[:, h * width : (h + 1) * width], 1, 0)
-        p_o[:, h * width : (h + 1) * width] = proj
+    every = range(heads)
+    hs = [slice(h * dh, (h + 1) * dh) for h in every]
+    scores = [jnp.where(causal, mm(q[:, hs[h]], k[:, hs[h]], 1, 1) * scaling, NEGATIVE) for h in every]
+    proj = [mm(li[...], wv[:, h * width : (h + 1) * width], 1, 0) for h in every]
+    vs, weights = [], []
+    for h in every:
+        p_o[:, h * width : (h + 1) * width] = proj[h]
         v = jnp.zeros((T, dh), f32)
         for e in range(ea):
-            v += gt[:, h * ea + e : h * ea + e + 1] * proj[:, e * dh : (e + 1) * dh]
-        v = v.astype(bf16)
-        v_o[:, h * dh : (h + 1) * dh] = v
-        s = mm(q[:, h * dh : (h + 1) * dh], k[:, h * dh : (h + 1) * dh], 1, 1) * scaling
-        s = jnp.where(causal, s, NEGATIVE)
-        ex = jnp.exp(s - jnp.max(s, axis=-1, keepdims=True))
+            v += gt[:, h * ea + e : h * ea + e + 1] * proj[h][:, e * dh : (e + 1) * dh]
+        vs.append(v.astype(bf16))
+        v_o[:, hs[h]] = vs[h]
+        ex = jnp.exp(scores[h] - jnp.max(scores[h], axis=-1, keepdims=True))
         a = ex / jnp.sum(ex, axis=-1, keepdims=True)
         a_o[h] = a
-        o = mm(a.astype(bf16), v, 1, 0)
-        o_o[:, h * dh : (h + 1) * dh] = o
+        weights.append(a.astype(bf16))
+    attended = [mm(weights[h], vs[h], 1, 0) for h in every]
+    for h in every:
+        o_o[:, hs[h]] = attended[h]
         for e in range(ea):
             c = he + h * ea + e
-            mixed[:, (h * ea + e) * dh : (h * ea + e + 1) * dh] = (gt[:, c : c + 1] * o).astype(bf16)
+            mixed[:, (h * ea + e) * dh : (h * ea + e + 1) * dh] = (gt[:, c : c + 1] * attended[h]).astype(bf16)
     h1 = x + mm(mixed[...], wo[...], 1, 0)
     h1_o[...] = h1
     hat2, _ = centre(h1)

time: 238 us -> 238 us (level)
  no operation moved by 1% of the time
where the time goes in v2:
time: 238 us; the launch traced here: 237 us
  Pallas kernels  122 us (51%)
  starting transfers between devices  56.4 us (24%)
  waiting for transfers between devices  38 us (16%)
  local copies, waits for them, and re-layouts  11.2 us (5%)
  other arithmetic  7.12 us (3%)
    pallas_call x13, Pallas kernels, call(): pl.pallas_call(body, out_shape=[jax.ShapeDtypeStruct(s, d) for s, d in ou...  64.5 us
    pallas_call x1, Pallas kernels, fast_path(): pl.pallas_call(partial(experts_body, S, eb), grid=(n_eb,), out_shape=[jax...  27.9 us
    all_to_all x5, starting transfers between devices, chips(): lax.all_to_all(v, 'expert', 0, 0, axis_index_groups=groups, tiled=True)  22.8 us
    ppermute x18, starting transfers between devices, plane(): return lax.ppermute(v, 'dp', [(p, p ^ s) for p in range(self.n_p)])  22.4 us
    pallas_call x2, Pallas kernels, expert_grads(): pl.pallas_call(partial(expert_grads_body, n_p, eb, first), grid=(last - f...  19 us
    ppermute x6, waiting for transfers between devices, near(): lax.ppermute(msgs[s], 'expert', pairs[s])  12.2 us
    ppermute x9, waiting for transfers between devices, core(): return lax.ppermute(v, 'expert', [(e, e ^ 1) for e in range(self.n_e)])  11.6 us
    ppermute x18, waiting for transfers between devices, plane(): return lax.ppermute(v, 'dp', [(p, p ^ s) for p in range(self.n_p)])  10.6 us
  transfers between devices with their start and end apart: 38, of which 10 were waited for; matrix products, arithmetic and copies ran while one was open for 3% of the time, Pallas kernels for 50%

profile of v2, /device:TPU:0, one launch (start us, length us, event | category | flops | bytes accessed | tf_op | source)
XLA Modules:
  0.0 236.8 jit_solution(1611841727134667148)
XLA Ops:
  2.6 1.0 pad_maximum_fusion.3
  3.6 5.1 %collective-permute-start.2 = (bf16[144,1024]{1,0:T(8,128)(2,1)S(1)}, bf16[144,1024]{1,0:T(8,128)(2,1)S(1)}, u32[]{:S(2)}, u32[]{:S(2)}) collective-permute-start(bf16[144,1024]{1,0:T(8,128)(2,1)S(1)} %pad_maximum_fusion.3), channel_id=1, source_target_pairs={{0,6},{1,7},{2,4},{3,5},{4,2},{5,3},{6,0},{7,1},{8,14},{9,15},{10,... | collective-permute-start | bytes 884744 | tf_op jit(solution)/shard_map/ppermute | solution.py:947
  9.4 10.2 %forward.1 = (f32[128,1024]{1,0:T(8,128)}, bf16[4,144,1024]{2,1,0:T(8,128)(2,1)}, bf16[128,512]{1,0:T(8,128)(2,1)}, bf16[128,512]{1,0:T(8,128)(2,1)}, bf16[128,5...) custom-call(s32[1]{0:T(128)} %copy.44.length, ...), custom_call_target="tpu_custom_call" | custom-call | flops 1 | bytes 1 | tf_op jit(solution)/shard_map/forward/pallas_call | solution.py:335
  19.6 5.0 %all-to-all-start = ((bf16[4,144,1024]{2,1,0:T(8,128)(2,1)}), bf16[4,144,1024]{2,1,0:T(8,128)(2,1)S(1)}, u32[]{:S(2)}, u32[]{:S(2)}) async-start(bf16[4,144,1024]{2,1,0:T(8,128)(2,1)} %get-tuple-element.181), calls=%async_computation | async-start | bytes 2359296 | tf_op jit(solution)/shard_map/all_to_all | solution.py:937
  25.2 3.2 %early_slices.1 = bf16[4,128,1408]{2,1,0:T(8,128)(2,1)} custom-call(s32[4]{0:T(128)} %pad_add_fusion.ids, bf16[128,1024]{1,0:T(8,128)(2,1)} %li.5, bf16[128,1024]{1,0:T(8,128)(2,1)} %get-tuple-element.182.a1, bf16[128,1024]{1,0:T(8,128)(2,1)} %get-tuple-element.183.a2, f32[128,512]{1,0:T(8,128)} %get-tuple-element.184.o, f32[128,128]{1,0:T(8,128)} %get-tuple-element.185.gt), custom_call_target="tpu_custom_call" | custom-call | flops 1 | bytes 1 | tf_op jit(solution)/shard_map/early_slices/pallas_call | solution.py:335
  28.6 0.8 pad.19.selw
  29.7 1.1 pad.18
  30.8 12.2 %collective-permute-done.1 = bf16[144,1024]{1,0:T(8,128)(2,1)} collective-permute-done((bf16[144,1024]{1,0:T(8,128)(2,1)S(1)}, bf16[144,1024]{1,0:T(8,128)(2,1)}, u32[]{:S(2)}, u32[]{:S(2)}) %collective-permute-start.1) | collective-permute-done | bytes 294944 | tf_op jit(solution)/shard_map/ppermute | solution.py:947
  43.0 1.2 pad_maximum_fusion.1.x.refs_0_.refs_2_
  44.3 2.8 %collective-permute-done.3.refs_1_.refs_3_ = bf16[4,144,1024]{2,1,0:T(8,128)(2,1)S(1)} collective-permute-done((bf16[4,144,1024]{2,1,0:T(8,128)(2,1)S(1)}, bf16[4,144,1024]{2,1,0:T(8,128)(2,1)S(1)}, u32[]{:S(2)}, u32[]{:S(2)}) %collective-permute-start.3) | collective-permute-done | bytes 1179680 | tf_op jit(solution)/shard_map/ppermute | solution.py:933
  47.1 2.8 %cotangent_columns.1 = (bf16[4,128,256]{2,1,0:T(8,128)(2,1)}, bf16[4,128,256]{2,1,0:T(8,128)(2,1)}, bf16[4,128,256]{2,1,0:T(8,128)(2,1)}, bf16[4,128,256]{2,1,0:T(8,128)(2,1)}) custom-call(s32[4]{0:T(128)} %pad_add_fusion.ids, bf16[4,144,1024]{2,1,0:T(8,128)(2,1)} %copy-done), custom_call_target="tpu_custom_call" | custom-call | flops 1 | bytes 1 | tf_op jit(solution)/shard_map/cotangent_columns/pallas_call | solution.py:335
  49.9 1.5 collective-permute-start.4
  51.4 1.5 collective-permute-start.5
  52.9 1.9 codes.1
  54.8 3.6 %collective-permute-done.4 = bf16[4,128,256]{2,1,0:T(8,128)(2,1)S(1)} collective-permute-done((bf16[4,128,256]{2,1,0:T(8,128)(2,1)}, bf16[4,128,256]{2,1,0:T(8,128)(2,1)S(1)}, u32[]{:S(2)}, u32[]{:S(2)}) %collective-permute-start.4) | collective-permute-done | bytes 262176 | tf_op jit(solution)/shard_map/ppermute | solution.py:943
  59.8 3.7 %all-to-all-start.1 = ((bf16[4,128,1408]{2,1,0:T(8,128)(2,1)}), bf16[4,128,1408]{2,1,0:T(8,128)(2,1)S(1)}, u32[]{:S(2)}, u32[]{:S(2)}) async-start(bf16[4,128,1408]{2,1,0:T(8,128)(2,1)} %early_slices.1), calls=%async_computation.1 | async-start | bytes 2883584 | tf_op jit(solution)/shard_map/all_to_all | solution.py:937
  63.6 2.6 %token_columns.1 = (bf16[4,192,256]{2,1,0:T(8,128)(2,1)}, bf16[4,192,256]{2,1,0:T(8,128)(2,1)}, bf16[4,192,256]{2,1,0:T(8,128)(2,1)}, bf16[4,192,256]{2,1,0:T(8,128)(2,1)}) custom-call(s32[4]{0:T(128)} %pad_add_fusion.ids, bf16[4,144,1024]{2,1,0:T(8,128)(2,1)} %copy-done.2, bf16[4,64,256]{2,1,0:T(8,128)(2,1)} %get-tuple-element.200.refs_0_.refs_4_), custom_call_target="tpu_custom_call" | custom-call | flops 1 | bytes 1 | tf_op jit(solution)/shard_map/token_columns/pallas_call | solution.py:335
  66.2 0.9 collective-permute-start.7
  67.1 1.5 collective-permute-start.8
  68.6 1.1 collective-permute-start.9
  69.7 1.1 copy-done.22
  70.8 27.9 %experts.1 = (bf16[4,144,1024]{2,1,0:T(8,128)(2,1)}, bf16[4,144,1024]{2,1,0:T(8,128)(2,1)}, bf16[4,128,1024]{2,1,0:T(8,128)(2,1)}, bf16[4,128,1024]{2,1,0:T(8,12...) custom-call(s32[4]{0:T(128)} %pad_add_fusion.ids, bf16[4,144,1024]{2,1,0:T(8,128)(2,1)} %copy-done.2, ...), custom_call_target="tpu_custom_call" | custom-call | flops 1 | bytes 1 | tf_op jit(solution)/shard_map/experts/pallas_call | solution.py:1047
  98.8 3.0 %collective-permute-done.10.recv = bf16[4,144,1024]{2,1,0:T(8,128)(2,1)S(1)} collective-permute-done((bf16[4,144,1024]{2,1,0:T(8,128)(2,1)}, bf16[4,144,1024]{2,1,0:T(8,128)(2,1)S(1)}, u32[]{:S(2)}, u32[]{:S(2)}) %collective-permute-start.10) | collective-permute-done | bytes 1179680 | tf_op jit(solution)/shard_map/ppermute | solution.py:933
  101.9 1.0 copy-done.23
  102.9 3.0 %join_dx.1 = bf16[4,144,1024]{2,1,0:T(8,128)(2,1)} custom-call(bf16[4,144,1024]{2,1,0:T(8,128)(2,1)} %get-tuple-element.210.mine, bf16[4,144,1024]{2,1,0:T(8,128)(2,1)} %copy-done.23), custom_call_target="tpu_custom_call" | custom-call | flops 1 | bytes 1 | tf_op jit(solution)/shard_map/join_dx/pallas_call | solution.py:335
  105.8 4.9 %all-to-all-start.2 = ((bf16[4,144,1024]{2,1,0:T(8,128)(2,1)}), bf16[4,144,1024]{2,1,0:T(8,128)(2,1)S(1)}, u32[]{:S(2)}, u32[]{:S(2)}) async-start(bf16[4,144,1024]{2,1,0:T(8,128)(2,1)} %join_dx.1), calls=%async_computation.2 | async-start | bytes 2359296 | tf_op jit(solution)/shard_map/all_to_all | solution.py:937
  110.8 1.5 pad_maximum_fusion.xm
  112.9 1.1 collective-permute-start.11
  114.0 1.5 collective-permute-start.12
  115.5 4.1 %collective-permute-done.14.recv = bf16[4,128,1024]{2,1,0:T(8,128)(2,1)} collective-permute-done((bf16[4,128,1024]{2,1,0:T(8,128)(2,1)}, bf16[4,128,1024]{2,1,0:T(8,128)(2,1)}, u32[]{:S(2)}, u32[]{:S(2)}) %collective-permute-start.14) | collective-permute-done | bytes 1048608 | tf_op jit(solution)/shard_map/ppermute | solution.py:933
  119.6 2.0 collective-permute-start.15
  121.7 2.7 %join_out.1 = (bf16[128,1024]{1,0:T(8,128)(2,1)}, bf16[128,1024]{1,0:T(8,128)(2,1)}, bf16[128,1024]{1,0:T(8,128)(2,1)}, bf16[128,1024]{1,0:T(8,128)(2,1)}) custom-call(s32[4]{0:T(128)} %pad_add_fusion.ids, bf16[4,128,1024]{2,1,0:T(8,128)(2,1)} %get-tuple-element.225.mine, bf16[4,128,1024]{2,1,0:T(8,128)(2,1)} %collective-permute-done.14.recv), custom_call_target="tpu_custom_call" | custom-call | flops 1 | bytes 1 | tf_op jit(solution)/shard_map/join_out/pallas_call | solution.py:335
  124.4 9.2 %spread_tokens.1 = (bf16[1024,2560]{1,0:T(8,128)(2,1)}, bf16[1024,128]{1,0:T(8,128)(2,1)}, bf16[256,1024]{1,0:T(8,128)(2,1)}, f32[128,1024]{1,0:T(8,128)}, f32[1...) custom-call(s32[4]{0:T(128)} %pad_add_fusion.ids, bf16[4,128,1408]{2,1,0:T(8,128)(2,1)} %copy-done.6, ...), custom_call_target="tpu_custom_call" | custom-call | flops 1 | bytes 268435456 | tf_op jit(solution)/shard_map/spread_tokens/pallas_call | solution.py:335
  133.6 6.3 %collective-permute-done.15 = bf16[4,128,256]{2,1,0:T(8,128)(2,1)} collective-permute-done((bf16[4,128,256]{2,1,0:T(8,128)(2,1)}, bf16[4,128,256]{2,1,0:T(8,128)(2,1)}, u32[]{:S(2)}, u32[]{:S(2)}) %collective-permute-start.15) | collective-permute-done | bytes 262176 | tf_op jit(solution)/shard_map/ppermute | solution.py:943
  139.8 0.9 copy-done.13
  141.4 1.1 collective-permute-start.18
  142.5 4.3 %ffn_back.1 = (f32[128,1024]{1,0:T(8,128)}, bf16[128,1024]{1,0:T(8,128)(2,1)}, bf16[4,160,256]{2,1,0:T(8,128)(2,1)}) custom-call(s32[4]{0:T(128)} %pad_add_fusion.ids, bf16[4,144,1024]{2,1,0:T(8,128)(2,1)} %copy-done.9, f32[128,1024]{1,0:T(8,128)} %get-tuple-element.180.h1, bf16[128,1024]{1,0:T(8,128)(2,1)} %c.1, bf16[512,1024]{1,0:T(8,128)(2,1)} %bitcast.40, ...), custom_call_target="tpu_custom_call" | custom-call | flops 1 | bytes 1 | tf_op jit(solution)/shard_map/ffn_back/pallas_call | solution.py:335
  146.8 5.1 %all-to-all-start.3 = ((bf16[4,160,256]{2,1,0:T(8,128)(2,1)}), bf16[4,160,256]{2,1,0:T(8,128)(2,1)S(1)}, u32[]{:S(2)}, u32[]{:S(2)}) async-start(bf16[4,160,256]{2,1,0:T(8,128)(2,1)} %get-tuple-element.249), calls=%async_computation.3 | async-start | bytes 655360 | tf_op jit(solution)/shard_map/all_to_all | solution.py:937
  151.9 7.6 %attention_back.1 = (bf16[4,128,1664]{2,1,0:T(8,128)(2,1)}, bf16[128,2560]{1,0:T(8,128)(2,1)}) custom-call(bf16[128,1024]{1,0:T(8,128)(2,1)} %get-tuple-element.242.db, bf16[2560,1024]{1,0:T(8,128)(2,1)} %wo.3, f32[128,128]{1,0:T(8,128)} %get-tuple-element.185.gt, f32[128,512]{1,0:T(8,128)} %get-tuple-element.184.o, bf16[128,512]{1,0:T(8,128)(2,1)} %get-tuple-element.243.q, ...), custom_call_target="tpu_custom_call" | custom-call | flops 1 | bytes 268435456 | tf_op jit(solution)/shard_map/attention_back/pallas_call | solution.py:335
  159.5 1.9 all-to-all-done.3.m0
  162.1 4.0 %all-to-all-start.4 = ((bf16[4,128,1664]{2,1,0:T(8,128)(2,1)}), bf16[4,128,1664]{2,1,0:T(8,128)(2,1)S(1)}, u32[]{:S(2)}, u32[]{:S(2)}) async-start(bf16[4,128,1664]{2,1,0:T(8,128)(2,1)} %get-tuple-element.252.late), calls=%async_computation.4 | async-start | bytes 3407872 | tf_op jit(solution)/shard_map/all_to_all | solution.py:937
  166.1 1.2 pad_maximum_fusion.2.cm
  167.5 1.5 collective-permute-start.24
  169.0 1.1 collective-permute-start.25
  170.0 7.5 %input_back.1 = f32[128,1024]{1,0:T(8,128)} custom-call(bf16[4,128,1664]{2,1,0:T(8,128)(2,1)} %get-tuple-element.252.late, bf16[128,2560]{1,0:T(8,128)(2,1)} %get-tuple-element.253.dp, bf16[1024,512]{1,0:T(8,128)(2,1)} %wq.5, bf16[1024,512]{1,0:T(8,128)(2,1)} %wk.5, bf16[1024,2560]{1,0:T(8,128)(2,1)} %wv.3, bf16[1024,128]{1,0:T(8,128)(2,1)} %pad.19.selw, ...), custom_call_target="tpu_custom_call" | custom-call | flops 1 | bytes 1 | tf_op jit(solution)/shard_map/input_back/pallas_call | solution.py:335
  177.6 1.6 collective-permute-done.19.m1
  180.0 7.3 %out_grads.1 = (f32[32,3200]{1,0:T(8,128)}, bf16[32,3200]{1,0:T(8,128)(2,1)}, bf16[32,3200]{1,0:T(8,128)(2,1)}, bf16[32,3200]{1,0:T(8,128)(2,1)}) custom-call(s32[4]{0:T(128)} %pad_add_fusion.ids, bf16[4,160,256]{2,1,0:T(8,128)(2,1)} %copy-done.20, bf16[4,160,256]{2,1,0:T(8,128)(2,1)} %copy-done.26, bf16[1024,2560]{1,0:T(8,128)(2,1)} %get-tuple-element.256.z, ...), custom_call_target="tpu_custom_call" | custom-call | flops 1 | bytes 1 | tf_op jit(solution)/shard_map/out_grads/pallas_call | solution.py:335
  187.2 0.9 collective-permute-start.20
  188.8 2.0 collective-permute-start.22
  190.8 0.9 copy-done.16
  191.6 1.0 copy-done.10
  192.6 10.1 %expert_grads.2 = (f32[49,256,128]{2,1,0:T(8,128)}, f32[49,128,256]{2,1,0:T(8,128)}) custom-call(bf16[4,4,192,256]{3,2,1,0:T(8,128)(2,1)} %copy-done.1, bf16[4,4,192,256]{3,2,1,0:T(8,128)(2,1)} %copy-done.5, bf16[4,4,128,256]{3,2,1,0:T(8,128)(2,1)} %copy-done.3, bf16[4,4,128,256]{3,2,1,0:T(8,128)(2,1)} %copy-done.10, ...), custom_call_target="tpu_custom_call" | custom-call | flops 1 | bytes 1 | tf_op jit(solution)/shard_map/expert_grads/pallas_call | solution.py:1151
  202.8 1.6 all-to-all-done.4.l0
  205.0 2.4 %collective-permute-start.27 = (bf16[128,1024]{1,0:T(8,128)(2,1)S(1)}, bf16[128,1024]{1,0:T(8,128)(2,1)S(1)}, u32[]{:S(2)}, u32[]{:S(2)}) collective-permute-start(bf16[128,1024]{1,0:T(8,128)(2,1)S(1)} %copy-done.41), channel_id=1, source_target_pairs={{0,4},{1,5},{2,6},{3,7},{4,0},{5,1},{6,2},{7,3},{8,12},{9,13},{10,... | collective-permute-start | bytes 786440 | tf_op jit(solution)/shard_map/ppermute | solution.py:947
  207.4 1.5 collective-permute-start.28
  208.9 1.2 copy-done.19
  210.1 9.0 %in_grads.1 = (f32[32,3712]{1,0:T(8,128)}, bf16[32,3712]{1,0:T(8,128)(2,1)}, bf16[32,3712]{1,0:T(8,128)(2,1)}, bf16[32,3712]{1,0:T(8,128)(2,1)}) custom-call(s32[4]{0:T(128)} %pad_add_fusion.ids, bf16[4,128,1664]{2,1,0:T(8,128)(2,1)} %copy-done.4, bf16[4,128,1664]{2,1,0:T(8,128)(2,1)} %copy-done.19, bf16[256,1024]{1,0:T(8,128)(2,1)} %get-tuple-element.288.lia1, ...), custom_call_target="tpu_custom_call" | custom-call | flops 1 | bytes 268435456 | tf_op jit(solution)/shard_map/in_grads/pallas_call | solution.py:1178
  219.2 1.1 collective-permute-start.30
  220.2 1.5 collective-permute-start.31
  221.8 0.9 collective-permute-start.32
  222.7 8.9 %expert_grads.3 = (f32[49,256,128]{2,1,0:T(8,128)}, f32[49,128,256]{2,1,0:T(8,128)}) custom-call(bf16[4,4,192,256]{3,2,1,0:T(8,128)(2,1)} %copy-done.1, bf16[4,4,192,256]{3,2,1,0:T(8,128)(2,1)} %copy-done.5, bf16[4,4,128,256]{3,2,1,0:T(8,128)(2,1)} %copy-done.3, bf16[4,4,128,256]{3,2,1,0:T(8,128)(2,1)} %copy-done.10, ...), custom_call_target="tpu_custom_call", output_to_operand_aliasing={{0}: (12, {}), {1}: (13, {})} | custom-call | flops 1 | bytes 1 | tf_op jit(solution)/shard_map/expert_grads/pallas_call | solution.py:1151
  231.6 2.1 last_sum_a.1
  233.8 0.9 add_convert_fusion
  234.7 2.1 last_sum_b.1
  (132 shorter events, 8.8 us)
Async XLA Ops:
  3.6 27.2 %collective-permute-start.2 = (bf16[144,1024]{1,0:T(8,128)(2,1)S(1)}, bf16[144,1024]{1,0:T(8,128)(2,1)S(1)}, u32[]{:S(2)}, u32[]{:S(2)}) collective-permute-start(bf16[144,1024]{1,0:T(8,128)(2,1)S(1)} %pad_maximum_fusion.3), channel_id=1, source_target_pairs={{0,6},{1,7},{2,4},{3,5},{4,2},{5,3},{6,0},{7,1},{8,14},{9,15},{10,... | collective-permute-start | bytes 884744 | tf_op jit(solution)/shard_map/ppermute | solution.py:947
  8.7 34.3 %collective-permute-start.1 = (bf16[144,1024]{1,0:T(8,128)(2,1)S(1)}, bf16[144,1024]{1,0:T(8,128)(2,1)}, u32[]{:S(2)}, u32[]{:S(2)}) collective-permute-start(bf16[144,1024]{1,0:T(8,128)(2,1)S(1)} %pad_maximum_fusion.3), channel_id=1, source_target_pairs={{0,4},{1,5},{2,6},{3,7},{4,0},{5,1},{6,2},{7,3},{8,12},{9,13},{10,... | collective-permute-start | bytes 884744 | tf_op jit(solution)/shard_map/ppermute | solution.py:947
  8.7 34.3 %collective-permute-start = (bf16[144,1024]{1,0:T(8,128)(2,1)S(1)}, bf16[144,1024]{1,0:T(8,128)(2,1)}, u32[]{:S(2)}, u32[]{:S(2)}) collective-permute-start(bf16[144,1024]{1,0:T(8,128)(2,1)S(1)} %pad_maximum_fusion.3), channel_id=1, source_target_pairs={{0,2},{1,3},{2,0},{3,1},{4,6},{5,7},{6,4},{7,5},{8,10},{9,11},{10,... | collective-permute-start | bytes 884744 | tf_op jit(solution)/shard_map/ppermute | solution.py:947
  19.6 40.2 %all-to-all-start = ((bf16[4,144,1024]{2,1,0:T(8,128)(2,1)}), bf16[4,144,1024]{2,1,0:T(8,128)(2,1)S(1)}, u32[]{:S(2)}, u32[]{:S(2)}) async-start(bf16[4,144,1024]{2,1,0:T(8,128)(2,1)} %get-tuple-element.181), calls=%async_computation | async-start | bytes 2359296 | tf_op jit(solution)/shard_map/all_to_all | solution.py:937
  24.6 3.8 %copy-start.37 = (bf16[1024,20]{0,1:T(8,128)(2,1)S(1)}, bf16[1024,20]{0,1:T(8,128)(2,1)}, u32[]{:S(2)}) copy-start(bf16[1024,20]{0,1:T(8,128)(2,1)} %param.31) | copy-start | bytes 122884
  24.6 3.8 %copy-start.38 = (bf16[1024,20]{0,1:T(8,128)(2,1)S(1)}, bf16[1024,20]{0,1:T(8,128)(2,1)}, u32[]{:S(2)}) copy-start(bf16[1024,20]{0,1:T(8,128)(2,1)} %param.32) | copy-start | bytes 122884
  25.2 4.1 %copy-start.17 = (bf16[1024,387]{0,1:T(8,128)(2,1)S(1)}, bf16[1024,387]{0,1:T(8,128)(2,1)}, u32[]{:S(2)}) copy-start(bf16[1024,387]{0,1:T(8,128)(2,1)} %param.35) | copy-start | bytes 2377732
  44.2 2.9 %copy-start = (bf16[4,144,1024]{2,1,0:T(8,128)(2,1)}, bf16[4,144,1024]{2,1,0:T(8,128)(2,1)S(1)}, u32[]{:S(2)}) copy-start(bf16[4,144,1024]{2,1,0:T(8,128)(2,1)S(1)} %pad_maximum_fusion.1.x.refs_0_.refs_2_) | copy-start | bytes 3538948
  44.2 2.9 %collective-permute-start.3 = (bf16[4,144,1024]{2,1,0:T(8,128)(2,1)S(1)}, bf16[4,144,1024]{2,1,0:T(8,128)(2,1)S(1)}, u32[]{:S(2)}, u32[]{:S(2)}) collective-permute-start(bf16[4,144,1024]{2,1,0:T(8,128)(2,1)S(1)} %pad_maximum_fusion.1.x.refs_0_.refs_2_), channel_id=1, source_target_pairs={{0,1},{1,0},{2,3},{3,2},{4,5},{5,4},{6,7},{7,6},{8,9},{9,8},{10,11... | collective-permute-start | bytes 3538952 | tf_op jit(solution)/shard_map/ppermute | solution.py:933
  47.1 5.8 %copy-start.8 = (bf16[4,144,1024]{2,1,0:T(8,128)(2,1)}, bf16[4,144,1024]{2,1,0:T(8,128)(2,1)S(1)}, u32[]{:S(2)}) copy-start(bf16[4,144,1024]{2,1,0:T(8,128)(2,1)S(1)} %collective-permute-done.3.refs_1_.refs_3_) | copy-start | bytes 3538948
  49.9 8.6 %collective-permute-start.4 = (bf16[4,128,256]{2,1,0:T(8,128)(2,1)}, bf16[4,128,256]{2,1,0:T(8,128)(2,1)S(1)}, u32[]{:S(2)}, u32[]{:S(2)}) collective-permute-start(bf16[4,128,256]{2,1,0:T(8,128)(2,1)} %get-tuple-element.195), channel_id=1, source_target_pairs={{0,8},{8,0},{16,24},{24,16},{1,9},{9,1},{17,25},{25,17},{2,10},{10... | collective-permute-start | bytes 786440 | tf_op jit(solution)/shard_map/ppermute | solution.py:943
  51.4 8.4 %collective-permute-start.5 = (bf16[4,128,256]{2,1,0:T(8,128)(2,1)}, bf16[4,128,256]{2,1,0:T(8,128)(2,1)}, u32[]{:S(2)}, u32[]{:S(2)}) collective-permute-start(bf16[4,128,256]{2,1,0:T(8,128)(2,1)} %get-tuple-element.196), channel_id=1, source_target_pairs={{0,16},{8,24},{16,0},{24,8},{1,17},{9,25},{17,1},{25,9},{2,18},{10... | collective-permute-start | bytes 786440 | tf_op jit(solution)/shard_map/ppermute | solution.py:943
  59.8 3.8 %copy-start.2 = (bf16[4,144,1024]{2,1,0:T(8,128)(2,1)}, bf16[4,144,1024]{2,1,0:T(8,128)(2,1)S(1)}, u32[]{:S(2)}) copy-start(bf16[4,144,1024]{2,1,0:T(8,128)(2,1)S(1)} %all-to-all-done.x.refs_0_) | copy-start | bytes 3538948
  59.8 38.9 %all-to-all-start.1 = ((bf16[4,128,1408]{2,1,0:T(8,128)(2,1)}), bf16[4,128,1408]{2,1,0:T(8,128)(2,1)S(1)}, u32[]{:S(2)}, u32[]{:S(2)}) async-start(bf16[4,128,1408]{2,1,0:T(8,128)(2,1)} %early_slices.1), calls=%async_computation.1 | async-start | bytes 2883584 | tf_op jit(solution)/shard_map/all_to_all | solution.py:937
  63.5 6.1 %collective-permute-start.6 = (bf16[4,144,1024]{2,1,0:T(8,128)(2,1)S(1)}, bf16[4,144,1024]{2,1,0:T(8,128)(2,1)S(1)}, u32[]{:S(2)}, u32[]{:S(2)}) collective-permute-start(bf16[4,144,1024]{2,1,0:T(8,128)(2,1)S(1)} %all-to-all-done.x.refs_0_), channel_id=1, source_target_pairs={{0,1},{1,0},{2,3},{3,2},{4,5},{5,4},{6,7},{7,6},{8,9},{9,8},{10,11... | collective-permute-start | bytes 3538952 | tf_op jit(solution)/shard_map/ppermute | solution.py:933
  66.2 32.5 %collective-permute-start.7 = (bf16[4,192,256]{2,1,0:T(8,128)(2,1)}, bf16[4,192,256]{2,1,0:T(8,128)(2,1)S(1)}, u32[]{:S(2)}, u32[]{:S(2)}) collective-permute-start(bf16[4,192,256]{2,1,0:T(8,128)(2,1)} %get-tuple-element.203), channel_id=1, source_target_pairs={{0,8},{8,0},{16,24},{24,16},{1,9},{9,1},{17,25},{25,17},{2,10},{10... | collective-permute-start | bytes 1179656 | tf_op jit(solution)/shard_map/ppermute | solution.py:943
  67.1 31.6 %collective-permute-start.8 = (bf16[4,192,256]{2,1,0:T(8,128)(2,1)}, bf16[4,192,256]{2,1,0:T(8,128)(2,1)S(1)}, u32[]{:S(2)}, u32[]{:S(2)}) collective-permute-start(bf16[4,192,256]{2,1,0:T(8,128)(2,1)} %get-tuple-element.204), channel_id=1, source_target_pairs={{0,16},{8,24},{16,0},{24,8},{1,17},{9,25},{17,1},{25,9},{2,18},{10... | collective-permute-start | bytes 1179656 | tf_op jit(solution)/shard_map/ppermute | solution.py:943
  68.6 30.1 %collective-permute-start.9 = (bf16[4,192,256]{2,1,0:T(8,128)(2,1)}, bf16[4,192,256]{2,1,0:T(8,128)(2,1)}, u32[]{:S(2)}, u32[]{:S(2)}) collective-permute-start(bf16[4,192,256]{2,1,0:T(8,128)(2,1)} %get-tuple-element.205), channel_id=1, source_target_pairs={{0,24},{8,16},{16,8},{24,0},{1,25},{9,17},{17,9},{25,1},{2,26},{10... | collective-permute-start | bytes 1179656 | tf_op jit(solution)/shard_map/ppermute | solution.py:943
  98.7 3.2 %copy-start.25 = (bf16[4,192,256]{2,1,0:T(8,128)(2,1)}, bf16[4,192,256]{2,1,0:T(8,128)(2,1)S(1)}, u32[]{:S(2)}) copy-start(bf16[4,192,256]{2,1,0:T(8,128)(2,1)S(1)} %collective-permute-done.8) | copy-start | bytes 1179652
  98.7 7.1 %copy-start.6 = (bf16[4,128,1408]{2,1,0:T(8,128)(2,1)}, bf16[4,128,1408]{2,1,0:T(8,128)(2,1)S(1)}, u32[]{:S(2)}) copy-start(bf16[4,128,1408]{2,1,0:T(8,128)(2,1)S(1)} %all-to-all-done.1.e0) | copy-start | bytes 4325380
  98.7 3.1 %collective-permute-start.10 = (bf16[4,144,1024]{2,1,0:T(8,128)(2,1)}, bf16[4,144,1024]{2,1,0:T(8,128)(2,1)S(1)}, u32[]{:S(2)}, u32[]{:S(2)}) collective-permute-start(bf16[4,144,1024]{2,1,0:T(8,128)(2,1)} %get-tuple-element.211), channel_id=1, source_target_pairs={{0,1},{1,0},{2,3},{3,2},{4,5},{5,4},{6,7},{7,6},{8,9},{9,8},{10,11... | collective-permute-start | bytes 3538952 | tf_op jit(solution)/shard_map/ppermute | solution.py:933
  105.8 4.9 %copy-start.24 = (bf16[4,192,256]{2,1,0:T(8,128)(2,1)S(1)}, bf16[4,192,256]{2,1,0:T(8,128)(2,1)}, u32[]{:S(2)}) copy-start(bf16[4,192,256]{2,1,0:T(8,128)(2,1)} %get-tuple-element.232) | copy-start | bytes 1179652
  105.8 34.9 %all-to-all-start.2 = ((bf16[4,144,1024]{2,1,0:T(8,128)(2,1)}), bf16[4,144,1024]{2,1,0:T(8,128)(2,1)S(1)}, u32[]{:S(2)}, u32[]{:S(2)}) async-start(bf16[4,144,1024]{2,1,0:T(8,128)(2,1)} %join_dx.1), calls=%async_computation.2 | async-start | bytes 2359296 | tf_op jit(solution)/shard_map/all_to_all | solution.py:937
  110.8 2.2 copy-start.11
  110.8 3.2 %copy-start.12 = (bf16[49,64,128]{2,1,0:T(8,128)(2,1)S(1)}, bf16[49,64,128]{2,1,0:T(8,128)(2,1)}, u32[]{:S(2)}) copy-start(bf16[49,64,128]{2,1,0:T(8,128)(2,1)} %get-tuple-element.308.refs_4_) | copy-start | bytes 2408452
  112.3 21.3 %copy-start.1 = (bf16[4,4,192,256]{3,2,1,0:T(8,128)(2,1)}, bf16[4,4,192,256]{3,2,1,0:T(8,128)(2,1)S(1)}, u32[]{:S(2)}) copy-start(bf16[4,4,192,256]{3,2,1,0:T(8,128)(2,1)S(1)} %pad_maximum_fusion.xm) | copy-start | bytes 4718596
  112.3 28.5 %collective-permute-start.16 = (bf16[4,4,192,256]{3,2,1,0:T(8,128)(2,1)S(1)}, bf16[4,4,192,256]{3,2,1,0:T(8,128)(2,1)S(1)}, u32[]{:S(2)}, u32[]{:S(2)}) collective-permute-start(bf16[4,4,192,256]{3,2,1,0:T(8,128)(2,1)S(1)} %pad_maximum_fusion.xm), channel_id=1, source_target_pairs={{0,1},{1,0},{2,3},{3,2},{4,5},{5,4},{6,7},{7,6},{8,9},{9,8},{10,11... | collective-permute-start | bytes 4718600 | tf_op jit(solution)/shard_map/ppermute | solution.py:933
  112.4 12.0 %collective-permute-start.13 = (bf16[4,128,1408]{2,1,0:T(8,128)(2,1)S(1)}, bf16[4,128,1408]{2,1,0:T(8,128)(2,1)}, u32[]{:S(2)}, u32[]{:S(2)}) collective-permute-start(bf16[4,128,1408]{2,1,0:T(8,128)(2,1)S(1)} %copy-done.7), channel_id=1, source_target_pairs={{0,1},{1,0},{2,3},{3,2},{4,5},{5,4},{6,7},{7,6},{8,9},{9,8},{10,11... | collective-permute-start | bytes 4325384 | tf_op jit(solution)/shard_map/ppermute | solution.py:933
  112.8 6.8 %collective-permute-start.14 = (bf16[4,128,1024]{2,1,0:T(8,128)(2,1)}, bf16[4,128,1024]{2,1,0:T(8,128)(2,1)}, u32[]{:S(2)}, u32[]{:S(2)}) collective-permute-start(bf16[4,128,1024]{2,1,0:T(8,128)(2,1)} %get-tuple-element.226), channel_id=1, source_target_pairs={{0,1},{1,0},{2,3},{3,2},{4,5},{5,4},{6,7},{7,6},{8,9},{9,8},{10,11... | collective-permute-start | bytes 3145736 | tf_op jit(solution)/shard_map/ppermute | solution.py:933
  112.9 26.9 %collective-permute-start.11 = (bf16[49,64,128]{2,1,0:T(8,128)(2,1)S(1)}, bf16[49,64,128]{2,1,0:T(8,128)(2,1)S(1)}, u32[]{:S(2)}, u32[]{:S(2)}) collective-permute-start(bf16[49,64,128]{2,1,0:T(8,128)(2,1)S(1)} %copy-done.11), channel_id=1, source_target_pairs={{0,8},{8,0},{16,24},{24,16},{1,9},{9,1},{17,25},{25,17},{2,10},{10... | collective-permute-start | bytes 2408456 | tf_op jit(solution)/shard_map/ppermute | solution.py:943
  114.0 25.8 %collective-permute-start.12 = (bf16[49,64,128]{2,1,0:T(8,128)(2,1)S(1)}, bf16[49,64,128]{2,1,0:T(8,128)(2,1)}, u32[]{:S(2)}, u32[]{:S(2)}) collective-permute-start(bf16[49,64,128]{2,1,0:T(8,128)(2,1)S(1)} %copy-done.12), channel_id=1, source_target_pairs={{0,16},{8,24},{16,0},{24,8},{1,17},{9,25},{17,1},{25,9},{2,18},{10... | collective-permute-start | bytes 2408456 | tf_op jit(solution)/shard_map/ppermute | solution.py:943
  119.6 20.2 %collective-permute-start.15 = (bf16[4,128,256]{2,1,0:T(8,128)(2,1)}, bf16[4,128,256]{2,1,0:T(8,128)(2,1)}, u32[]{:S(2)}, u32[]{:S(2)}) collective-permute-start(bf16[4,128,256]{2,1,0:T(8,128)(2,1)} %get-tuple-element.231), channel_id=1, source_target_pairs={{0,24},{8,16},{16,8},{24,0},{1,25},{9,17},{17,9},{25,1},{2,26},{10... | collective-permute-start | bytes 786440 | tf_op jit(solution)/shard_map/ppermute | solution.py:943
  140.7 6.1 %copy-start.5 = (bf16[4,4,192,256]{3,2,1,0:T(8,128)(2,1)}, bf16[4,4,192,256]{3,2,1,0:T(8,128)(2,1)S(1)}, u32[]{:S(2)}) copy-start(bf16[4,4,192,256]{3,2,1,0:T(8,128)(2,1)S(1)} %collective-permute-done.16.xo) | copy-start | bytes 4718596
  140.8 20.6 %collective-permute-start.17 = (bf16[49,64,128]{2,1,0:T(8,128)(2,1)S(1)}, bf16[49,64,128]{2,1,0:T(8,128)(2,1)}, u32[]{:S(2)}, u32[]{:S(2)}) collective-permute-start(bf16[49,64,128]{2,1,0:T(8,128)(2,1)S(1)} %copy-done.11), channel_id=1, source_target_pairs={{0,16},{8,24},{16,0},{24,8},{1,17},{9,25},{17,1},{25,9},{2,18},{10... | collective-permute-start | bytes 2408456 | tf_op jit(solution)/shard_map/ppermute | solution.py:943
  141.4 19.9 %collective-permute-start.18 = (bf16[49,64,128]{2,1,0:T(8,128)(2,1)}, bf16[49,64,128]{2,1,0:T(8,128)(2,1)}, u32[]{:S(2)}, u32[]{:S(2)}) collective-permute-start(bf16[49,64,128]{2,1,0:T(8,128)(2,1)} %get-tuple-element.308.refs_4_), channel_id=1, source_target_pairs={{0,8},{8,0},{16,24},{24,16},{1,9},{9,1},{17,25},{25,17},{2,10},{10... | collective-permute-start | bytes 2408456 | tf_op jit(solution)/shard_map/ppermute | solution.py:943
  146.8 14.6 %all-to-all-start.3 = ((bf16[4,160,256]{2,1,0:T(8,128)(2,1)}), bf16[4,160,256]{2,1,0:T(8,128)(2,1)S(1)}, u32[]{:S(2)}, u32[]{:S(2)}) async-start(bf16[4,160,256]{2,1,0:T(8,128)(2,1)} %get-tuple-element.249), calls=%async_computation.3 | async-start | bytes 655360 | tf_op jit(solution)/shard_map/all_to_all | solution.py:937
  161.4 4.7 %copy-start.28 = (bf16[4,128,256]{2,1,0:T(8,128)(2,1)S(1)}, bf16[4,128,256]{2,1,0:T(8,128)(2,1)}, u32[]{:S(2)}) copy-start(bf16[4,128,256]{2,1,0:T(8,128)(2,1)} %get-tuple-element.265) | copy-start | bytes 786436
  161.4 4.7 %copy-start.30 = (bf16[4,128,256]{2,1,0:T(8,128)(2,1)S(1)}, bf16[4,128,256]{2,1,0:T(8,128)(2,1)}, u32[]{:S(2)}) copy-start(bf16[4,128,256]{2,1,0:T(8,128)(2,1)} %copy-done.29) | copy-start | bytes 786436
  162.1 42.3 %all-to-all-start.4 = ((bf16[4,128,1664]{2,1,0:T(8,128)(2,1)}), bf16[4,128,1664]{2,1,0:T(8,128)(2,1)S(1)}, u32[]{:S(2)}, u32[]{:S(2)}) async-start(bf16[4,128,1664]{2,1,0:T(8,128)(2,1)} %get-tuple-element.252.late), calls=%async_computation.4 | async-start | bytes 3407872 | tf_op jit(solution)/shard_map/all_to_all | solution.py:937
  167.4 10.2 %copy-start.3 = (bf16[4,4,128,256]{3,2,1,0:T(8,128)(2,1)}, bf16[4,4,128,256]{3,2,1,0:T(8,128)(2,1)S(1)}, u32[]{:S(2)}) copy-start(bf16[4,4,128,256]{3,2,1,0:T(8,128)(2,1)S(1)} %pad_maximum_fusion.2.cm) | copy-start | bytes 3145732
  167.4 23.4 %collective-permute-start.23 = (bf16[4,4,128,256]{3,2,1,0:T(8,128)(2,1)S(1)}, bf16[4,4,128,256]{3,2,1,0:T(8,128)(2,1)S(1)}, u32[]{:S(2)}, u32[]{:S(2)}) collective-permute-start(bf16[4,4,128,256]{3,2,1,0:T(8,128)(2,1)S(1)} %pad_maximum_fusion.2.cm), channel_id=1, source_target_pairs={{0,1},{1,0},{2,3},{3,2},{4,5},{5,4},{6,7},{7,6},{8,9},{9,8},{10,11... | collective-permute-start | bytes 3145736 | tf_op jit(solution)/shard_map/ppermute | solution.py:933
  167.5 21.3 %collective-permute-start.24 = (bf16[49,64,128]{2,1,0:T(8,128)(2,1)S(1)}, bf16[49,64,128]{2,1,0:T(8,128)(2,1)S(1)}, u32[]{:S(2)}, u32[]{:S(2)}) collective-permute-start(bf16[49,64,128]{2,1,0:T(8,128)(2,1)S(1)} %copy-done.14), channel_id=1, source_target_pairs={{0,16},{8,24},{16,0},{24,8},{1,17},{9,25},{17,1},{25,9},{2,18},{10... | collective-permute-start | bytes 2408456 | tf_op jit(solution)/shard_map/ppermute | solution.py:943
  169.0 21.8 %collective-permute-start.25 = (bf16[49,64,128]{2,1,0:T(8,128)(2,1)}, bf16[49,64,128]{2,1,0:T(8,128)(2,1)S(1)}, u32[]{:S(2)}, u32[]{:S(2)}) collective-permute-start(bf16[49,64,128]{2,1,0:T(8,128)(2,1)} %collective-permute-done.12.refs_6_), channel_id=1, source_target_pairs={{0,8},{8,0},{16,24},{24,16},{1,9},{9,1},{17,25},{25,17},{2,10},{10... | collective-permute-start | bytes 2408456 | tf_op jit(solution)/shard_map/ppermute | solution.py:943
  170.0 7.5 %copy-start.21 = (bf16[4,160,256]{2,1,0:T(8,128)(2,1)S(1)}, bf16[4,160,256]{2,1,0:T(8,128)(2,1)}, u32[]{:S(2)}) copy-start(bf16[4,160,256]{2,1,0:T(8,128)(2,1)} %copy-done.20) | copy-start | bytes 983044
  177.5 1.7 collective-permute-start.19
  187.2 15.5 %collective-permute-start.20 = (bf16[32,3200]{1,0:T(8,128)(2,1)}, bf16[32,3200]{1,0:T(8,128)(2,1)S(1)}, u32[]{:S(2)}, u32[]{:S(2)}) collective-permute-start(bf16[32,3200]{1,0:T(8,128)(2,1)} %get-tuple-element.260), channel_id=1, source_target_pairs={{0,8},{8,0},{16,24},{24,16},{1,9},{9,1},{17,25},{25,17},{2,10},{10... | collective-permute-start | bytes 614408 | tf_op jit(solution)/shard_map/ppermute | solution.py:943
  188.2 14.6 %collective-permute-start.21 = (bf16[32,3200]{1,0:T(8,128)(2,1)}, bf16[32,3200]{1,0:T(8,128)(2,1)S(1)}, u32[]{:S(2)}, u32[]{:S(2)}) collective-permute-start(bf16[32,3200]{1,0:T(8,128)(2,1)} %get-tuple-element.261), channel_id=1, source_target_pairs={{0,16},{8,24},{16,0},{24,8},{1,17},{9,25},{17,1},{25,9},{2,18},{10... | collective-permute-start | bytes 614408 | tf_op jit(solution)/shard_map/ppermute | solution.py:943
  188.8 14.0 %collective-permute-start.22 = (bf16[32,3200]{1,0:T(8,128)(2,1)}, bf16[32,3200]{1,0:T(8,128)(2,1)S(1)}, u32[]{:S(2)}, u32[]{:S(2)}) collective-permute-start(bf16[32,3200]{1,0:T(8,128)(2,1)} %get-tuple-element.262), channel_id=1, source_target_pairs={{0,24},{8,16},{16,8},{24,0},{1,25},{9,17},{17,9},{25,1},{2,26},{10... | collective-permute-start | bytes 614408 | tf_op jit(solution)/shard_map/ppermute | solution.py:943
  190.7 13.7 %copy-start.42 = (bf16[128,1024]{1,0:T(8,128)(2,1)S(1)}, bf16[128,1024]{1,0:T(8,128)(2,1)}, u32[]{:S(2)}) copy-start(bf16[128,1024]{1,0:T(8,128)(2,1)} %get-tuple-element.285) | copy-start | bytes 786436
  190.7 14.3 %copy-start.41 = (bf16[128,1024]{1,0:T(8,128)(2,1)S(1)}, bf16[128,1024]{1,0:T(8,128)(2,1)}, u32[]{:S(2)}) copy-start(bf16[128,1024]{1,0:T(8,128)(2,1)} %get-tuple-element.286) | copy-start | bytes 786436
  190.7 16.6 %copy-start.40 = (bf16[128,1024]{1,0:T(8,128)(2,1)S(1)}, bf16[128,1024]{1,0:T(8,128)(2,1)}, u32[]{:S(2)}) copy-start(bf16[128,1024]{1,0:T(8,128)(2,1)} %get-tuple-element.287) | copy-start | bytes 786436
  202.7 28.8 %copy-start.34 = (bf16[32,3200]{1,0:T(8,128)(2,1)}, bf16[32,3200]{1,0:T(8,128)(2,1)S(1)}, u32[]{:S(2)}) copy-start(bf16[32,3200]{1,0:T(8,128)(2,1)S(1)} %collective-permute-done.20.refs_1_) | copy-start | bytes 614404
  202.8 28.8 %copy-start.35 = (bf16[32,3200]{1,0:T(8,128)(2,1)}, bf16[32,3200]{1,0:T(8,128)(2,1)S(1)}, u32[]{:S(2)}) copy-start(bf16[32,3200]{1,0:T(8,128)(2,1)S(1)} %collective-permute-done.21.refs_2_) | copy-start | bytes 614404
  202.8 28.8 %copy-start.36 = (bf16[32,3200]{1,0:T(8,128)(2,1)}, bf16[32,3200]{1,0:T(8,128)(2,1)S(1)}, u32[]{:S(2)}) copy-start(bf16[32,3200]{1,0:T(8,128)(2,1)S(1)} %collective-permute-done.22.refs_3_) | copy-start | bytes 614404
  204.4 4.5 %copy-start.4 = (bf16[4,128,1664]{2,1,0:T(8,128)(2,1)}, bf16[4,128,1664]{2,1,0:T(8,128)(2,1)S(1)}, u32[]{:S(2)}) copy-start(bf16[4,128,1664]{2,1,0:T(8,128)(2,1)S(1)} %all-to-all-done.4.l0) | copy-start | bytes 5111812
  204.4 4.5 %collective-permute-start.29 = (bf16[4,128,1664]{2,1,0:T(8,128)(2,1)S(1)}, bf16[4,128,1664]{2,1,0:T(8,128)(2,1)S(1)}, u32[]{:S(2)}, u32[]{:S(2)}) collective-permute-start(bf16[4,128,1664]{2,1,0:T(8,128)(2,1)S(1)} %all-to-all-done.4.l0), channel_id=1, source_target_pairs={{0,1},{1,0},{2,3},{3,2},{4,5},{5,4},{6,7},{7,6},{8,9},{9,8},{10,11... | collective-permute-start | bytes 5111816 | tf_op jit(solution)/shard_map/ppermute | solution.py:933
  204.4 17.3 %collective-permute-start.26 = (bf16[128,1024]{1,0:T(8,128)(2,1)S(1)}, bf16[128,1024]{1,0:T(8,128)(2,1)S(1)}, u32[]{:S(2)}, u32[]{:S(2)}) collective-permute-start(bf16[128,1024]{1,0:T(8,128)(2,1)S(1)} %copy-done.42), channel_id=1, source_target_pairs={{0,2},{1,3},{2,0},{3,1},{4,6},{5,7},{6,4},{7,5},{8,10},{9,11},{10,... | collective-permute-start | bytes 786440 | tf_op jit(solution)/shard_map/ppermute | solution.py:947
  205.0 28.7 %collective-permute-start.27 = (bf16[128,1024]{1,0:T(8,128)(2,1)S(1)}, bf16[128,1024]{1,0:T(8,128)(2,1)S(1)}, u32[]{:S(2)}, u32[]{:S(2)}) collective-permute-start(bf16[128,1024]{1,0:T(8,128)(2,1)S(1)} %copy-done.41), channel_id=1, source_target_pairs={{0,4},{1,5},{2,6},{3,7},{4,0},{5,1},{6,2},{7,3},{8,12},{9,13},{10,... | collective-permute-start | bytes 786440 | tf_op jit(solution)/shard_map/ppermute | solution.py:947
  207.4 26.3 %collective-permute-start.28 = (bf16[128,1024]{1,0:T(8,128)(2,1)S(1)}, bf16[128,1024]{1,0:T(8,128)(2,1)S(1)}, u32[]{:S(2)}, u32[]{:S(2)}) collective-permute-start(bf16[128,1024]{1,0:T(8,128)(2,1)S(1)} %copy-done.40), channel_id=1, source_target_pairs={{0,6},{1,7},{2,4},{3,5},{4,2},{5,3},{6,0},{7,1},{8,14},{9,15},{10,... | collective-permute-start | bytes 786440 | tf_op jit(solution)/shard_map/ppermute | solution.py:947
  219.2 14.6 %collective-permute-start.30 = (bf16[32,3712]{1,0:T(8,128)(2,1)}, bf16[32,3712]{1,0:T(8,128)(2,1)S(1)}, u32[]{:S(2)}, u32[]{:S(2)}) collective-permute-start(bf16[32,3712]{1,0:T(8,128)(2,1)} %get-tuple-element.293), channel_id=1, source_target_pairs={{0,8},{8,0},{16,24},{24,16},{1,9},{9,1},{17,25},{25,17},{2,10},{10... | collective-permute-start | bytes 712712 | tf_op jit(solution)/shard_map/ppermute | solution.py:943
  220.2 13.5 %collective-permute-start.31 = (bf16[32,3712]{1,0:T(8,128)(2,1)}, bf16[32,3712]{1,0:T(8,128)(2,1)S(1)}, u32[]{:S(2)}, u32[]{:S(2)}) collective-permute-start(bf16[32,3712]{1,0:T(8,128)(2,1)} %get-tuple-element.294), channel_id=1, source_target_pairs={{0,16},{8,24},{16,0},{24,8},{1,17},{9,25},{17,1},{25,9},{2,18},{10... | collective-permute-start | bytes 712712 | tf_op jit(solution)/shard_map/ppermute | solution.py:943
  221.8 12.0 %collective-permute-start.32 = (bf16[32,3712]{1,0:T(8,128)(2,1)}, bf16[32,3712]{1,0:T(8,128)(2,1)S(1)}, u32[]{:S(2)}, u32[]{:S(2)}) collective-permute-start(bf16[32,3712]{1,0:T(8,128)(2,1)} %get-tuple-element.295), channel_id=1, source_target_pairs={{0,24},{8,16},{16,8},{24,0},{1,25},{9,17},{17,9},{25,1},{2,26},{10... | collective-permute-start | bytes 712712 | tf_op jit(solution)/shard_map/ppermute | solution.py:943
  222.7 11.1 %copy-start.18 = (f32[128,1024]{1,0:T(8,128)S(1)}, f32[128,1024]{1,0:T(8,128)}, u32[]{:S(2)}) copy-start(f32[128,1024]{1,0:T(8,128)} %get-tuple-element.180.h1) | copy-start | bytes 1572868
  222.7 11.1 %copy-start.27 = (bf16[128,1024]{1,0:T(8,128)(2,1)S(1)}, bf16[128,1024]{1,0:T(8,128)(2,1)}, u32[]{:S(2)}) copy-start(bf16[128,1024]{1,0:T(8,128)(2,1)} %get-tuple-element.320) | copy-start | bytes 786436
  (17 other events, 18.4 us)
